TPU v7x, 256 devices: a whole 4x4x8 slice. The times are simulated.
256 devices in a mesh: seq: 64 (over z, y, core), head: 4 (over x).
Axes of the slice: x: 4, y: 4, z: 8, core: 2. Of those that a mesh axis runs over, the one named last changes fastest.
Arguments:
- video_tokens: bfloat16 [32768, 3072], P('seq'), may hold values from -56 to 56
- text_tokens: bfloat16 [256, 3072], P('seq'), may hold values from -6 to 6
- project_in: bfloat16 [3072, 12, 384], P(None, 'head'), may hold values from -0.1875 to 0.1875
- project_out: bfloat16 [12, 128, 3072], P('head'), may hold values from -0.15625 to 0.15625
- head_class: int32 [12], replicated, may hold values from 0 to 1, as said below
- text_length: int32 [1], replicated, may hold values from 32 to 256
Outputs:
- block_output: bfloat16 [32768, 3072], P(('seq', 'head'))
Inputs may be any that keep to these rules, and one draw needn't show every extreme that they name: `head_class`: 1 marks a spatial head and 0 a temporal one; from 3 to 9 heads are spatial, which ones varies. The first text_length text slots hold real text, the others padding.
All inputs are finite; a program needn't handle non-finite values.
Results may differ from a plain program's by a relative error of at most 0.006.
The roundings to bfloat16 on the way count: a program that leaves them out, or rounds other values in their place, can miss the bound.
Values may be sent and summed in bfloat16 or wider, within the bound.
No kernel may reach another device: no remote copies, remote signals or barrier semaphores. Data moves between devices by JAX's collectives and lax.ppermute only.
A program may use at most 128 MiB of HBM per device.

v0:
```python
import jax
import jax.numpy as jnp
from jax import lax
from jax.sharding import PartitionSpec as P

FRAME_BITS = 1


masked_score = -1e30


def shifted(value, axis, by):
    count = lax.axis_size(axis)
    pairs = [(i, i + by) for i in range(count) if 0 <= i + by < count]
    return lax.ppermute(value, axis, pairs)


def from_root(value, axis, source):
    kept = jnp.where(lax.axis_index(axis) == source, value, 0).astype(value.dtype)
    return lax.psum(kept, axis)


def spatial_head(query_rows, key_rows, value_rows, key_valid, score_scale):
    scores = (
        lax.dot_general(
            query_rows, key_rows, (((1,), (1,)), ((), ())), preferred_element_type=jnp.float32
        )
        * score_scale
    )
    scores = jnp.where(key_valid[None, :], scores, masked_score)
    highest = jnp.max(scores, axis=1, keepdims=True)
    weights = jnp.exp(scores - highest)
    totals = jnp.sum(weights, axis=1, keepdims=True)
    summed = jnp.dot(weights.astype(jnp.bfloat16), value_rows, preferred_element_type=jnp.float32)
    return (summed / totals).astype(jnp.bfloat16)


def temporal_head(
    query_grid, key_grid, value_grid, text_keys, text_values, text_valid, score_scale
):
    frame_scores = (
        jnp.einsum("fpd,epd->fpe", query_grid, key_grid, preferred_element_type=jnp.float32)
        * score_scale
    )
    text_scores = (
        jnp.einsum("fpd,sd->fps", query_grid, text_keys, preferred_element_type=jnp.float32)
        * score_scale
    )
    text_scores = jnp.where(text_valid[None, None, :], text_scores, masked_score)
    highest = jnp.maximum(jnp.max(frame_scores, axis=2), jnp.max(text_scores, axis=2))[:, :, None]
    frame_weights = jnp.exp(frame_scores - highest)
    text_weights = jnp.exp(text_scores - highest)
    totals = jnp.sum(frame_weights, axis=2) + jnp.sum(text_weights, axis=2)
    summed = jnp.einsum(
        "fpe,epd->fpd",
        frame_weights.astype(jnp.bfloat16),
        value_grid,
        preferred_element_type=jnp.float32,
    )
    summed = summed + jnp.einsum(
        "fps,sd->fpd",
        text_weights.astype(jnp.bfloat16),
        text_values,
        preferred_element_type=jnp.float32,
    )
    return (summed / totals[:, :, None]).astype(jnp.bfloat16)


def local(video_tokens, text_tokens, project_in, project_out, head_class, text_length):
    tok_rows, model_width = video_tokens.shape
    heads_here = project_in.shape[1]
    head_size = project_in.shape[2] // 3
    score_scale = head_size ** (-0.5)
    seq_count = lax.axis_size("seq")
    seq_place = lax.axis_index("seq")
    frame_shards = 2**FRAME_BITS
    frame_rows = frame_shards * tok_rows
    frame_count = seq_count // frame_shards
    own_frame = seq_place // frame_shards
    flat_in = project_in.reshape(model_width, heads_here * 3 * head_size)
    packed = jnp.dot(video_tokens, flat_in, preferred_element_type=jnp.float32).astype(jnp.bfloat16)
    packed = packed.reshape(tok_rows, heads_here, 3 * head_size)
    text_packed = jnp.dot(text_tokens, flat_in, preferred_element_type=jnp.float32).astype(
        jnp.bfloat16
    )
    text_packed = text_packed.reshape(text_tokens.shape[0], heads_here, 3 * head_size)
    text_all = lax.all_gather(text_packed[:, :, head_size:], "seq", axis=0, tiled=True)
    text_valid = jnp.arange(text_all.shape[0], dtype=jnp.int32) < text_length[0]
    pair_rows = packed[:, :, head_size:]
    earlier = [shifted(pair_rows, "seq", 1)]
    later = [shifted(pair_rows, "seq", -1)]
    ordered = jnp.stack(earlier[::-1] + [pair_rows] + later)
    frame_pairs_all = lax.dynamic_slice_in_dim(
        ordered, frame_shards - 1 - seq_place % frame_shards, frame_shards, 0
    )
    first_pairs = from_root(frame_pairs_all, "seq", frame_shards - 1)
    frame_flat = frame_pairs_all.reshape(frame_rows, heads_here, 2 * head_size)
    first_flat = first_pairs.reshape(frame_rows, heads_here, 2 * head_size)
    key_all = jnp.concatenate([frame_flat, first_flat, text_all], axis=0)
    key_valid = jnp.concatenate(
        [jnp.ones((frame_rows,), bool), jnp.broadcast_to(own_frame != 0, (frame_rows,)), text_valid]
    )
    moved_rows = lax.all_to_all(packed, "seq", split_axis=0, concat_axis=0, tiled=True)
    moved_rows = moved_rows.reshape(frame_count, tok_rows // frame_count, heads_here, 3 * head_size)
    local_class = lax.dynamic_slice_in_dim(
        head_class, lax.axis_index("head") * heads_here, heads_here
    )
    spatial_list = []
    temporal_list = []
    for head_slot in range(heads_here):

        def run_spatial(head_slot=head_slot):
            return spatial_head(
                packed[:, head_slot, :head_size],
                key_all[:, head_slot, :head_size],
                key_all[:, head_slot, head_size:],
                key_valid,
                score_scale,
            )

        def run_temporal(head_slot=head_slot):
            result = temporal_head(
                moved_rows[:, :, head_slot, :head_size],
                moved_rows[:, :, head_slot, head_size : 2 * head_size],
                moved_rows[:, :, head_slot, 2 * head_size :],
                text_all[:, head_slot, :head_size],
                text_all[:, head_slot, head_size:],
                text_valid,
                score_scale,
            )
            return result.reshape(tok_rows, head_size)

        spatial_list.append(run_spatial())
        temporal_list.append(run_temporal())
    spatial_all = jnp.stack(spatial_list, axis=1)
    temporal_moved = jnp.stack(temporal_list, axis=1)
    temporal_all = lax.all_to_all(temporal_moved, "seq", split_axis=0, concat_axis=0, tiled=True)
    attention = jnp.where(local_class[None, :, None] == 1, spatial_all, temporal_all)
    attention_flat = attention.reshape(tok_rows, heads_here * head_size)
    flat_out = project_out.reshape(heads_here * head_size, model_width)
    summed = lax.psum_scatter(
        jnp.dot(attention_flat, flat_out, preferred_element_type=jnp.float32),
        "head",
        scatter_dimension=0,
        tiled=True,
    )
    return summed.astype(jnp.bfloat16)


def solution(mesh):
    placed = (
        P("seq", None),
        P("seq", None),
        P(None, "head", None),
        P("head", None, None),
        P(),
        P(),
    )
    return jax.shard_map(
        local, mesh=mesh, in_specs=placed, out_specs=P(("seq", "head"), None), check_vma=False
    )
```

profile of v0, /device:TPU:32, one launch (start us, length us, event | category | flops | bytes accessed | tf_op | source)
XLA Modules:
  0.0 375.6 jit_solution(3548408786516061016)
XLA Ops:
  6.5 10.4 %copy.174 = bf16[3072,3,384]{0,2,1:T(8,128)(2,1)} copy(bf16[3072,3,384]{2,0,1:T(8,128)(2,1)} %param.8) | data formatting | bytes 14155776 | tf_op args[2]
  17.0 8.3 %convolution_convert_fusion = bf16[512,1152]{1,0:T(8,128)(2,1)} fusion(bf16[512,3072]{1,0:T(8,128)(2,1)S(1)} %copy-done, bf16[3072,1152]{0,1:T(8,128)(2,1)} %bitcast.166), kind=kOutput, calls=%fused_computation.17 | convolution fusion | flops 3624468480 | bytes 11403264 | tf_op jit(solution)/shard_map/dot_general | solution.py:81
  25.2 1.6 copy.175
  26.8 1.0 slice_bitcast_fusion.30
  27.8 3.9 %collective-permute-start.1 = (bf16[512,3,256]{0,2,1:T(8,128)(2,1)S(1)}, bf16[512,3,256]{0,2,1:T(8,128)(2,1)S(1)}, u32[]{:S(2)}, u32[]{:S(2)}) collective-permute-start(bf16[512,3,256]{0,2,1:T(8,128)(2,1)S(1)} %get-tuple-element.17), channel_id=1, source_target_pairs={{4,0},{8,4},{12,8},{16,12},{20,16},{24,20},{28,24},{32,28},{36,32}... | collective-permute-start | bytes 2359304 | tf_op jit(solution)/shard_map/ppermute | solution.py:15
  31.7 1.9 collective-permute-start
  33.7 2.3 copy.183
  35.9 13.0 %all-to-all-start = ((bf16[512,3,384]{2,1,0:T(4,128)(2,1)}), bf16[512,3,384]{2,1,0:T(4,128)(2,1)}, u32[]{:S(2)}, u32[]{:S(2)}) async-start(bf16[512,3,384]{2,1,0:T(4,128)(2,1)} %copy.183), calls=%async_computation | async-start | bytes 3145728 | tf_op jit(solution)/shard_map/all_to_all | solution.py:103
  49.1 0.9 copy-done.5
  50.0 3.4 broadcast_select_fusion
  53.4 1.6 copy.178
  55.0 4.9 %convolution_convert_fusion.1 = bf16[4,1152]{1,0:T(4,128)(2,1)S(1)} fusion(bf16[4,3072]{1,0:T(4,128)(2,1)S(1)} %copy-done.10, bf16[3072,1152]{0,1:T(8,128)(2,1)} %bitcast.167), kind=kOutput, calls=%fused_computation.27 | convolution fusion | flops 28316160 | bytes 7111680 | tf_op jit(solution)/shard_map/dot_general | solution.py:83
  60.0 70.1 %all_gather.3 = bf16[256,3,256]{2,1,0:T(4,128)(2,1)S(1)} all-gather(bf16[4,3,256]{2,1,0:T(4,128)(2,1)S(1)} %copy.179), channel_id=1, replica_groups=mesh['seq'=64,'head'=4] {'seq'}, dimensions={0}, use_global_device_ids=true | all-gather | bytes 399360 | tf_op jit(solution)/shard_map/all_gather | solution.py:87
  130.9 0.6 dynamic-slice_compare_fusion
  131.5 1.9 copy.177
  133.4 113.3 %all-reduce.2.cloned.1.call-done = bf16[1024,3,256]{2,0,1:T(8,128)(2,1)} async-done(((bf16[1024,3,256]{2,0,1:T(8,128)(2,1)}), bf16[1024,3,256]{2,0,1:T(8,128)(2,1)}) %all-reduce.2.cloned.1.call-update) | async-done | bytes 1572880 | tf_op jit(solution)/shard_map/psum | solution.py:20
  246.7 1.8 pad_maximum_fusion
  248.5 1.0 fusion.95
  249.5 0.8 fusion.7
  250.2 1.0 fusion.96
  251.3 1.8 fusion.5
  253.0 3.6 fusion.97
  256.6 0.9 fusion.56
  257.5 1.6 copy.184
  259.1 1.0 fusion.94
  260.1 0.9 fusion.99
  261.0 0.9 fusion.101
  261.9 1.0 fusion.103
  262.9 0.8 copy.214
  263.7 1.2 fusion.98
  265.0 1.2 convolution_bitcast_fusion.1
  266.2 0.2 fusion.63
  266.6 0.2 fusion.49
  266.9 0.8 copy.202
  268.3 0.2 fusion.61
  268.6 0.2 fusion.48
  269.6 0.2 fusion.59
  269.9 0.2 fusion.47
  270.3 1.1 copy.221
  271.5 10.2 %all-to-all-start.1 = ((bf16[512,3,128]{2,1,0:T(4,128)(2,1)}), bf16[512,3,128]{2,1,0:T(4,128)(2,1)S(1)}, u32[]{:S(2)}, u32[]{:S(2)}) async-start(bf16[512,3,128]{2,1,0:T(4,128)(2,1)} %copy.221), calls=%async_computation.1 | async-start | bytes 1048576 | tf_op jit(solution)/shard_map/all_to_all | solution.py:137
  281.7 0.3 reduce-scatter.2.cloned.1.call-start
  282.0 3.1 fusion.3
  285.1 3.3 fusion.53
  288.5 3.5 fusion.50
  291.9 6.5 %all-to-all-done.1 = bf16[512,3,128]{2,1,0:T(4,128)(2,1)S(1)} async-done(((bf16[512,3,128]{2,1,0:T(4,128)(2,1)}), bf16[512,3,128]{2,1,0:T(4,128)(2,1)S(1)}, u32[]{:S(2)}, u32[]{:S(2)}) %all-to-all-start.1) | async-done | bytes 393248 | tf_op jit(solution)/shard_map/all_to_all | solution.py:137
  298.5 3.8 %convolution_bitcast_fusion = f32[512,3072]{1,0:T(8,128)} fusion(bf16[3,128,3072]{2,1,0:T(8,128)(2,1)S(1)} %copy-done.4, bf16[512,1,128]{2,0,1:T(8,128)(2,1)S(1)} %fusion.56, bf16[512,1,128]{2,0,1:T(8,128)(2,1)S(1)} %fusion.53, bf16[512,1,128]{2,0,1:T(8,128)(2,1)S(1)} %fusion.50, bf16[512,3,128]{2,1,0:T(4,128)(2,1)S(1)} %all-to-all-done.1, ...), kind=kOutput, calls=%fused_computation.6 | convolution fusion | flops 1208549376 | bytes 9437187 | tf_op jit(solution)/shard_map/dot_general | solution.py:142
  302.3 64.1 %reduce-scatter.2.cloned.1.call-done = f32[128,3072]{1,0:T(8,128)} async-done(((f32[512,3072]{1,0:T(8,128)}), f32[128,3072]{1,0:T(8,128)}) %reduce-scatter.2.cloned.1.call-update) | async-done | bytes 1572880 | tf_op jit(solution)/shard_map/reduce_scatter | solution.py:141
  366.4 2.4 convert_element_type.73
  (74 shorter events, 2.1 us)
Async XLA Ops:
  6.5 10.4 %copy-start = (bf16[512,3072]{1,0:T(8,128)(2,1)S(1)}, bf16[512,3072]{1,0:T(8,128)(2,1)}, u32[]{:S(2)}) copy-start(bf16[512,3072]{1,0:T(8,128)(2,1)} %param.6) | copy-start | bytes 9437188
  27.8 21.2 %collective-permute-start.1 = (bf16[512,3,256]{0,2,1:T(8,128)(2,1)S(1)}, bf16[512,3,256]{0,2,1:T(8,128)(2,1)S(1)}, u32[]{:S(2)}, u32[]{:S(2)}) collective-permute-start(bf16[512,3,256]{0,2,1:T(8,128)(2,1)S(1)} %get-tuple-element.17), channel_id=1, source_target_pairs={{4,0},{8,4},{12,8},{16,12},{20,16},{24,20},{28,24},{32,28},{36,32}... | collective-permute-start | bytes 2359304 | tf_op jit(solution)/shard_map/ppermute | solution.py:15
  31.7 17.4 %collective-permute-start = (bf16[512,3,256]{0,2,1:T(8,128)(2,1)S(1)}, bf16[512,3,256]{0,2,1:T(8,128)(2,1)}, u32[]{:S(2)}, u32[]{:S(2)}) collective-permute-start(bf16[512,3,256]{0,2,1:T(8,128)(2,1)S(1)} %get-tuple-element.17), channel_id=1, source_target_pairs={{0,4},{4,8},{8,12},{12,16},{16,20},{20,24},{24,28},{28,32},{32,36}... | collective-permute-start | bytes 2359304 | tf_op jit(solution)/shard_map/ppermute | solution.py:15
  35.9 221.5 %all-to-all-start = ((bf16[512,3,384]{2,1,0:T(4,128)(2,1)}), bf16[512,3,384]{2,1,0:T(4,128)(2,1)}, u32[]{:S(2)}, u32[]{:S(2)}) async-start(bf16[512,3,384]{2,1,0:T(4,128)(2,1)} %copy.183), calls=%async_computation | async-start | bytes 3145728 | tf_op jit(solution)/shard_map/all_to_all | solution.py:103
  49.0 197.7 %all-reduce.2.cloned.1.call-start = ((), (), s32[]{:S(2)}) async-start(), calls=%async_computation.3 | async-start | bytes 3145728 | tf_op jit(solution)/shard_map/psum | solution.py:20
  49.1 0.9 copy-start.5
  53.4 1.6 copy-start.10
  55.0 75.9 %copy-start.18 = (s32[12]{0:T(128)S(1)}, s32[12]{0:T(128)}, u32[]{:S(2)}) copy-start(s32[12]{0:T(128)} %param.10) | copy-start | bytes 148
  130.9 130.1 %copy-start.17 = (pred[256]{0:T(512)(128)(4,1)}, pred[256]{0:T(512)(128)(4,1)S(1)}, u32[]{:S(2)}) copy-start(pred[256]{0:T(512)(128)(4,1)S(1)} %iota_compare_fusion) | copy-start | bytes 772
  248.4 8.2 %copy-start.3 = (bf16[2304,3,256]{2,0,1:T(8,128)(2,1)}, bf16[2304,3,256]{2,0,1:T(8,128)(2,1)S(1)}, u32[]{:S(2)}) copy-start(bf16[2304,3,256]{2,0,1:T(8,128)(2,1)S(1)} %pad_maximum_fusion) | copy-start | bytes 10616836
  251.2 5.4 %copy-start.2 = (f32[512,2304]{1,0:T(8,128)}, f32[512,2304]{1,0:T(8,128)S(1)}, u32[]{:S(2)}) copy-start(f32[512,2304]{1,0:T(8,128)S(1)} %get-tuple-element.27) | copy-start | bytes 14155780
  251.2 5.4 %copy-start.11 = (f32[512]{0:T(512)}, f32[512]{0:T(512)S(1)}, u32[]{:S(2)}) copy-start(f32[512]{0:T(512)S(1)} %get-tuple-element.26) | copy-start | bytes 6148
  262.8 4.8 %copy-start.8 = (bf16[32,16,1,128]{3,1,0,2:T(8,128)(2,1)S(1)}, bf16[32,16,1,128]{3,1,0,2:T(8,128)(2,1)}, u32[]{:S(2)}) copy-start(bf16[32,16,1,128]{3,1,0,2:T(8,128)(2,1)} %get-tuple-element.10) | copy-start | bytes 393220
  262.8 4.8 %copy-start.9 = (bf16[32,16,1,128]{3,1,0,2:T(8,128)(2,1)S(1)}, bf16[32,16,1,128]{3,1,0,2:T(8,128)(2,1)}, u32[]{:S(2)}) copy-start(bf16[32,16,1,128]{3,1,0,2:T(8,128)(2,1)} %get-tuple-element.11) | copy-start | bytes 393220
  262.9 5.2 %copy-start.7 = (bf16[32,16,1,128]{3,1,0,2:T(8,128)(2,1)S(1)}, bf16[32,16,1,128]{3,1,0,2:T(8,128)(2,1)}, u32[]{:S(2)}) copy-start(bf16[32,16,1,128]{3,1,0,2:T(8,128)(2,1)} %get-tuple-element.12) | copy-start | bytes 393220
  265.0 4.0 %copy-start.6 = (bf16[32,16,1,128]{3,1,0,2:T(8,128)(2,1)S(1)}, bf16[32,16,1,128]{3,1,0,2:T(8,128)(2,1)}, u32[]{:S(2)}) copy-start(bf16[32,16,1,128]{3,1,0,2:T(8,128)(2,1)} %get-tuple-element.14) | copy-start | bytes 393220
  268.9 13.1 %copy-start.13 = (f32[512]{0:T(512)S(1)}, f32[512]{0:T(512)}, u32[]{:S(2)}) copy-start(f32[512]{0:T(512)} %get-tuple-element.28) | copy-start | bytes 6148
  270.3 14.8 %copy-start.12 = (f32[512]{0:T(512)S(1)}, f32[512]{0:T(512)}, u32[]{:S(2)}) copy-start(f32[512]{0:T(512)} %copy-done.11) | copy-start | bytes 6148
  270.3 14.8 %copy-start.15 = (f32[512]{0:T(512)S(1)}, f32[512]{0:T(512)}, u32[]{:S(2)}) copy-start(f32[512]{0:T(512)} %fusion.5) | copy-start | bytes 6148
  271.5 27.0 %all-to-all-start.1 = ((bf16[512,3,128]{2,1,0:T(4,128)(2,1)}), bf16[512,3,128]{2,1,0:T(4,128)(2,1)S(1)}, u32[]{:S(2)}, u32[]{:S(2)}) async-start(bf16[512,3,128]{2,1,0:T(4,128)(2,1)} %copy.221), calls=%async_computation.1 | async-start | bytes 1048576 | tf_op jit(solution)/shard_map/all_to_all | solution.py:137
  281.7 84.7 %reduce-scatter.2.cloned.1.call-start = ((), (), s32[]{:S(2)}) async-start(), calls=%async_computation.4 | async-start | bytes 7864320 | tf_op jit(solution)/shard_map/reduce_scatter | solution.py:141
  285.1 3.3 copy-start.14
  288.5 10.0 %copy-start.4 = (bf16[3,128,3072]{2,1,0:T(8,128)(2,1)S(1)}, bf16[3,128,3072]{2,1,0:T(8,128)(2,1)}, u32[]{:S(2)}) copy-start(bf16[3,128,3072]{2,1,0:T(8,128)(2,1)} %param.9) | copy-start | bytes 7077892
  288.5 10.0 %copy-start.16 = (pred[3]{0:T(512)(128)(4,1)S(1)}, pred[3]{0:T(512)(128)(4,1)}, u32[]{:S(2)}) copy-start(pred[3]{0:T(512)(128)(4,1)} %dynamic-slice_compare_fusion) | copy-start | bytes 13
  302.2 66.5 %copy-start.1 = (bf16[512,3072]{1,0:T(8,128)(2,1)S(1)}, bf16[512,3072]{1,0:T(8,128)(2,1)}, u32[]{:S(2)}) copy-start(bf16[512,3072]{1,0:T(8,128)(2,1)} %param.6) | copy-start | bytes 9437188
Sparse Core Ops, SparseCore 0:
  55.1 191.5 all-reduce.1
  302.4 63.9 reduce-scatter.1
where the time goes:
time: 378 us; the launch traced here: 376 us
  waiting for transfers between devices  184 us (49%)
  blocking collectives  70.1 us (19%)
  matrix products  37 us (10%)
  starting transfers between devices  29.4 us (8%)
  local copies, waits for them, and re-layouts  25.7 us (7%)
  other arithmetic  14.9 us (4%)
  between operations  14.6 us (4%)
    psum x1, waiting for transfers between devices, from_root(): return lax.psum(kept, axis)  113 us
    all_gather x1, blocking collectives, local(): lax.all_gather(text_packed[:, :, head_size:], 'seq', axis=0, tiled=True)  70.1 us
    reduce_scatter x1, waiting for transfers between devices, local(): lax.psum_scatter(jnp.dot(attention_flat, flat_out, preferred_element_type...  64.1 us
    all_to_all x1, starting transfers between devices, local(): lax.all_to_all(packed, 'seq', split_axis=0, concat_axis=0, tiled=True)  13 us
    unnamed x39, local copies, waits for them, and re-layouts  11.4 us
    all_to_all x1, starting transfers between devices, local(): lax.all_to_all(temporal_moved, 'seq', split_axis=0, concat_axis=0, tiled=...  10.2 us
    dot_general x1, matrix products, local(): jnp.dot(video_tokens, flat_in, preferred_element_type=jnp.float32)  8.28 us
    dot_general x3, matrix products, spatial_head(): jnp.dot(weights.astype(jnp.bfloat16), value_rows, preferred_element_type=...  7.64 us
  transfers between devices with their start and end apart: 6, of which 3 were waited for; matrix products, arithmetic and copies ran while one was open for 9% of the time, Pallas kernels for 0%

commit v1 on v0

v1 whole, which is shorter than its diff:
```python
import functools
import math

import jax
import jax.numpy as jnp
from jax import lax
from jax.experimental import pallas as pl
from jax.experimental.pallas import tpu as pltpu
from jax.sharding import Mesh, PartitionSpec as P

Z, Y, CORES, PLANES = 8, 4, 2, 4
CHIPS = Z * Y
HEADS_HERE = 3
HEAD = 128
TRIPLE = 3 * HEAD
ROWS = 512
PIECE = ROWS // CHIPS
TEXT_HERE = 4
TEXT_CORE = CHIPS * TEXT_HERE
TOKEN_PART = HEADS_HERE * PIECE
CHUNK = TOKEN_PART + 2 * TEXT_HERE
WIDTH = 3072
MASKED = -1e30
FACTOR = HEAD**-0.5 * math.log2(math.e)
VMEM_LIMIT = 48 * 1024 * 1024

f32 = jnp.float32
bf16 = jnp.bfloat16


def params(**kw):
    return pltpu.CompilerParams(vmem_limit_bytes=VMEM_LIMIT, **kw)


def nt(a, b):
    return lax.dot_general(a, b, (((1,), (1,)), ((), ())), preferred_element_type=f32)


def project_kernel(x_ref, text_ref, w_ref, out_ref, text_rows):
    head = pl.program_id(0)
    w = w_ref[0]
    rows = jnp.dot(x_ref[...], w, preferred_element_type=f32).astype(bf16)
    rows = rows.reshape(CHIPS, PIECE, TRIPLE)
    text = jnp.dot(text_ref[...], w, preferred_element_type=f32)
    for h in range(HEADS_HERE):

        @pl.when(head == h)
        def _():
            out_ref[:, h * PIECE : (h + 1) * PIECE, :] = rows
            lanes = slice(h * HEAD, (h + 1) * HEAD)
            text_rows[0:TEXT_HERE, lanes] = text[:, HEAD : 2 * HEAD]
            text_rows[TEXT_HERE : 2 * TEXT_HERE, lanes] = text[:, 2 * HEAD :]

    @pl.when(head == HEADS_HERE - 1)
    def _():
        out_ref[:, TOKEN_PART:, :] = jnp.broadcast_to(
            text_rows[...].astype(bf16)[None], (CHIPS, 2 * TEXT_HERE, TRIPLE)
        )


def project(video_tokens, text_tokens, weights):
    return pl.pallas_call(
        project_kernel,
        grid=(HEADS_HERE,),
        in_specs=[
            pl.BlockSpec((ROWS, WIDTH), lambda h: (0, 0)),
            pl.BlockSpec((TEXT_HERE, WIDTH), lambda h: (0, 0)),
            pl.BlockSpec((1, WIDTH, TRIPLE), lambda h: (h, 0, 0)),
        ],
        out_specs=pl.BlockSpec((CHIPS, CHUNK, TRIPLE), lambda h: (0, 0, 0)),
        out_shape=jax.ShapeDtypeStruct((CHIPS, CHUNK, TRIPLE), bf16),
        scratch_shapes=[pltpu.VMEM((2 * TEXT_HERE, TRIPLE), f32)],
        compiler_params=params(),
        cost_estimate=pl.CostEstimate(
            flops=2 * ROWS * WIDTH * 3 * TRIPLE, bytes_accessed=12_000_000, transcendentals=0
        ),
        name="project",
    )(video_tokens, text_tokens, weights)


def text_slots(rows, core):
    place = lax.broadcasted_iota(jnp.int32, (rows, TEXT_CORE), 1)
    return (
        lax.shift_right_logical(place, 2) * (CORES * TEXT_HERE) + core * TEXT_HERE + (place & 3)
    )


def text_scores(query, keys, core, length):
    scores = nt(query, keys)
    return jnp.where(text_slots(query.shape[0], core) < length, scores, MASKED)


def finish(parts, values, shifts=None):
    highest = functools.reduce(
        jnp.maximum, [jnp.max(s, axis=1, keepdims=True) for s in parts]
    )
    top = highest * FACTOR
    total = 0.0
    summed = 0.0
    for index, (s, v) in enumerate(zip(parts, values)):
        low = top if shifts is None or shifts[index] is None else top + shifts[index]
        w = jnp.exp2(s * FACTOR - low)
        total = total + jnp.sum(w, axis=1, keepdims=True)
        summed = summed + jnp.dot(w.astype(bf16), v, preferred_element_type=f32)
    return (summed / total).astype(bf16)


def temporal_kernel(info, rows_ref, text_a, text_b, out_ref):
    head = pl.program_id(0)
    core, length = info[3], info[4]

    @pl.when(info[head] == 0)
    def _():
        block = rows_ref[...].reshape(ROWS, TRIPLE)
        keys = block[:, HEAD : 2 * HEAD]
        values = block[:, 2 * HEAD :]
        step = 128
        for start in range(0, ROWS, step):
            query = block[start : start + step, :HEAD]
            scores = nt(query, keys)
            own = lax.broadcasted_iota(jnp.int32, scores.shape, 0) & (PIECE - 1)
            other = lax.broadcasted_iota(jnp.int32, scores.shape, 1) & (PIECE - 1)
            scores = jnp.where(own == other, scores, MASKED)
            result = finish(
                [
                    scores,
                    text_scores(query, text_a[0], core, length),
                    text_scores(query, text_b[0], 1 - core, length),
                ],
                [values, text_a[1], text_b[1]],
            )
            count = step // PIECE
            place = start // PIECE
            out_ref[place : place + count] = result.reshape(count, PIECE, HEAD)

    @pl.when(info[head] != 0)
    def _():
        out_ref[...] = jnp.zeros_like(out_ref)


def temporal(info, rows, text_a, text_b):
    text_spec = pl.BlockSpec((2, TEXT_CORE, HEAD), lambda h, _: (0, 0, h))
    return pl.pallas_call(
        temporal_kernel,
        grid_spec=pltpu.PrefetchScalarGridSpec(
            num_scalar_prefetch=1,
            grid=(HEADS_HERE,),
            in_specs=[
                pl.BlockSpec((CHIPS, PIECE, TRIPLE), lambda h, _: (0, h, 0)),
                text_spec,
                text_spec,
            ],
            out_specs=pl.BlockSpec((CHIPS, PIECE, HEAD), lambda h, _: (0, h, 0)),
        ),
        out_shape=jax.ShapeDtypeStruct((CHIPS, TOKEN_PART, HEAD), bf16),
        compiler_params=params(),
        cost_estimate=pl.CostEstimate(
            flops=400_000_000, bytes_accessed=3_000_000, transcendentals=1_200_000
        ),
        name="temporal",
    )(info, rows, text_a, text_b)


def spatial_kernel(info, own, partner, first_a, first_b, text_a, text_b, back, out_ref):
    head = pl.program_id(0)
    core, length, frame = info[3], info[4], info[5]

    @pl.when(info[head] != 0)
    def _():
        shift = jnp.where(frame == 0, -MASKED, 0.0).astype(f32)
        step = 128

        def body(index, _):
            count = step // PIECE
            query = own[pl.ds(index * count, count), :, :HEAD].reshape(step, HEAD)
            pairs = []
            for ref, at in ((own, 1), (partner, 1), (first_a, 0), (first_b, 0)):
                keys = ref[:, :, at * HEAD : (at + 1) * HEAD].reshape(ROWS, HEAD)
                values = ref[:, :, (at + 1) * HEAD : (at + 2) * HEAD].reshape(ROWS, HEAD)
                pairs.append((nt(query, keys), values))
            pairs.append((text_scores(query, text_a[0], core, length), text_a[1]))
            pairs.append((text_scores(query, text_b[0], 1 - core, length), text_b[1]))
            result = finish(
                [p[0] for p in pairs],
                [p[1] for p in pairs],
                [None, None, shift, shift, None, None],
            )
            out_ref[pl.ds(pl.multiple_of(index * step, step), step), :] = result
            return 0

        lax.fori_loop(0, ROWS // step, body, 0)

    @pl.when(info[head] == 0)
    def _():
        out_ref[...] = back[...].reshape(ROWS, HEAD)


def spatial(info, own, partner, first_a, first_b, text_a, text_b, back):
    text_spec = pl.BlockSpec((2, TEXT_CORE, HEAD), lambda h, _: (0, 0, h))
    packed_spec = pl.BlockSpec((CHIPS, PIECE, TRIPLE), lambda h, _: (0, h, 0))
    first_spec = pl.BlockSpec((CHIPS, PIECE, 2 * HEAD), lambda h, _: (0, h, 0))
    return pl.pallas_call(
        spatial_kernel,
        grid_spec=pltpu.PrefetchScalarGridSpec(
            num_scalar_prefetch=1,
            grid=(HEADS_HERE,),
            in_specs=[
                packed_spec,
                packed_spec,
                first_spec,
                first_spec,
                text_spec,
                text_spec,
                pl.BlockSpec((CHIPS, PIECE, HEAD), lambda h, _: (0, h, 0)),
            ],
            out_specs=pl.BlockSpec((ROWS, HEAD), lambda h, _: (0, h)),
        ),
        out_shape=jax.ShapeDtypeStruct((ROWS, TRIPLE), bf16),
        compiler_params=params(),
        cost_estimate=pl.CostEstimate(
            flops=1_800_000_000, bytes_accessed=6_000_000, transcendentals=3_600_000
        ),
        name="spatial",
    )(info, own, partner, first_a, first_b, text_a, text_b, back)


def out_kernel(place, rows_ref, own, a1, a2, a3, b1, b2, b3, out_ref):
    plane = place[0]
    half = pl.program_id(0)

    def partial(index, w):
        rows = rows_ref[(plane + PLANES - index) % PLANES]
        return jnp.dot(rows, w[...], preferred_element_type=f32)

    base = partial(0, own)

    @pl.when(half == 0)
    def _():
        total = base + partial(1, a1) + partial(2, a2) + partial(3, a3)
        out_ref[...] = total.astype(bf16)

    @pl.when(half == 1)
    def _():
        total = base + partial(1, b1) + partial(2, b2) + partial(3, b3)
        out_ref[...] = total.astype(bf16)


def out_project(place, rows, own, mine, theirs):
    wide = 512
    count = WIDTH // CORES // wide

    def column(half, n, place):
        return (0, jnp.where(half == 0, place[1], 1 - place[1]) * count + n)

    mine_spec = pl.BlockSpec(
        (TRIPLE, wide), lambda half, n, place: (0, jnp.where(half == 0, n, count - 1))
    )
    theirs_spec = pl.BlockSpec(
        (TRIPLE, wide), lambda half, n, place: (0, jnp.where(half == 0, 0, n))
    )
    out_rows = rows.shape[1]
    return pl.pallas_call(
        out_kernel,
        grid_spec=pltpu.PrefetchScalarGridSpec(
            num_scalar_prefetch=1,
            grid=(CORES, count),
            in_specs=[
                pl.BlockSpec(rows.shape, lambda half, n, place: (0, 0, 0)),
                pl.BlockSpec((TRIPLE, wide), column),
            ]
            + [mine_spec] * 3
            + [theirs_spec] * 3,
            out_specs=pl.BlockSpec((out_rows, wide), column),
        ),
        out_shape=jax.ShapeDtypeStruct((out_rows, WIDTH), bf16),
        compiler_params=params(),
        cost_estimate=pl.CostEstimate(
            flops=2 * out_rows * 1536 * WIDTH, bytes_accessed=10_500_000, transcendentals=0
        ),
        name="out_project",
    )(place, rows, own, *mine, *theirs)


def swap_cores(value):
    return lax.ppermute(value, "core", [(0, 1), (1, 0)])


def local(video_tokens, text_tokens, project_in, project_out, head_class, text_length):
    z, y = lax.axis_index("z"), lax.axis_index("y")
    core, plane = lax.axis_index("core"), lax.axis_index("head")
    here = lax.dynamic_slice_in_dim(head_class, plane * HEADS_HERE, HEADS_HERE)
    info = jnp.concatenate([here, jnp.stack([core, text_length[0], z * Y + y, 0, 0])])
    place = jnp.stack([plane, core])

    own_out = project_out.reshape(TRIPLE, WIDTH)
    half_out = lax.dynamic_slice_in_dim(own_out, core * (WIDTH // CORES), WIDTH // CORES, 1)
    mine = [
        lax.ppermute(half_out, "head", [(i, (i + k) % PLANES) for i in range(PLANES)])
        for k in (1, 2, 3)
    ]
    theirs = [swap_cores(m) for m in mine]

    weights = jnp.transpose(project_in, (1, 0, 2))
    packed = project(video_tokens, text_tokens, weights)
    moved = lax.all_to_all(packed, ("z", "y"), 0, 0, tiled=True)
    partner = swap_cores(packed)

    text_part = moved[:, TOKEN_PART:, :].reshape(CHIPS, 2, TEXT_HERE, TRIPLE)
    text_a = jnp.transpose(text_part, (1, 0, 2, 3)).reshape(2, TEXT_CORE, TRIPLE)
    text_b = swap_cores(text_a)

    first_piece = moved[0, :TOKEN_PART, HEAD:]
    copies = jnp.broadcast_to(first_piece[None], (Z,) + first_piece.shape)
    column = lax.all_to_all(copies, "z", 0, 0, tiled=True)
    copies = jnp.broadcast_to(column[None], (Y,) + column.shape)
    first_a = lax.all_to_all(copies, "y", 0, 0, tiled=True).reshape(
        CHIPS, TOKEN_PART, 2 * HEAD
    )
    first_b = swap_cores(first_a)

    over_time = temporal(info, moved, text_a, text_b)
    back = lax.all_to_all(over_time, ("z", "y"), 0, 0, tiled=True)
    attention = spatial(info, packed, partner, first_a, first_b, text_a, text_b, back)

    gathered = lax.all_to_all(
        attention.reshape(PLANES, ROWS // PLANES, TRIPLE), "head", 0, 0, tiled=True
    )
    return out_project(place, gathered, own_out, mine, theirs)


def solution(mesh):
    split = Mesh(mesh.devices.reshape(Z, Y, CORES, PLANES), ("z", "y", "core", "head"))
    seq = ("z", "y", "core")
    placed = (
        P(seq, None),
        P(seq, None),
        P(None, "head", None),
        P("head", None, None),
        P(),
        P(),
    )
    return jax.shard_map(
        local, mesh=split, in_specs=placed, out_specs=P(seq + ("head",), None), check_vma=False
    )
```

time: 378 us -> 139 us (0.37)
  waiting for transfers between devices: 184 us -> 52.6 us
  blocking collectives: 70.1 us -> 13.1 us
  matrix products: 37 us -> 0 us
  Pallas kernels: 0 us -> 29.7 us
  other arithmetic: 14.9 us -> 0.07 us
  local copies, waits for them, and re-layouts: 25.7 us -> 11 us
  between operations: 14.6 us -> 0.77 us
    psum x1 -> x0, waiting for transfers between devices: 113 us -> none  [from_root(): return lax.psum(kept, axis)]
    all_gather x1 -> x0, blocking collectives: 70.1 us -> none  [local(): lax.all_gather(text_packed[:, :, head_size:], 'seq', axis=0, tiled=True)]
    reduce_scatter x1 -> x0, waiting for transfers between devices: 64.1 us -> none  [local(): lax.psum_scatter(jnp.dot(attention_flat, flat_out, preferred_element_type...]
    all_to_all x2 -> x4, waiting for transfers between devices: 6.51 us -> 52.3 us  [the longest x1 26.1 us: local(): moved = lax.all_to_all(packed, ('z', 'y'), 0, 0, tiled=True)]
    dot_general x21 -> x0, matrix products: 37 us -> none  [the longest x1 8.28 us: local(): jnp.dot(video_tokens, flat_in, preferred_element_type=jnp.float32)]
    pallas_call x0 -> x4, Pallas kernels: none -> 29.7 us  [the longest x1 9.17 us: project(): pl.pallas_call(project_kernel, grid=(HEADS_HERE,), in_specs=[pl.BlockSpec...]
    all_to_all x0 -> x1, blocking collectives: none -> 13.1 us  [local(): column = lax.all_to_all(copies, 'z', 0, 0, tiled=True)]
    unnamed x39 -> x10, local copies, waits for them, and re-layouts: 11.4 us -> 4.11 us
  transfers between devices with their start and end apart: 6 -> 13, of which waited for: 3 -> 5; matrix products, arithmetic and copies ran while one was open for 9% -> 5% of each run, Pallas kernels for 0% -> 9%
where the time goes in v1:
time: 139 us; the launch traced here: 140 us
  waiting for transfers between devices  52.6 us (38%)
  starting transfers between devices  32.4 us (23%)
  Pallas kernels  29.7 us (21%)
  blocking collectives  13.1 us (9%)
  local copies, waits for them, and re-layouts  11 us (8%)
    all_to_all x1, waiting for transfers between devices, local(): moved = lax.all_to_all(packed, ('z', 'y'), 0, 0, tiled=True)  26.1 us
    all_to_all x1, waiting for transfers between devices, local(): back = lax.all_to_all(over_time, ('z', 'y'), 0, 0, tiled=True)  14.7 us
    all_to_all x1, blocking collectives, local(): column = lax.all_to_all(copies, 'z', 0, 0, tiled=True)  13.1 us
    all_to_all x1, starting transfers between devices, local(): moved = lax.all_to_all(packed, ('z', 'y'), 0, 0, tiled=True)  11.4 us
    pallas_call x1, Pallas kernels, project(): pl.pallas_call(project_kernel, grid=(HEADS_HERE,), in_specs=[pl.BlockSpec...  9.17 us
    pallas_call x1, Pallas kernels, spatial(): pl.pallas_call(spatial_kernel, grid_spec=pltpu.PrefetchScalarGridSpec(num...  8.29 us
    pallas_call x1, Pallas kernels, out_project(): pl.pallas_call(out_kernel, grid_spec=pltpu.PrefetchScalarGridSpec(num_sca...  8.19 us
    all_to_all x1, waiting for transfers between devices, local(): lax.all_to_all(attention.reshape(PLANES, ROWS // PLANES, TRIPLE), 'head',...  7.29 us
  transfers between devices with their start and end apart: 13, of which 5 were waited for; matrix products, arithmetic and copies ran while one was open for 5% of the time, Pallas kernels for 9%

profile of v1, /device:TPU:32, one launch (start us, length us, event | category | flops | bytes accessed | tf_op | source)
XLA Modules:
  0.0 139.7 jit_solution(930121829900714674)
XLA Ops:
  0.0 0.0 copy-start.2
  0.0 1.9 %copy-done.2 = bf16[512,3072]{1,0:T(8,128)(2,1)S(1)} copy-done((bf16[512,3072]{1,0:T(8,128)(2,1)S(1)}, bf16[512,3072]{1,0:T(8,128)(2,1)}, u32[]{:S(2)}) %copy-start.2) | copy-done | bytes 3145752
  1.9 0.7 copy-done.3
  2.6 9.2 %project.1.own = bf16[32,56,384]{2,1,0:T(8,128)(2,1)} custom-call(bf16[512,3072]{1,0:T(8,128)(2,1)S(1)} %copy-done.2, bf16[4,3072]{1,0:T(4,128)(2,1)S(1)} %copy-done.3, bf16[3,3072,384]{2,1,0:T(8,128)(2,1)} %bitcast.18), custom_call_target="tpu_custom_call" | custom-call | flops 3623878656 | bytes 12000000 | tf_op jit(solution)/shard_map/project/pallas_call | solution.py:62
  11.8 11.4 %all-to-all-start = ((bf16[32,56,384]{2,1,0:T(8,128)(2,1)}), bf16[32,56,384]{2,1,0:T(8,128)(2,1)S(1)}, u32[]{:S(2)}, u32[]{:S(2)}) async-start(bf16[32,56,384]{2,1,0:T(8,128)(2,1)} %project.1.own), calls=%async_computation | async-start | bytes 2752512 | tf_op jit(solution)/shard_map/all_to_all | solution.py:305
  23.2 2.4 %constant_dynamic-slice_fusion = bf16[384,1536]{1,0:T(8,128)(2,1)} fusion(bf16[384,3072]{1,0:T(8,128)(2,1)} %bitcast.15, s32[]{:T(128)S(6)} %select_n.7), kind=kLoop, calls=%fused_computation.3 | loop fusion | bytes 2359300 | tf_op jit(solution)/shard_map/dynamic_slice | solution.py:296
  25.6 1.5 %collective-permute-start.3 = (bf16[384,1536]{1,0:T(8,128)(2,1)}, bf16[384,1536]{1,0:T(8,128)(2,1)S(1)}, u32[]{:S(2)}, u32[]{:S(2)}) collective-permute-start(bf16[384,1536]{1,0:T(8,128)(2,1)} %constant_dynamic-slice_fusion), channel_id=1, source_target_pairs={{0,1},{1,2},{2,3},{3,0},{4,5},{5,6},{6,7},{7,4},{8,9},{9,10},{10,1... | collective-permute-start | bytes 3538952 | tf_op jit(solution)/shard_map/ppermute | solution.py:298
  27.1 2.7 %collective-permute-start.4 = (bf16[384,1536]{1,0:T(8,128)(2,1)}, bf16[384,1536]{1,0:T(8,128)(2,1)}, u32[]{:S(2)}, u32[]{:S(2)}) collective-permute-start(bf16[384,1536]{1,0:T(8,128)(2,1)} %constant_dynamic-slice_fusion), channel_id=1, source_target_pairs={{0,2},{1,3},{2,0},{3,1},{4,6},{5,7},{6,4},{7,5},{8,10},{9,11},{10,... | collective-permute-start | bytes 3538952 | tf_op jit(solution)/shard_map/ppermute | solution.py:298
  29.8 1.4 %collective-permute-start.5 = (bf16[384,1536]{1,0:T(8,128)(2,1)}, bf16[384,1536]{1,0:T(8,128)(2,1)}, u32[]{:S(2)}, u32[]{:S(2)}) collective-permute-start(bf16[384,1536]{1,0:T(8,128)(2,1)} %constant_dynamic-slice_fusion), channel_id=1, source_target_pairs={{0,3},{1,0},{2,1},{3,2},{4,7},{5,4},{6,5},{7,6},{8,11},{9,8},{10,9... | collective-permute-start | bytes 3538952 | tf_op jit(solution)/shard_map/ppermute | solution.py:298
  31.2 26.1 %all-to-all-done.rows_ref = bf16[32,56,384]{2,1,0:T(8,128)(2,1)S(1)} async-done(((bf16[32,56,384]{2,1,0:T(8,128)(2,1)}), bf16[32,56,384]{2,1,0:T(8,128)(2,1)S(1)}, u32[]{:S(2)}, u32[]{:S(2)}) %all-to-all-start) | async-done | bytes 1376288 | tf_op jit(solution)/shard_map/all_to_all | solution.py:305
  57.4 13.1 %all_to_all.25 = bf16[8,48,256]{2,1,0:T(8,128)(2,1)S(1)} all-to-all(bf16[8,48,256]{2,1,0:T(8,128)(2,1)S(1)} %broadcast_in_dim.14), channel_id=1, replica_groups=mesh['z'=8,'y'=4,'core'=2,'head'=4] {'z'}, dimensions={0} | all-to-all | bytes 393216 | tf_op jit(solution)/shard_map/all_to_all | solution.py:314
  70.5 0.9 broadcast_in_dim.15
  71.4 3.6 %all-to-all-start.2 = ((bf16[4,8,48,256]{3,2,1,0:T(8,128)(2,1)}), bf16[4,8,48,256]{3,2,1,0:T(8,128)(2,1)S(1)}, u32[]{:S(2)}, u32[]{:S(2)}) async-start(bf16[4,8,48,256]{3,2,1,0:T(8,128)(2,1)} %broadcast_in_dim.15), calls=%async_computation.2 | async-start | bytes 1572864 | tf_op jit(solution)/shard_map/all_to_all | solution.py:316
  75.1 0.1 collective-permute-start
  75.2 0.7 slice.9
  75.9 1.0 reshape.17
  76.9 0.7 copy.9
  77.6 1.0 reshape.18.text_a
  78.6 0.6 collective-permute-start.2
  79.8 0.0 copy-done.4
  79.8 0.1 dynamic_slice.6
  79.9 0.1 concatenate.3.info
  80.0 0.4 collective-permute-done.2.text_b
  80.4 4.2 %all-to-all-done.2 = bf16[4,8,48,256]{3,2,1,0:T(8,128)(2,1)S(1)} async-done(((bf16[4,8,48,256]{3,2,1,0:T(8,128)(2,1)}), bf16[4,8,48,256]{3,2,1,0:T(8,128)(2,1)S(1)}, u32[]{:S(2)}, u32[]{:S(2)}) %all-to-all-start.2) | async-done | bytes 786464 | tf_op jit(solution)/shard_map/all_to_all | solution.py:316
  84.5 0.0 collective-permute-start.1
  84.5 4.0 %temporal.1 = bf16[32,48,128]{2,1,0:T(8,128)(2,1)S(1)} custom-call(s32[8]{0:T(128)S(1)} %concatenate.3.info, bf16[32,56,384]{2,1,0:T(8,128)(2,1)S(1)} %all-to-all-done.rows_ref, bf16[2,128,384]{2,1,0:T(8,128)(2,1)S(1)} %reshape.18.text_a, bf16[2,128,384]{2,1,0:T(8,128)(2,1)} %collective-permute-done.2.text_b), custom_call_target="tpu_custom_call" | custom-call | flops 400000000 | bytes 3000000 | tf_op jit(solution)/shard_map/temporal/pallas_call | solution.py:143
  88.6 0.0 copy-start
  88.6 0.7 copy-done
  89.3 5.0 %all-to-all-start.3 = ((bf16[32,48,128]{2,1,0:T(8,128)(2,1)}), bf16[32,48,128]{2,1,0:T(8,128)(2,1)S(1)}, u32[]{:S(2)}, u32[]{:S(2)}) async-start(bf16[32,48,128]{2,1,0:T(8,128)(2,1)} %copy-done), calls=%async_computation.3 | async-start | bytes 786432 | tf_op jit(solution)/shard_map/all_to_all | solution.py:322
  94.4 0.0 collective-permute-done.3.a1
  94.4 0.3 collective-permute-start.6
  94.7 0.0 collective-permute-done.4.a2
  94.7 0.3 collective-permute-start.7
  95.0 0.0 collective-permute-done.5.a3
  95.0 0.2 collective-permute-start.8
  95.2 0.0 collective-permute-done.partner
  95.2 14.7 %all-to-all-done.3.back = bf16[32,48,128]{2,1,0:T(8,128)(2,1)S(1)} async-done(((bf16[32,48,128]{2,1,0:T(8,128)(2,1)}), bf16[32,48,128]{2,1,0:T(8,128)(2,1)S(1)}, u32[]{:S(2)}, u32[]{:S(2)}) %all-to-all-start.3) | async-done | bytes 393248 | tf_op jit(solution)/shard_map/all_to_all | solution.py:322
  109.9 0.0 collective-permute-done.1.first_b
  109.9 8.3 %spatial.1 = bf16[512,384]{1,0:T(8,128)(2,1)S(1)} custom-call(s32[8]{0:T(128)S(1)} %concatenate.3.info, bf16[32,56,384]{2,1,0:T(8,128)(2,1)} %project.1.own, bf16[32,56,384]{2,1,0:T(8,128)(2,1)} %collective-permute-done.partner, bf16[32,48,256]{2,1,0:T(8,128)(2,1)S(1)} %bitcast.13, bf16[32,48,256]{2,1,0:T(8,128)(2,1)} %collective-permute-done.1.first_b, ...), custom_call_target="tpu_custom_call" | custom-call | flops 1800000000 | bytes 6000000 | tf_op jit(solution)/shard_map/spatial/pallas_call | solution.py:202
  118.2 0.0 copy-start.1
  118.2 0.7 copy-done.1
  118.9 5.2 %all-to-all-start.4 = ((bf16[4,128,384]{2,1,0:T(8,128)(2,1)}), bf16[4,128,384]{2,1,0:T(8,128)(2,1)S(1)}, u32[]{:S(2)}, u32[]{:S(2)}) async-start(bf16[4,128,384]{2,1,0:T(8,128)(2,1)} %bitcast.14), calls=%async_computation.4 | async-start | bytes 786432 | tf_op jit(solution)/shard_map/all_to_all | solution.py:325
  124.2 0.1 pad_add_fusion.place
  124.3 0.0 collective-permute-done.6.b1
  124.3 0.0 collective-permute-done.7.b2
  124.3 0.0 collective-permute-done.8.b3
  124.3 7.3 %all-to-all-done.4.rows_ref = bf16[4,128,384]{2,1,0:T(8,128)(2,1)S(1)} async-done(((bf16[4,128,384]{2,1,0:T(8,128)(2,1)}), bf16[4,128,384]{2,1,0:T(8,128)(2,1)S(1)}, u32[]{:S(2)}, u32[]{:S(2)}) %all-to-all-start.4) | async-done | bytes 393248 | tf_op jit(solution)/shard_map/all_to_all | solution.py:325
  131.6 8.2 %out_project.1 = bf16[128,3072]{1,0:T(8,128)(2,1)} custom-call(s32[2]{0:T(128)S(1)} %pad_add_fusion.place, bf16[4,128,384]{2,1,0:T(8,128)(2,1)S(1)} %all-to-all-done.4.rows_ref, bf16[384,3072]{1,0:T(8,128)(2,1)} %bitcast.16, bf16[384,1536]{1,0:T(8,128)(2,1)S(1)} %collective-permute-done.3.a1, bf16[384,1536]{1,0:T(8,128)(2,1)} %collective-permute-done.4.a2, ...), custom_call_target="tpu_custom_call" | custom-call | flops 1207959552 | bytes 10500000 | tf_op jit(solution)/shard_map/out_project/pallas_call | solution.py:262
  (5 shorter events, 0.0 us)
Async XLA Ops:
  0.0 1.9 %copy-start.2 = (bf16[512,3072]{1,0:T(8,128)(2,1)S(1)}, bf16[512,3072]{1,0:T(8,128)(2,1)}, u32[]{:S(2)}) copy-start(bf16[512,3072]{1,0:T(8,128)(2,1)} %x_ref.1) | copy-start | bytes 9437188
  1.9 0.7 copy-start.3
  11.8 45.6 %all-to-all-start = ((bf16[32,56,384]{2,1,0:T(8,128)(2,1)}), bf16[32,56,384]{2,1,0:T(8,128)(2,1)S(1)}, u32[]{:S(2)}, u32[]{:S(2)}) async-start(bf16[32,56,384]{2,1,0:T(8,128)(2,1)} %project.1.own), calls=%async_computation | async-start | bytes 2752512 | tf_op jit(solution)/shard_map/all_to_all | solution.py:305
  25.6 68.8 %collective-permute-start.3 = (bf16[384,1536]{1,0:T(8,128)(2,1)}, bf16[384,1536]{1,0:T(8,128)(2,1)S(1)}, u32[]{:S(2)}, u32[]{:S(2)}) collective-permute-start(bf16[384,1536]{1,0:T(8,128)(2,1)} %constant_dynamic-slice_fusion), channel_id=1, source_target_pairs={{0,1},{1,2},{2,3},{3,0},{4,5},{5,6},{6,7},{7,4},{8,9},{9,10},{10,1... | collective-permute-start | bytes 3538952 | tf_op jit(solution)/shard_map/ppermute | solution.py:298
  27.1 67.6 %collective-permute-start.4 = (bf16[384,1536]{1,0:T(8,128)(2,1)}, bf16[384,1536]{1,0:T(8,128)(2,1)}, u32[]{:S(2)}, u32[]{:S(2)}) collective-permute-start(bf16[384,1536]{1,0:T(8,128)(2,1)} %constant_dynamic-slice_fusion), channel_id=1, source_target_pairs={{0,2},{1,3},{2,0},{3,1},{4,6},{5,7},{6,4},{7,5},{8,10},{9,11},{10,... | collective-permute-start | bytes 3538952 | tf_op jit(solution)/shard_map/ppermute | solution.py:298
  29.8 65.2 %collective-permute-start.5 = (bf16[384,1536]{1,0:T(8,128)(2,1)}, bf16[384,1536]{1,0:T(8,128)(2,1)}, u32[]{:S(2)}, u32[]{:S(2)}) collective-permute-start(bf16[384,1536]{1,0:T(8,128)(2,1)} %constant_dynamic-slice_fusion), channel_id=1, source_target_pairs={{0,3},{1,0},{2,1},{3,2},{4,7},{5,4},{6,5},{7,6},{8,11},{9,8},{10,9... | collective-permute-start | bytes 3538952 | tf_op jit(solution)/shard_map/ppermute | solution.py:298
  71.4 8.4 %copy-start.4 = (s32[12]{0:T(128)S(1)}, s32[12]{0:T(128)}, u32[]{:S(2)}) copy-start(s32[12]{0:T(128)} %param.10) | copy-start | bytes 148
  71.4 13.1 %all-to-all-start.2 = ((bf16[4,8,48,256]{3,2,1,0:T(8,128)(2,1)}), bf16[4,8,48,256]{3,2,1,0:T(8,128)(2,1)S(1)}, u32[]{:S(2)}, u32[]{:S(2)}) async-start(bf16[4,8,48,256]{3,2,1,0:T(8,128)(2,1)} %broadcast_in_dim.15), calls=%async_computation.2 | async-start | bytes 1572864 | tf_op jit(solution)/shard_map/all_to_all | solution.py:316
  75.1 20.1 %collective-permute-start = (bf16[32,56,384]{2,1,0:T(8,128)(2,1)}, bf16[32,56,384]{2,1,0:T(8,128)(2,1)}, u32[]{:S(2)}, u32[]{:S(2)}) collective-permute-start(bf16[32,56,384]{2,1,0:T(8,128)(2,1)} %project.1.own), channel_id=1, source_target_pairs={{0,4},{4,0},{1,5},{5,1},{2,6},{6,2},{3,7},{7,3},{8,12},{12,8},{9,1... | collective-permute-start | bytes 4128776 | tf_op jit(solution)/shard_map/ppermute | solution.py:285
  78.6 1.8 %collective-permute-start.2 = (bf16[2,128,384]{2,1,0:T(8,128)(2,1)S(1)}, bf16[2,128,384]{2,1,0:T(8,128)(2,1)}, u32[]{:S(2)}, u32[]{:S(2)}) collective-permute-start(bf16[2,128,384]{2,1,0:T(8,128)(2,1)S(1)} %reshape.18.text_a), channel_id=1, source_target_pairs={{0,4},{4,0},{1,5},{5,1},{2,6},{6,2},{3,7},{7,3},{8,12},{12,8},{9,1... | collective-permute-start | bytes 589832 | tf_op jit(solution)/shard_map/ppermute | solution.py:285
  84.5 25.4 %collective-permute-start.1 = (bf16[32,48,256]{2,1,0:T(8,128)(2,1)S(1)}, bf16[32,48,256]{2,1,0:T(8,128)(2,1)}, u32[]{:S(2)}, u32[]{:S(2)}) collective-permute-start(bf16[32,48,256]{2,1,0:T(8,128)(2,1)S(1)} %bitcast.12), channel_id=1, source_target_pairs={{0,4},{4,0},{1,5},{5,1},{2,6},{6,2},{3,7},{7,3},{8,12},{12,8},{9,1... | collective-permute-start | bytes 2359304 | tf_op jit(solution)/shard_map/ppermute | solution.py:285
  88.6 0.7 copy-start
  89.3 20.6 %all-to-all-start.3 = ((bf16[32,48,128]{2,1,0:T(8,128)(2,1)}), bf16[32,48,128]{2,1,0:T(8,128)(2,1)S(1)}, u32[]{:S(2)}, u32[]{:S(2)}) async-start(bf16[32,48,128]{2,1,0:T(8,128)(2,1)} %copy-done), calls=%async_computation.3 | async-start | bytes 786432 | tf_op jit(solution)/shard_map/all_to_all | solution.py:322
  94.4 29.9 %collective-permute-start.6 = (bf16[384,1536]{1,0:T(8,128)(2,1)S(1)}, bf16[384,1536]{1,0:T(8,128)(2,1)}, u32[]{:S(2)}, u32[]{:S(2)}) collective-permute-start(bf16[384,1536]{1,0:T(8,128)(2,1)S(1)} %collective-permute-done.3.a1), channel_id=1, source_target_pairs={{0,4},{4,0},{1,5},{5,1},{2,6},{6,2},{3,7},{7,3},{8,12},{12,8},{9,1... | collective-permute-start | bytes 3538952 | tf_op jit(solution)/shard_map/ppermute | solution.py:285
  94.7 29.5 %collective-permute-start.7 = (bf16[384,1536]{1,0:T(8,128)(2,1)}, bf16[384,1536]{1,0:T(8,128)(2,1)}, u32[]{:S(2)}, u32[]{:S(2)}) collective-permute-start(bf16[384,1536]{1,0:T(8,128)(2,1)} %collective-permute-done.4.a2), channel_id=1, source_target_pairs={{0,4},{4,0},{1,5},{5,1},{2,6},{6,2},{3,7},{7,3},{8,12},{12,8},{9,1... | collective-permute-start | bytes 3538952 | tf_op jit(solution)/shard_map/ppermute | solution.py:285
  95.0 29.3 %collective-permute-start.8 = (bf16[384,1536]{1,0:T(8,128)(2,1)}, bf16[384,1536]{1,0:T(8,128)(2,1)}, u32[]{:S(2)}, u32[]{:S(2)}) collective-permute-start(bf16[384,1536]{1,0:T(8,128)(2,1)} %collective-permute-done.5.a3), channel_id=1, source_target_pairs={{0,4},{4,0},{1,5},{5,1},{2,6},{6,2},{3,7},{7,3},{8,12},{12,8},{9,1... | collective-permute-start | bytes 3538952 | tf_op jit(solution)/shard_map/ppermute | solution.py:285
  118.2 0.7 copy-start.1
  118.9 12.6 %all-to-all-start.4 = ((bf16[4,128,384]{2,1,0:T(8,128)(2,1)}), bf16[4,128,384]{2,1,0:T(8,128)(2,1)S(1)}, u32[]{:S(2)}, u32[]{:S(2)}) async-start(bf16[4,128,384]{2,1,0:T(8,128)(2,1)} %bitcast.14), calls=%async_computation.4 | async-start | bytes 786432 | tf_op jit(solution)/shard_map/all_to_all | solution.py:325

commit v2 on v0

v2 whole, which is shorter than its diff:
```python
import functools
import math

import jax
import jax.numpy as jnp
from jax import lax
from jax.experimental import pallas as pl
from jax.experimental.pallas import tpu as pltpu
from jax.sharding import Mesh, PartitionSpec as P

Z, Y, CORES, PLANES = 8, 4, 2, 4
CHIPS = Z * Y
HEADS_HERE = 3
HEAD = 128
TRIPLE = 3 * HEAD
ROWS = 512
BLOCK = ROWS // PLANES
PIECE = ROWS // CHIPS
TEXT_HERE = 4
TEXT_CORE = CHIPS * TEXT_HERE
TOKEN_PART = HEADS_HERE * PIECE
CHUNK = TOKEN_PART + 2 * TEXT_HERE
WIDTH = 3072
MASKED = -1e30
FACTOR = HEAD**-0.5 * math.log2(math.e)
MIB = 1024 * 1024

f32 = jnp.float32
bf16 = jnp.bfloat16


def params(mib):
    return pltpu.CompilerParams(vmem_limit_bytes=mib * MIB)


def nt(a, b):
    return lax.dot_general(a, b, (((1,), (1,)), ((), ())), preferred_element_type=f32)


CUTS = ((0, 768), (768, 2304))
TALL = ROWS + 16


def project_kernel(x_hbm, text_ref, w_hbm, out_ref, x, w, total, text_rows, x_sem, w_sem):
    def fetch(part):
        depth = pl.ds(*CUTS[part])
        yield pltpu.make_async_copy(x_hbm.at[:, depth], x.at[pl.ds(0, ROWS), depth], x_sem.at[part])
        for h in range(HEADS_HERE):
            lanes = pl.ds(h * TRIPLE, TRIPLE)
            yield pltpu.make_async_copy(
                w_hbm.at[h, depth], w.at[depth, lanes], w_sem.at[part, h]
            )

    for part in range(len(CUTS)):
        for copy in fetch(part):
            copy.start()
    padding = jnp.zeros((TALL - ROWS - TEXT_HERE, WIDTH), f32)
    x[ROWS:, :] = jnp.concatenate([text_ref[...].astype(f32), padding], axis=0).astype(bf16)

    def partial(part):
        for copy in fetch(part):
            copy.wait()
        first, depth = CUTS[part]
        return jnp.dot(
            x[:, first : first + depth], w[first : first + depth, :], preferred_element_type=f32
        )

    total[...] = partial(0)
    rows = total[...] + partial(1)
    for h in range(HEADS_HERE):
        lanes = slice(h * TRIPLE, (h + 1) * TRIPLE)
        piece = rows[:ROWS, lanes].astype(bf16)
        out_ref[:, h * PIECE : (h + 1) * PIECE, :] = piece.reshape(CHIPS, PIECE, TRIPLE)
        text = rows[ROWS : ROWS + 8, lanes]
        lanes = slice(h * HEAD, (h + 1) * HEAD)
        text_rows[0:TEXT_HERE, lanes] = text[0:TEXT_HERE, HEAD : 2 * HEAD]
        text_rows[TEXT_HERE : 2 * TEXT_HERE, lanes] = text[0:TEXT_HERE, 2 * HEAD :]
    out_ref[:, TOKEN_PART:, :] = jnp.broadcast_to(
        text_rows[...].astype(bf16)[None], (CHIPS, 2 * TEXT_HERE, TRIPLE)
    )


def project(video_tokens, text_tokens, weights):
    vmem = pl.BlockSpec(memory_space=pltpu.VMEM)
    hbm = pl.BlockSpec(memory_space=pltpu.HBM)
    return pl.pallas_call(
        project_kernel,
        in_specs=[hbm, vmem, hbm],
        out_specs=vmem,
        out_shape=jax.ShapeDtypeStruct((CHIPS, CHUNK, TRIPLE), bf16),
        scratch_shapes=[
            pltpu.VMEM((TALL, WIDTH), bf16),
            pltpu.VMEM((WIDTH, HEADS_HERE * TRIPLE), bf16),
            pltpu.VMEM((TALL, HEADS_HERE * TRIPLE), f32),
            pltpu.VMEM((2 * TEXT_HERE, TRIPLE), f32),
            pltpu.SemaphoreType.DMA((len(CUTS),)),
            pltpu.SemaphoreType.DMA((len(CUTS), HEADS_HERE)),
        ],
        compiler_params=params(62),
        cost_estimate=pl.CostEstimate(
            flops=2 * ROWS * WIDTH * 3 * TRIPLE, bytes_accessed=12_000_000, transcendentals=0
        ),
        name="project",
    )(video_tokens, text_tokens, weights)


def text_slots(rows, core):
    row = lax.broadcasted_iota(jnp.int32, (rows, TEXT_CORE), 1)
    chip = row & (CHIPS - 1)
    return chip * (CORES * TEXT_HERE) + core * TEXT_HERE + lax.shift_right_logical(row, 5)


def weigh(scores, top, values, total, summed):
    weights = jnp.exp2(scores * FACTOR - top)
    total = total + jnp.sum(weights, axis=1, keepdims=True)
    summed = summed + jnp.dot(weights.astype(bf16), values, preferred_element_type=f32)
    return total, summed


def mask_text(scores, core, length):
    slots = jnp.concatenate(
        [text_slots(scores.shape[0], core), text_slots(scores.shape[0], 1 - core)], axis=1
    )
    return jnp.where(slots < length, scores, MASKED)


def temporal_kernel(info, rows_ref, text_own, text_other, out_ref, text_ref, spread):
    core, length = info[3], info[4]

    for side, source in enumerate((text_own, text_other)):
        for h in range(HEADS_HERE):
            lanes = source[:, :, h * HEAD : (h + 1) * HEAD].astype(f32)
            spread[...] = lanes.reshape(CHIPS * 2 * TEXT_HERE, HEAD)
            for kind in range(2):
                for t in range(TEXT_HERE):
                    rows = pl.ds(kind * TEXT_HERE + t, CHIPS, stride=2 * TEXT_HERE)
                    first = side * TEXT_CORE + t * CHIPS
                    text_ref[h, kind, first : first + CHIPS, :] = spread[rows, :].astype(bf16)

    step = 128
    count = step // PIECE
    for h in range(HEADS_HERE):
        part = slice(h * PIECE, (h + 1) * PIECE)

        @pl.when(info[h] == 0)
        def _():
            keys = rows_ref[:, part, HEAD : 2 * HEAD].reshape(ROWS, HEAD)
            values = rows_ref[:, part, 2 * HEAD :].reshape(ROWS, HEAD)
            for index in range(ROWS // step):
                chips = slice(index * count, (index + 1) * count)
                query = rows_ref[chips, part, :HEAD].reshape(step, HEAD)
                scores = nt(query, keys)
                own = lax.broadcasted_iota(jnp.int32, scores.shape, 0) & (PIECE - 1)
                other = lax.broadcasted_iota(jnp.int32, scores.shape, 1) & (PIECE - 1)
                scores = jnp.where(own == other, scores, MASKED)
                text = mask_text(nt(query, text_ref[h, 0]), core, length)
                top = FACTOR * jnp.maximum(
                    jnp.max(scores, axis=1, keepdims=True), jnp.max(text, axis=1, keepdims=True)
                )
                total, summed = weigh(scores, top, values, 0.0, 0.0)
                total, summed = weigh(text, top, text_ref[h, 1], total, summed)
                result = (summed / total).astype(bf16)
                out_ref[chips, part, :] = result.reshape(count, PIECE, HEAD)

        @pl.when(info[h] != 0)
        def _():
            out_ref[:, part, :] = jnp.zeros((CHIPS, PIECE, HEAD), bf16)


def specs(count):
    return [pl.BlockSpec(memory_space=pltpu.SMEM)] + [
        pl.BlockSpec(memory_space=pltpu.VMEM)
    ] * count


def temporal(info, rows, text_own, text_other):
    return pl.pallas_call(
        temporal_kernel,
        in_specs=specs(3),
        out_specs=[pl.BlockSpec(memory_space=pltpu.VMEM)] * 2,
        out_shape=[
            jax.ShapeDtypeStruct((CHIPS, TOKEN_PART, HEAD), bf16),
            jax.ShapeDtypeStruct((HEADS_HERE, 2, CORES * TEXT_CORE, HEAD), bf16),
        ],
        scratch_shapes=[pltpu.VMEM((CHIPS * 2 * TEXT_HERE, HEAD), f32)],
        compiler_params=params(14),
        cost_estimate=pl.CostEstimate(
            flops=400_000_000, bytes_accessed=3_000_000, transcendentals=1_200_000
        ),
        name="temporal",
    )(info, rows, text_own, text_other)


FRAME_KEYS = 2 * ROWS
VIDEO_KEYS = 2 * FRAME_KEYS
ALL_KEYS = VIDEO_KEYS + CORES * TEXT_CORE


def spatial_kernel(info, own, partner, *refs):
    firsts, (text_ref, out_ref, keys, values) = refs[: 2 * Y], refs[2 * Y :]
    core, length, frame = info[3], info[4], info[5]
    shift = jnp.where(frame == 0, -MASKED, 0.0).astype(f32)
    step = 256
    count = step // PIECE
    for h in range(HEADS_HERE):
        part = slice(h * PIECE, (h + 1) * PIECE)
        head_lanes = slice(h * HEAD, (h + 1) * HEAD)

        @pl.when(info[h] != 0)
        def _():
            place = 0
            for ref in (own, partner, *firsts):
                rows = ref.shape[0] * PIECE
                width = ref.shape[2]
                block = ref[:, part, width - 2 * HEAD :].reshape(rows, 2 * HEAD)
                keys[place : place + rows, :] = block[:, :HEAD]
                values[place : place + rows, :] = block[:, HEAD:]
                place += rows
            keys[VIDEO_KEYS:, :] = text_ref[h, 0]
            values[VIDEO_KEYS:, :] = text_ref[h, 1]

            def body(index, _):
                query = own[pl.ds(index * count, count), part, :HEAD].reshape(step, HEAD)
                here = nt(query, keys[:FRAME_KEYS, :])
                first = nt(query, keys[FRAME_KEYS:VIDEO_KEYS, :])
                text = mask_text(nt(query, keys[VIDEO_KEYS:, :]), core, length)
                top = FACTOR * functools.reduce(
                    jnp.maximum, [jnp.max(s, axis=1, keepdims=True) for s in (here, first, text)]
                )
                total, summed = weigh(here, top, values[:FRAME_KEYS, :], 0.0, 0.0)
                total, summed = weigh(
                    first, top + shift, values[FRAME_KEYS:VIDEO_KEYS, :], total, summed
                )
                total, summed = weigh(text, top, values[VIDEO_KEYS:, :], total, summed)
                rows = pl.ds(pl.multiple_of(index * step, step), step)
                out_ref[rows, head_lanes] = (summed / total).astype(bf16)
                return 0

            lax.fori_loop(0, ROWS // step, body, 0)


def spatial(info, own, partner, firsts, text):
    return pl.pallas_call(
        spatial_kernel,
        in_specs=specs(3 + 2 * Y),
        out_specs=pl.BlockSpec(memory_space=pltpu.VMEM),
        out_shape=jax.ShapeDtypeStruct((ROWS, TRIPLE), bf16),
        scratch_shapes=[pltpu.VMEM((ALL_KEYS, HEAD), bf16)] * 2,
        compiler_params=params(20),
        cost_estimate=pl.CostEstimate(
            flops=500_000_000, bytes_accessed=1_000_000, transcendentals=0
        ),
        name="spatial",
    )(info, own, partner, *firsts, text)


def merge_kernel(info, spatial_ref, back, *outs):
    plane = info[6]
    count = CHIPS // PLANES
    for index in range(PLANES):
        step = (index - plane) & (PLANES - 1)
        for k, out_ref in enumerate(outs):

            @pl.when(step == k)
            def _():
                out_ref[...] = spatial_ref[index * BLOCK : (index + 1) * BLOCK, :]
                for h in range(HEADS_HERE):

                    @pl.when(info[h] == 0)
                    def _():
                        rows = back[
                            index * count : (index + 1) * count, h * PIECE : (h + 1) * PIECE, :
                        ]
                        out_ref[:, h * HEAD : (h + 1) * HEAD] = rows.reshape(BLOCK, HEAD)


def merge(info, over_space, back):
    return pl.pallas_call(
        merge_kernel,
        in_specs=specs(2),
        out_specs=[pl.BlockSpec(memory_space=pltpu.VMEM)] * PLANES,
        out_shape=[jax.ShapeDtypeStruct((BLOCK, TRIPLE), bf16)] * PLANES,
        compiler_params=params(4),
        name="merge",
    )(info, over_space, back)


def out_kernel(place, *refs):
    rows, own, mine, theirs, out_ref = refs[:4], refs[4], refs[5:8], refs[8:11], refs[11]
    core = place[3]
    wide = WIDTH // CORES
    for which in range(CORES):
        for side, weights in ((which, mine), (1 - which, theirs)):
            lanes = slice(side * wide, (side + 1) * wide)

            @pl.when(core == which)
            def _():
                total = jnp.dot(rows[0][...], own[:, lanes], preferred_element_type=f32)
                for k in range(3):
                    total += jnp.dot(rows[k + 1][...], weights[k][...], preferred_element_type=f32)
                out_ref[:, lanes] = total.astype(bf16)


def out_project(info, rows, own, mine, theirs):
    return pl.pallas_call(
        out_kernel,
        in_specs=specs(11),
        out_specs=pl.BlockSpec(memory_space=pltpu.VMEM),
        out_shape=jax.ShapeDtypeStruct((BLOCK, WIDTH), bf16),
        compiler_params=params(12),
        cost_estimate=pl.CostEstimate(
            flops=2 * BLOCK * 1536 * WIDTH, bytes_accessed=10_500_000, transcendentals=0
        ),
        name="out_project",
    )(info, *rows, own, *mine, *theirs)


def swap_cores(value):
    return lax.ppermute(value, "core", [(0, 1), (1, 0)])


def shifted(value, axis, count, k):
    return lax.ppermute(value, axis, [(i, (i + k) % count) for i in range(count)])


def local(video_tokens, text_tokens, project_in, project_out, head_class, text_length):
    z, y = lax.axis_index("z"), lax.axis_index("y")
    core, plane = lax.axis_index("core"), lax.axis_index("head")
    here = lax.dynamic_slice_in_dim(head_class, plane * HEADS_HERE, HEADS_HERE)
    info = jnp.concatenate([here, jnp.stack([core, text_length[0], z * Y + y, plane])])

    own_out = project_out.reshape(TRIPLE, WIDTH)
    half_out = lax.dynamic_slice_in_dim(own_out, core * (WIDTH // CORES), WIDTH // CORES, 1)
    mine = [shifted(half_out, "head", PLANES, k) for k in (1, 2, 3)]

    weights = jnp.transpose(project_in, (1, 0, 2))
    packed = project(video_tokens, text_tokens, weights)
    moved = lax.all_to_all(packed, ("z", "y"), 0, 0, tiled=True)
    partner = swap_cores(packed)

    text_own = moved[:, TOKEN_PART:, :]
    text_other = swap_cores(text_own)

    first_piece = moved[0, :TOKEN_PART, HEAD:]
    copies = jnp.broadcast_to(first_piece[None], (Z,) + first_piece.shape)
    column = lax.all_to_all(copies, "z", 0, 0, tiled=True)
    over_time, text = temporal(info, moved, text_own, text_other)
    column, over_time = lax.optimization_barrier((column, over_time))
    back = lax.all_to_all(over_time, ("z", "y"), 0, 0, tiled=True)
    columns = [column] + [shifted(column, "y", Y, k) for k in range(1, Y)]
    firsts = columns + [swap_cores(c) for c in columns]

    over_space = spatial(info, packed, partner, firsts, text)
    mine, over_space, back = lax.optimization_barrier((mine, over_space, back))
    theirs = [swap_cores(m) for m in mine]
    parts = merge(info, over_space, back)
    gathered = [parts[0]] + [shifted(parts[k], "head", PLANES, k) for k in (1, 2, 3)]
    return out_project(info, gathered, own_out, mine, theirs)


def solution(mesh):
    split = Mesh(mesh.devices.reshape(Z, Y, CORES, PLANES), ("z", "y", "core", "head"))
    seq = ("z", "y", "core")
    placed = (
        P(seq, None),
        P(seq, None),
        P(None, "head", None),
        P("head", None, None),
        P(),
        P(),
    )
    return jax.shard_map(
        local, mesh=split, in_specs=placed, out_specs=P(seq + ("head",), None), check_vma=False
    )
```

time: 378 us -> 121 us (0.32)
  waiting for transfers between devices: 184 us -> 43.8 us
  blocking collectives: 70.1 us -> 0 us
  matrix products: 37 us -> 0 us
  Pallas kernels: 0 us -> 23.8 us
  local copies, waits for them, and re-layouts: 25.7 us -> 6.54 us
  other arithmetic: 14.9 us -> 0 us
  starting transfers between devices: 29.4 us -> 44 us
  between operations: 14.6 us -> 0.83 us
    psum x1 -> x0, waiting for transfers between devices: 113 us -> none  [from_root(): return lax.psum(kept, axis)]
    all_gather x1 -> x0, blocking collectives: 70.1 us -> none  [local(): lax.all_gather(text_packed[:, :, head_size:], 'seq', axis=0, tiled=True)]
    reduce_scatter x1 -> x0, waiting for transfers between devices: 64.1 us -> none  [local(): lax.psum_scatter(jnp.dot(attention_flat, flat_out, preferred_element_type...]
    dot_general x21 -> x0, matrix products: 37 us -> none  [the longest x1 8.28 us: local(): jnp.dot(video_tokens, flat_in, preferred_element_type=jnp.float32)]
    pallas_call x0 -> x5, Pallas kernels: none -> 23.8 us  [the longest x1 9.84 us: project(): pl.pallas_call(project_kernel, in_specs=[hbm, vmem, hbm], out_specs=vmem,...]
    all_to_all x2 -> x3, waiting for transfers between devices: 6.51 us -> 26.9 us  [the longest x1 26 us: local(): moved = lax.all_to_all(packed, ('z', 'y'), 0, 0, tiled=True)]
    ppermute x2 -> x18, waiting for transfers between devices: 0.01 us -> 16.9 us  [the longest x9 14.1 us: shifted(): lax.ppermute(value, axis, [(i, (i + k) % count) for i in range(count)])]
    ppermute x2 -> x18, starting transfers between devices: 5.81 us -> 20.8 us  [the longest x9 19.2 us: shifted(): lax.ppermute(value, axis, [(i, (i + k) % count) for i in range(count)])]
  transfers between devices with their start and end apart: 6 -> 21, of which waited for: 3 -> 11; matrix products, arithmetic and copies ran while one was open for 9% -> 3% of each run, Pallas kernels for 0% -> 8%
where the time goes in v2:
time: 121 us; the launch traced here: 119 us
  starting transfers between devices  44 us (36%)
  waiting for transfers between devices  43.8 us (36%)
  Pallas kernels  23.8 us (20%)
  local copies, waits for them, and re-layouts  6.54 us (5%)
    all_to_all x1, waiting for transfers between devices, local(): moved = lax.all_to_all(packed, ('z', 'y'), 0, 0, tiled=True)  26 us
    ppermute x9, starting transfers between devices, shifted(): lax.ppermute(value, axis, [(i, (i + k) % count) for i in range(count)])  19.2 us
    ppermute x9, waiting for transfers between devices, shifted(): lax.ppermute(value, axis, [(i, (i + k) % count) for i in range(count)])  14.1 us
    all_to_all x1, starting transfers between devices, local(): moved = lax.all_to_all(packed, ('z', 'y'), 0, 0, tiled=True)  11.5 us
    pallas_call x1, Pallas kernels, project(): pl.pallas_call(project_kernel, in_specs=[hbm, vmem, hbm], out_specs=vmem,...  9.84 us
    all_to_all x1, starting transfers between devices, local(): back = lax.all_to_all(over_time, ('z', 'y'), 0, 0, tiled=True)  6.77 us
    all_to_all x1, starting transfers between devices, local(): column = lax.all_to_all(copies, 'z', 0, 0, tiled=True)  5 us
    pallas_call x1, Pallas kernels, out_project(): pl.pallas_call(out_kernel, in_specs=specs(11), out_specs=pl.BlockSpec(mem...  4.89 us
  transfers between devices with their start and end apart: 21, of which 11 were waited for; matrix products, arithmetic and copies ran while one was open for 3% of the time, Pallas kernels for 8%

profile of v2, /device:TPU:32, one launch (start us, length us, event | category | flops | bytes accessed | tf_op | source)
XLA Modules:
  0.0 119.0 jit_solution(7277992113733336886)
XLA Ops:
  0.0 9.8 %project.1.own = bf16[32,56,384]{2,1,0:T(8,128)(2,1)} custom-call(bf16[512,3072]{1,0:T(8,128)(2,1)} %x_hbm.1, bf16[4,3072]{1,0:T(4,128)(2,1)} %text_ref.1, bf16[3,3072,384]{2,1,0:T(8,128)(2,1)} %bitcast.9), custom_call_target="tpu_custom_call" | custom-call | flops 3623878656 | bytes 12000000 | tf_op jit(solution)/shard_map/project/pallas_call | solution.py:86
  9.9 11.5 %all-to-all-start = ((bf16[32,56,384]{2,1,0:T(8,128)(2,1)}), bf16[32,56,384]{2,1,0:T(8,128)(2,1)S(1)}, u32[]{:S(2)}, u32[]{:S(2)}) async-start(bf16[32,56,384]{2,1,0:T(8,128)(2,1)} %project.1.own), calls=%async_computation | async-start | bytes 2752512 | tf_op jit(solution)/shard_map/all_to_all | solution.py:338
  21.4 0.1 collective-permute-start.3
  21.5 0.0 copy-start.4
  21.5 2.4 %constant_dynamic-slice_fusion = bf16[384,1536]{1,0:T(8,128)(2,1)} fusion(bf16[384,3072]{1,0:T(8,128)(2,1)} %bitcast.7, s32[]{:T(128)S(6)} %select_n.7), kind=kLoop, calls=%fused_computation.1 | loop fusion | bytes 2359300 | tf_op jit(solution)/shard_map/dynamic_slice | solution.py:333
  23.9 1.5 %collective-permute-start = (bf16[384,1536]{1,0:T(8,128)(2,1)}, bf16[384,1536]{1,0:T(8,128)(2,1)}, u32[]{:S(2)}, u32[]{:S(2)}) collective-permute-start(bf16[384,1536]{1,0:T(8,128)(2,1)} %constant_dynamic-slice_fusion), channel_id=1, source_target_pairs={{0,1},{1,2},{2,3},{3,0},{4,5},{5,6},{6,7},{7,4},{8,9},{9,10},{10,1... | collective-permute-start | bytes 3538952 | tf_op jit(solution)/shard_map/ppermute | solution.py:323
  25.4 2.7 %collective-permute-start.1 = (bf16[384,1536]{1,0:T(8,128)(2,1)}, bf16[384,1536]{1,0:T(8,128)(2,1)}, u32[]{:S(2)}, u32[]{:S(2)}) collective-permute-start(bf16[384,1536]{1,0:T(8,128)(2,1)} %constant_dynamic-slice_fusion), channel_id=1, source_target_pairs={{0,2},{1,3},{2,0},{3,1},{4,6},{5,7},{6,4},{7,5},{8,10},{9,11},{10,... | collective-permute-start | bytes 3538952 | tf_op jit(solution)/shard_map/ppermute | solution.py:323
  28.1 1.4 %collective-permute-start.2 = (bf16[384,1536]{1,0:T(8,128)(2,1)}, bf16[384,1536]{1,0:T(8,128)(2,1)}, u32[]{:S(2)}, u32[]{:S(2)}) collective-permute-start(bf16[384,1536]{1,0:T(8,128)(2,1)} %constant_dynamic-slice_fusion), channel_id=1, source_target_pairs={{0,3},{1,0},{2,1},{3,2},{4,7},{5,4},{6,5},{7,6},{8,11},{9,8},{10,9... | collective-permute-start | bytes 3538952 | tf_op jit(solution)/shard_map/ppermute | solution.py:323
  29.5 26.0 %all-to-all-done.rows_ref = bf16[32,56,384]{2,1,0:T(8,128)(2,1)S(1)} async-done(((bf16[32,56,384]{2,1,0:T(8,128)(2,1)}), bf16[32,56,384]{2,1,0:T(8,128)(2,1)S(1)}, u32[]{:S(2)}, u32[]{:S(2)}) %all-to-all-start) | async-done | bytes 1376288 | tf_op jit(solution)/shard_map/all_to_all | solution.py:338
  55.6 0.7 broadcast_in_dim.8
  56.3 5.0 %all-to-all-start.1 = ((bf16[8,48,256]{2,1,0:T(8,128)(2,1)}), bf16[8,48,256]{2,1,0:T(8,128)(2,1)S(1)}, u32[]{:S(2)}, u32[]{:S(2)}) async-start(bf16[8,48,256]{2,1,0:T(8,128)(2,1)} %broadcast_in_dim.8), calls=%async_computation.1 | async-start | bytes 393216 | tf_op jit(solution)/shard_map/all_to_all | solution.py:346
  61.3 0.1 collective-permute-start.4
  62.1 0.1 dynamic_slice.6
  62.1 0.1 concatenate.3.info.place
  62.2 0.6 collective-permute-done.4.text_other
  62.8 0.7 copy-done.2
  63.5 0.9 copy-done.3
  64.4 4.3 %temporal.1 = (bf16[32,48,128]{2,1,0:T(8,128)(2,1)}, bf16[3,2,256,128]{3,2,1,0:T(8,128)(2,1)S(1)}) custom-call(s32[7]{0:T(128)S(1)} %concatenate.3.info.place, bf16[32,56,384]{2,1,0:T(8,128)(2,1)S(1)} %all-to-all-done.rows_ref, bf16[32,8,384]{2,1,0:T(8,128)(2,1)S(1)} %slice.9.text_own, bf16[32,8,384]{2,1,0:T(8,128)(2,1)S(1)} %copy-done.3), custom_call_target="tpu_custom_call" | custom-call | flops 400000000 | bytes 3000000 | tf_op jit(solution)/shard_map/temporal/pallas_call | solution.py:177
  68.8 0.8 all-to-all-done.1.refs_0_
  69.6 2.7 %collective-permute-start.6 = (bf16[8,48,256]{2,1,0:T(8,128)(2,1)S(1)}, bf16[8,48,256]{2,1,0:T(8,128)(2,1)S(1)}, u32[]{:S(2)}, u32[]{:S(2)}) collective-permute-start(bf16[8,48,256]{2,1,0:T(8,128)(2,1)S(1)} %all-to-all-done.1.refs_0_), channel_id=1, source_target_pairs={{0,16},{8,24},{16,0},{24,8},{1,17},{9,25},{17,1},{25,9},{2,18},{10... | collective-permute-start | bytes 589832 | tf_op jit(solution)/shard_map/ppermute | solution.py:323
  72.3 6.8 %all-to-all-start.2 = ((bf16[32,48,128]{2,1,0:T(8,128)(2,1)}), bf16[32,48,128]{2,1,0:T(8,128)(2,1)S(1)}, u32[]{:S(2)}, u32[]{:S(2)}) async-start(bf16[32,48,128]{2,1,0:T(8,128)(2,1)} %get-tuple-element.21), calls=%async_computation.2 | async-start | bytes 786432 | tf_op jit(solution)/shard_map/all_to_all | solution.py:349
  79.1 0.0 collective-permute-done.3.partner
  79.1 2.9 %collective-permute-start.7 = (bf16[8,48,256]{2,1,0:T(8,128)(2,1)S(1)}, bf16[8,48,256]{2,1,0:T(8,128)(2,1)S(1)}, u32[]{:S(2)}, u32[]{:S(2)}) collective-permute-start(bf16[8,48,256]{2,1,0:T(8,128)(2,1)S(1)} %all-to-all-done.1.refs_0_), channel_id=1, source_target_pairs={{0,24},{8,0},{16,8},{24,16},{1,25},{9,1},{17,9},{25,17},{2,26},{10... | collective-permute-start | bytes 589832 | tf_op jit(solution)/shard_map/ppermute | solution.py:323
  82.1 0.0 collective-permute-done.6.refs_2_
  82.1 0.0 collective-permute-start.5
  82.1 6.8 %collective-permute-done.7.refs_3_ = bf16[8,48,256]{2,1,0:T(8,128)(2,1)S(1)} collective-permute-done((bf16[8,48,256]{2,1,0:T(8,128)(2,1)S(1)}, bf16[8,48,256]{2,1,0:T(8,128)(2,1)S(1)}, u32[]{:S(2)}, u32[]{:S(2)}) %collective-permute-start.7) | collective-permute-done | bytes 196640 | tf_op jit(solution)/shard_map/ppermute | solution.py:323
  88.9 3.1 %collective-permute-done.5.refs_1_ = bf16[8,48,256]{2,1,0:T(8,128)(2,1)S(1)} collective-permute-done((bf16[8,48,256]{2,1,0:T(8,128)(2,1)S(1)}, bf16[8,48,256]{2,1,0:T(8,128)(2,1)S(1)}, u32[]{:S(2)}, u32[]{:S(2)}) %collective-permute-start.5) | collective-permute-done | bytes 196640 | tf_op jit(solution)/shard_map/ppermute | solution.py:323
  92.0 0.0 collective-permute-start.10
  92.0 0.0 collective-permute-done.8.refs_4_
  92.0 0.5 collective-permute-start.11
  92.5 0.9 collective-permute-done.10.refs_6_
  93.4 0.1 collective-permute-start.9
  93.5 0.1 collective-permute-done.11.refs_7_
  93.7 1.2 collective-permute-done.9.refs_5_
  94.9 4.0 %spatial.1.spatial_ref = bf16[512,384]{1,0:T(8,128)(2,1)S(1)} custom-call(s32[7]{0:T(128)S(1)} %concatenate.3.info.place, bf16[32,56,384]{2,1,0:T(8,128)(2,1)S(1)} %copy-done, bf16[32,56,384]{2,1,0:T(8,128)(2,1)} %collective-permute-done.3.partner, bf16[8,48,256]{2,1,0:T(8,128)(2,1)S(1)} %all-to-all-done.1.refs_0_, ...), custom_call_target="tpu_custom_call" | custom-call | flops 500000000 | bytes 1000000 | tf_op jit(solution)/shard_map/spatial/pallas_call | solution.py:243
  98.9 0.2 collective-permute-start.15
  99.2 0.4 collective-permute-start.16
  99.5 0.1 collective-permute-start.17
  99.7 0.7 merge.1
  100.4 1.6 %collective-permute-start.12 = (bf16[128,384]{1,0:T(8,128)(2,1)S(1)}, bf16[128,384]{1,0:T(8,128)(2,1)S(1)}, u32[]{:S(2)}, u32[]{:S(2)}) collective-permute-start(bf16[128,384]{1,0:T(8,128)(2,1)S(1)} %get-tuple-element.25), channel_id=1, source_target_pairs={{0,1},{1,2},{2,3},{3,0},{4,5},{5,6},{6,7},{7,4},{8,9},{9,10},{10,1... | collective-permute-start | bytes 294920 | tf_op jit(solution)/shard_map/ppermute | solution.py:323
  102.0 4.0 %collective-permute-start.13 = (bf16[128,384]{1,0:T(8,128)(2,1)S(1)}, bf16[128,384]{1,0:T(8,128)(2,1)S(1)}, u32[]{:S(2)}, u32[]{:S(2)}) collective-permute-start(bf16[128,384]{1,0:T(8,128)(2,1)S(1)} %get-tuple-element.26), channel_id=1, source_target_pairs={{0,2},{1,3},{2,0},{3,1},{4,6},{5,7},{6,4},{7,5},{8,10},{9,11},{10,... | collective-permute-start | bytes 294920 | tf_op jit(solution)/shard_map/ppermute | solution.py:323
  106.0 1.9 %collective-permute-done.12.refs_1_ = bf16[128,384]{1,0:T(8,128)(2,1)S(1)} collective-permute-done((bf16[128,384]{1,0:T(8,128)(2,1)S(1)}, bf16[128,384]{1,0:T(8,128)(2,1)S(1)}, u32[]{:S(2)}, u32[]{:S(2)}) %collective-permute-start.12) | collective-permute-done | bytes 98336 | tf_op jit(solution)/shard_map/ppermute | solution.py:323
  107.8 2.3 %collective-permute-start.14 = (bf16[128,384]{1,0:T(8,128)(2,1)S(1)}, bf16[128,384]{1,0:T(8,128)(2,1)S(1)}, u32[]{:S(2)}, u32[]{:S(2)}) collective-permute-start(bf16[128,384]{1,0:T(8,128)(2,1)S(1)} %get-tuple-element.27), channel_id=1, source_target_pairs={{0,3},{1,0},{2,1},{3,2},{4,7},{5,4},{6,5},{7,6},{8,11},{9,8},{10,9... | collective-permute-start | bytes 294920 | tf_op jit(solution)/shard_map/ppermute | solution.py:323
  110.1 1.0 collective-permute-done.13.refs_2_
  111.1 1.3 %collective-permute-done.14.refs_3_ = bf16[128,384]{1,0:T(8,128)(2,1)S(1)} collective-permute-done((bf16[128,384]{1,0:T(8,128)(2,1)S(1)}, bf16[128,384]{1,0:T(8,128)(2,1)S(1)}, u32[]{:S(2)}, u32[]{:S(2)}) %collective-permute-start.14) | collective-permute-done | bytes 98336 | tf_op jit(solution)/shard_map/ppermute | solution.py:323
  112.5 0.0 copy-start.1
  112.5 1.7 %copy-done.1 = bf16[3,128,3072]{2,1,0:T(8,128)(2,1)S(1)} copy-done((bf16[3,128,3072]{2,1,0:T(8,128)(2,1)S(1)}, bf16[3,128,3072]{2,1,0:T(8,128)(2,1)}, u32[]{:S(2)}) %copy-start.1) | copy-done | bytes 2359320
  114.1 4.9 %out_project.1 = bf16[128,3072]{1,0:T(8,128)(2,1)} custom-call(s32[7]{0:T(128)S(1)} %concatenate.3.info.place, bf16[128,384]{1,0:T(8,128)(2,1)S(1)} %get-tuple-element.24.refs_0_, bf16[128,384]{1,0:T(8,128)(2,1)S(1)} %collective-permute-done.12.refs_1_, bf16[128,384]{1,0:T(8,128)(2,1)S(1)} %collective-permute-done.13.refs_2_, ...), custom_call_target="tpu_custom_call" | custom-call | flops 1207959552 | bytes 10500000 | tf_op jit(solution)/shard_map/out_project/pallas_call | solution.py:305
  (15 shorter events, 0.1 us)
Async XLA Ops:
  9.8 11.5 %copy-start = (bf16[32,56,384]{2,1,0:T(8,128)(2,1)S(1)}, bf16[32,56,384]{2,1,0:T(8,128)(2,1)}, u32[]{:S(2)}) copy-start(bf16[32,56,384]{2,1,0:T(8,128)(2,1)} %project.1.own) | copy-start | bytes 4128772
  9.9 45.7 %all-to-all-start = ((bf16[32,56,384]{2,1,0:T(8,128)(2,1)}), bf16[32,56,384]{2,1,0:T(8,128)(2,1)S(1)}, u32[]{:S(2)}, u32[]{:S(2)}) async-start(bf16[32,56,384]{2,1,0:T(8,128)(2,1)} %project.1.own), calls=%async_computation | async-start | bytes 2752512 | tf_op jit(solution)/shard_map/all_to_all | solution.py:338
  21.4 57.7 %collective-permute-start.3 = (bf16[32,56,384]{2,1,0:T(8,128)(2,1)S(1)}, bf16[32,56,384]{2,1,0:T(8,128)(2,1)}, u32[]{:S(2)}, u32[]{:S(2)}) collective-permute-start(bf16[32,56,384]{2,1,0:T(8,128)(2,1)S(1)} %copy-done), channel_id=1, source_target_pairs={{0,4},{4,0},{1,5},{5,1},{2,6},{6,2},{3,7},{7,3},{8,12},{12,8},{9,1... | collective-permute-start | bytes 4128776 | tf_op jit(solution)/shard_map/ppermute | solution.py:319
  21.5 40.6 %copy-start.4 = (s32[12]{0:T(128)S(1)}, s32[12]{0:T(128)}, u32[]{:S(2)}) copy-start(s32[12]{0:T(128)} %param.10) | copy-start | bytes 148
  23.9 75.0 %collective-permute-start = (bf16[384,1536]{1,0:T(8,128)(2,1)}, bf16[384,1536]{1,0:T(8,128)(2,1)}, u32[]{:S(2)}, u32[]{:S(2)}) collective-permute-start(bf16[384,1536]{1,0:T(8,128)(2,1)} %constant_dynamic-slice_fusion), channel_id=1, source_target_pairs={{0,1},{1,2},{2,3},{3,0},{4,5},{5,6},{6,7},{7,4},{8,9},{9,10},{10,1... | collective-permute-start | bytes 3538952 | tf_op jit(solution)/shard_map/ppermute | solution.py:323
  25.4 73.5 %collective-permute-start.1 = (bf16[384,1536]{1,0:T(8,128)(2,1)}, bf16[384,1536]{1,0:T(8,128)(2,1)}, u32[]{:S(2)}, u32[]{:S(2)}) collective-permute-start(bf16[384,1536]{1,0:T(8,128)(2,1)} %constant_dynamic-slice_fusion), channel_id=1, source_target_pairs={{0,2},{1,3},{2,0},{3,1},{4,6},{5,7},{6,4},{7,5},{8,10},{9,11},{10,... | collective-permute-start | bytes 3538952 | tf_op jit(solution)/shard_map/ppermute | solution.py:323
  28.1 70.8 %collective-permute-start.2 = (bf16[384,1536]{1,0:T(8,128)(2,1)}, bf16[384,1536]{1,0:T(8,128)(2,1)}, u32[]{:S(2)}, u32[]{:S(2)}) collective-permute-start(bf16[384,1536]{1,0:T(8,128)(2,1)} %constant_dynamic-slice_fusion), channel_id=1, source_target_pairs={{0,3},{1,0},{2,1},{3,2},{4,7},{5,4},{6,5},{7,6},{8,11},{9,8},{10,9... | collective-permute-start | bytes 3538952 | tf_op jit(solution)/shard_map/ppermute | solution.py:323
  56.3 13.3 %all-to-all-start.1 = ((bf16[8,48,256]{2,1,0:T(8,128)(2,1)}), bf16[8,48,256]{2,1,0:T(8,128)(2,1)S(1)}, u32[]{:S(2)}, u32[]{:S(2)}) async-start(bf16[8,48,256]{2,1,0:T(8,128)(2,1)} %broadcast_in_dim.8), calls=%async_computation.1 | async-start | bytes 393216 | tf_op jit(solution)/shard_map/all_to_all | solution.py:346
  61.3 1.5 %collective-permute-start.4 = (bf16[32,8,384]{2,1,0:T(8,128)(2,1)S(1)}, bf16[32,8,384]{2,1,0:T(8,128)(2,1)S(1)}, u32[]{:S(2)}, u32[]{:S(2)}) collective-permute-start(bf16[32,8,384]{2,1,0:T(8,128)(2,1)S(1)} %slice.9.text_own), channel_id=1, source_target_pairs={{0,4},{4,0},{1,5},{5,1},{2,6},{6,2},{3,7},{7,3},{8,12},{12,8},{9,1... | collective-permute-start | bytes 589832 | tf_op jit(solution)/shard_map/ppermute | solution.py:319
  62.8 0.7 copy-start.2
  63.5 0.9 copy-start.3
  69.6 12.5 %collective-permute-start.6 = (bf16[8,48,256]{2,1,0:T(8,128)(2,1)S(1)}, bf16[8,48,256]{2,1,0:T(8,128)(2,1)S(1)}, u32[]{:S(2)}, u32[]{:S(2)}) collective-permute-start(bf16[8,48,256]{2,1,0:T(8,128)(2,1)S(1)} %all-to-all-done.1.refs_0_), channel_id=1, source_target_pairs={{0,16},{8,24},{16,0},{24,8},{1,17},{9,25},{17,1},{25,9},{2,18},{10... | collective-permute-start | bytes 589832 | tf_op jit(solution)/shard_map/ppermute | solution.py:323
  72.3 26.6 %all-to-all-start.2 = ((bf16[32,48,128]{2,1,0:T(8,128)(2,1)}), bf16[32,48,128]{2,1,0:T(8,128)(2,1)S(1)}, u32[]{:S(2)}, u32[]{:S(2)}) async-start(bf16[32,48,128]{2,1,0:T(8,128)(2,1)} %get-tuple-element.21), calls=%async_computation.2 | async-start | bytes 786432 | tf_op jit(solution)/shard_map/all_to_all | solution.py:349
  79.1 9.8 %collective-permute-start.7 = (bf16[8,48,256]{2,1,0:T(8,128)(2,1)S(1)}, bf16[8,48,256]{2,1,0:T(8,128)(2,1)S(1)}, u32[]{:S(2)}, u32[]{:S(2)}) collective-permute-start(bf16[8,48,256]{2,1,0:T(8,128)(2,1)S(1)} %all-to-all-done.1.refs_0_), channel_id=1, source_target_pairs={{0,24},{8,0},{16,8},{24,16},{1,25},{9,1},{17,9},{25,17},{2,26},{10... | collective-permute-start | bytes 589832 | tf_op jit(solution)/shard_map/ppermute | solution.py:323
  82.1 9.9 %collective-permute-start.5 = (bf16[8,48,256]{2,1,0:T(8,128)(2,1)S(1)}, bf16[8,48,256]{2,1,0:T(8,128)(2,1)S(1)}, u32[]{:S(2)}, u32[]{:S(2)}) collective-permute-start(bf16[8,48,256]{2,1,0:T(8,128)(2,1)S(1)} %all-to-all-done.1.refs_0_), channel_id=1, source_target_pairs={{0,8},{8,16},{16,24},{24,0},{1,9},{9,17},{17,25},{25,1},{2,10},{10... | collective-permute-start | bytes 589832 | tf_op jit(solution)/shard_map/ppermute | solution.py:323
  88.9 3.1 %collective-permute-start.8 = (bf16[8,48,256]{2,1,0:T(8,128)(2,1)S(1)}, bf16[8,48,256]{2,1,0:T(8,128)(2,1)S(1)}, u32[]{:S(2)}, u32[]{:S(2)}) collective-permute-start(bf16[8,48,256]{2,1,0:T(8,128)(2,1)S(1)} %all-to-all-done.1.refs_0_), channel_id=1, source_target_pairs={{0,4},{4,0},{1,5},{5,1},{2,6},{6,2},{3,7},{7,3},{8,12},{12,8},{9,1... | collective-permute-start | bytes 589832 | tf_op jit(solution)/shard_map/ppermute | solution.py:319
  92.0 1.4 %collective-permute-start.10 = (bf16[8,48,256]{2,1,0:T(8,128)(2,1)S(1)}, bf16[8,48,256]{2,1,0:T(8,128)(2,1)S(1)}, u32[]{:S(2)}, u32[]{:S(2)}) collective-permute-start(bf16[8,48,256]{2,1,0:T(8,128)(2,1)S(1)} %collective-permute-done.6.refs_2_), channel_id=1, source_target_pairs={{0,4},{4,0},{1,5},{5,1},{2,6},{6,2},{3,7},{7,3},{8,12},{12,8},{9,1... | collective-permute-start | bytes 589832 | tf_op jit(solution)/shard_map/ppermute | solution.py:319
  92.0 1.7 %collective-permute-start.11 = (bf16[8,48,256]{2,1,0:T(8,128)(2,1)S(1)}, bf16[8,48,256]{2,1,0:T(8,128)(2,1)S(1)}, u32[]{:S(2)}, u32[]{:S(2)}) collective-permute-start(bf16[8,48,256]{2,1,0:T(8,128)(2,1)S(1)} %collective-permute-done.7.refs_3_), channel_id=1, source_target_pairs={{0,4},{4,0},{1,5},{5,1},{2,6},{6,2},{3,7},{7,3},{8,12},{12,8},{9,1... | collective-permute-start | bytes 589832 | tf_op jit(solution)/shard_map/ppermute | solution.py:319
  93.4 1.4 %collective-permute-start.9 = (bf16[8,48,256]{2,1,0:T(8,128)(2,1)S(1)}, bf16[8,48,256]{2,1,0:T(8,128)(2,1)S(1)}, u32[]{:S(2)}, u32[]{:S(2)}) collective-permute-start(bf16[8,48,256]{2,1,0:T(8,128)(2,1)S(1)} %collective-permute-done.5.refs_1_), channel_id=1, source_target_pairs={{0,4},{4,0},{1,5},{5,1},{2,6},{6,2},{3,7},{7,3},{8,12},{12,8},{9,1... | collective-permute-start | bytes 589832 | tf_op jit(solution)/shard_map/ppermute | solution.py:319
  98.9 13.5 %collective-permute-start.15 = (bf16[384,1536]{1,0:T(8,128)(2,1)}, bf16[384,1536]{1,0:T(8,128)(2,1)S(1)}, u32[]{:S(2)}, u32[]{:S(2)}) collective-permute-start(bf16[384,1536]{1,0:T(8,128)(2,1)} %collective-permute-done.refs_5_), channel_id=1, source_target_pairs={{0,4},{4,0},{1,5},{5,1},{2,6},{6,2},{3,7},{7,3},{8,12},{12,8},{9,1... | collective-permute-start | bytes 3538952 | tf_op jit(solution)/shard_map/ppermute | solution.py:319
  99.2 13.3 %collective-permute-start.16 = (bf16[384,1536]{1,0:T(8,128)(2,1)}, bf16[384,1536]{1,0:T(8,128)(2,1)S(1)}, u32[]{:S(2)}, u32[]{:S(2)}) collective-permute-start(bf16[384,1536]{1,0:T(8,128)(2,1)} %collective-permute-done.1.refs_6_), channel_id=1, source_target_pairs={{0,4},{4,0},{1,5},{5,1},{2,6},{6,2},{3,7},{7,3},{8,12},{12,8},{9,1... | collective-permute-start | bytes 3538952 | tf_op jit(solution)/shard_map/ppermute | solution.py:319
  99.5 12.9 %collective-permute-start.17 = (bf16[384,1536]{1,0:T(8,128)(2,1)}, bf16[384,1536]{1,0:T(8,128)(2,1)S(1)}, u32[]{:S(2)}, u32[]{:S(2)}) collective-permute-start(bf16[384,1536]{1,0:T(8,128)(2,1)} %collective-permute-done.2.refs_7_), channel_id=1, source_target_pairs={{0,4},{4,0},{1,5},{5,1},{2,6},{6,2},{3,7},{7,3},{8,12},{12,8},{9,1... | collective-permute-start | bytes 3538952 | tf_op jit(solution)/shard_map/ppermute | solution.py:319
  100.4 7.4 %collective-permute-start.12 = (bf16[128,384]{1,0:T(8,128)(2,1)S(1)}, bf16[128,384]{1,0:T(8,128)(2,1)S(1)}, u32[]{:S(2)}, u32[]{:S(2)}) collective-permute-start(bf16[128,384]{1,0:T(8,128)(2,1)S(1)} %get-tuple-element.25), channel_id=1, source_target_pairs={{0,1},{1,2},{2,3},{3,0},{4,5},{5,6},{6,7},{7,4},{8,9},{9,10},{10,1... | collective-permute-start | bytes 294920 | tf_op jit(solution)/shard_map/ppermute | solution.py:323
  102.0 9.1 %collective-permute-start.13 = (bf16[128,384]{1,0:T(8,128)(2,1)S(1)}, bf16[128,384]{1,0:T(8,128)(2,1)S(1)}, u32[]{:S(2)}, u32[]{:S(2)}) collective-permute-start(bf16[128,384]{1,0:T(8,128)(2,1)S(1)} %get-tuple-element.26), channel_id=1, source_target_pairs={{0,2},{1,3},{2,0},{3,1},{4,6},{5,7},{6,4},{7,5},{8,10},{9,11},{10,... | collective-permute-start | bytes 294920 | tf_op jit(solution)/shard_map/ppermute | solution.py:323
  107.8 4.6 %collective-permute-start.14 = (bf16[128,384]{1,0:T(8,128)(2,1)S(1)}, bf16[128,384]{1,0:T(8,128)(2,1)S(1)}, u32[]{:S(2)}, u32[]{:S(2)}) collective-permute-start(bf16[128,384]{1,0:T(8,128)(2,1)S(1)} %get-tuple-element.27), channel_id=1, source_target_pairs={{0,3},{1,0},{2,1},{3,2},{4,7},{5,4},{6,5},{7,6},{8,11},{9,8},{10,9... | collective-permute-start | bytes 294920 | tf_op jit(solution)/shard_map/ppermute | solution.py:323
  112.5 1.7 %copy-start.1 = (bf16[3,128,3072]{2,1,0:T(8,128)(2,1)S(1)}, bf16[3,128,3072]{2,1,0:T(8,128)(2,1)}, u32[]{:S(2)}) copy-start(bf16[3,128,3072]{2,1,0:T(8,128)(2,1)} %param.9) | copy-start | bytes 7077892

commit v3 on v2

--- a/solution.py
+++ b/solution.py
@@ -37,11 +37,12 @@
     return lax.dot_general(a, b, (((1,), (1,)), ((), ())), preferred_element_type=f32)
 
 
-CUTS = ((0, 768), (768, 2304))
+CUTS = ((0, 1536), (1536, 1536))
 TALL = ROWS + 16
 
 
 def project_kernel(x_hbm, text_ref, w_hbm, out_ref, x, w, total, text_rows, x_sem, w_sem):
+
     def fetch(part):
         depth = pl.ds(*CUTS[part])
         yield pltpu.make_async_copy(x_hbm.at[:, depth], x.at[pl.ds(0, ROWS), depth], x_sem.at[part])
@@ -57,21 +58,29 @@
     padding = jnp.zeros((TALL - ROWS - TEXT_HERE, WIDTH), f32)
     x[ROWS:, :] = jnp.concatenate([text_ref[...].astype(f32), padding], axis=0).astype(bf16)
 
-    def partial(part):
+    blocks = ((0, 256), (256, TALL))
+    for part, (first, depth) in enumerate(CUTS):
         for copy in fetch(part):
             copy.wait()
-        first, depth = CUTS[part]
-        return jnp.dot(
-            x[:, first : first + depth], w[first : first + depth, :], preferred_element_type=f32
-        )
-
-    total[...] = partial(0)
-    rows = total[...] + partial(1)
+        for start, stop in blocks:
+            partial = jnp.dot(
+                x[start:stop, first : first + depth],
+                w[first : first + depth, :],
+                preferred_element_type=f32,
+            )
+            if part == 0:
+                total[start:stop, :] = partial
+                continue
+            rows = total[start:stop, :] + partial
+            tokens = min(stop, ROWS) - start
+            chips = slice(start // PIECE, (start + tokens) // PIECE)
+            for h in range(HEADS_HERE):
+                piece = rows[:tokens, h * TRIPLE : (h + 1) * TRIPLE].astype(bf16)
+                out_ref[chips, h * PIECE : (h + 1) * PIECE, :] = piece.reshape(
+                    tokens // PIECE, PIECE, TRIPLE
+                )
     for h in range(HEADS_HERE):
-        lanes = slice(h * TRIPLE, (h + 1) * TRIPLE)
-        piece = rows[:ROWS, lanes].astype(bf16)
-        out_ref[:, h * PIECE : (h + 1) * PIECE, :] = piece.reshape(CHIPS, PIECE, TRIPLE)
-        text = rows[ROWS : ROWS + 8, lanes]
+        text = rows[tokens : tokens + 8, h * TRIPLE : (h + 1) * TRIPLE]
         lanes = slice(h * HEAD, (h + 1) * HEAD)
         text_rows[0:TEXT_HERE, lanes] = text[0:TEXT_HERE, HEAD : 2 * HEAD]
         text_rows[TEXT_HERE : 2 * TEXT_HERE, lanes] = text[0:TEXT_HERE, 2 * HEAD :]
@@ -177,10 +186,10 @@
     return pl.pallas_call(
         temporal_kernel,
         in_specs=specs(3),
-        out_specs=[pl.BlockSpec(memory_space=pltpu.VMEM)] * 2,
+        out_specs=[pl.BlockSpec()] * 2,
         out_shape=[
-            jax.ShapeDtypeStruct((CHIPS, TOKEN_PART, HEAD), bf16),
-            jax.ShapeDtypeStruct((HEADS_HERE, 2, CORES * TEXT_CORE, HEAD), bf16),
+            pltpu.HBM((CHIPS, TOKEN_PART, HEAD), bf16),
+            pltpu.HBM((HEADS_HERE, 2, CORES * TEXT_CORE, HEAD), bf16),
         ],
         scratch_shapes=[pltpu.VMEM((CHIPS * 2 * TEXT_HERE, HEAD), f32)],
         compiler_params=params(14),
@@ -242,16 +251,16 @@
 def spatial(info, own, partner, firsts, text):
     return pl.pallas_call(
         spatial_kernel,
-        in_specs=specs(3 + 2 * Y),
-        out_specs=pl.BlockSpec(memory_space=pltpu.VMEM),
-        out_shape=jax.ShapeDtypeStruct((ROWS, TRIPLE), bf16),
+        in_specs=specs(2 + 2 * Y) + [pl.BlockSpec()],
+        out_specs=pl.BlockSpec(),
+        out_shape=pltpu.HBM((ROWS, TRIPLE), bf16),
         scratch_shapes=[pltpu.VMEM((ALL_KEYS, HEAD), bf16)] * 2,
         compiler_params=params(20),
         cost_estimate=pl.CostEstimate(
-            flops=500_000_000, bytes_accessed=1_000_000, transcendentals=0
+            flops=4_000_000_000, bytes_accessed=1_000_000, transcendentals=0
         ),
         name="spatial",
-    )(info, own, partner, *firsts, text)
+    )(info, own, partner, *firsts, pltpu.with_memory_space_constraint(text, pltpu.HBM))
 
 
 def merge_kernel(info, spatial_ref, back, *outs):
@@ -277,42 +286,75 @@
 def merge(info, over_space, back):
     return pl.pallas_call(
         merge_kernel,
-        in_specs=specs(2),
+        in_specs=specs(0) + [pl.BlockSpec()] + specs(1)[1:],
         out_specs=[pl.BlockSpec(memory_space=pltpu.VMEM)] * PLANES,
         out_shape=[jax.ShapeDtypeStruct((BLOCK, TRIPLE), bf16)] * PLANES,
         compiler_params=params(4),
         name="merge",
-    )(info, over_space, back)
-
-
-def out_kernel(place, *refs):
-    rows, own, mine, theirs, out_ref = refs[:4], refs[4], refs[5:8], refs[8:11], refs[11]
-    core = place[3]
-    wide = WIDTH // CORES
+    )(info, pltpu.with_memory_space_constraint(over_space, pltpu.HBM), back)
+
+
+QUARTER = WIDTH // CORES // 2
+FAR = PLANES - 1
+
+
+def hold_kernel(*refs):
+    sources, held, sem = refs[: 4 * FAR], refs[4 * FAR], refs[4 * FAR + 1]
+    copies = [
+        pltpu.make_async_copy(
+            source, held.at[n // (2 * FAR) * 2 + n % 2, n % (2 * FAR) // 2], sem.at[n]
+        )
+        for n, source in enumerate(sources)
+    ]
+    for copy in copies:
+        copy.start()
+    for copy in copies:
+        copy.wait()
+
+
+def hold(weights):
+    shape = (4, FAR, TRIPLE, QUARTER)
+    return pl.pallas_call(
+        hold_kernel,
+        in_specs=[pl.BlockSpec(memory_space=pltpu.HBM)] * len(weights),
+        out_specs=pl.BlockSpec(memory_space=pltpu.VMEM),
+        out_shape=pltpu.VMEM(shape, bf16),
+        scratch_shapes=[pltpu.SemaphoreType.DMA((4 * FAR,))],
+        compiler_params=params(4),
+        cost_estimate=pl.CostEstimate(
+            flops=1_000_000, bytes_accessed=7_000_000, transcendentals=0
+        ),
+        name="hold",
+    )(*[pltpu.with_memory_space_constraint(w, pltpu.HBM) for w in weights])
+
+
+def out_kernel(info, r0, r1, r2, r3, own, held, out_ref):
+    core = info[3]
     for which in range(CORES):
-        for side, weights in ((which, mine), (1 - which, theirs)):
-            lanes = slice(side * wide, (side + 1) * wide)
-
-            @pl.when(core == which)
-            def _():
-                total = jnp.dot(rows[0][...], own[:, lanes], preferred_element_type=f32)
-                for k in range(3):
-                    total += jnp.dot(rows[k + 1][...], weights[k][...], preferred_element_type=f32)
+
+        @pl.when(core == which)
+        def _():
+            for q in range(4):
+                first = ((which + q // 2) % CORES * 2 + q % 2) * QUARTER
+                lanes = slice(first, first + QUARTER)
+                total = jnp.dot(r0[...], own[:, lanes], preferred_element_type=f32)
+                for k, rows in enumerate((r1, r2, r3)):
+                    total += jnp.dot(rows[...], held[q, k], preferred_element_type=f32)
                 out_ref[:, lanes] = total.astype(bf16)
 
 
-def out_project(info, rows, own, mine, theirs):
+def out_project(info, rows, own, held):
     return pl.pallas_call(
         out_kernel,
-        in_specs=specs(11),
+        in_specs=specs(6),
         out_specs=pl.BlockSpec(memory_space=pltpu.VMEM),
         out_shape=jax.ShapeDtypeStruct((BLOCK, WIDTH), bf16),
-        compiler_params=params(12),
+        compiler_params=params(8),
         cost_estimate=pl.CostEstimate(
             flops=2 * BLOCK * 1536 * WIDTH, bytes_accessed=10_500_000, transcendentals=0
         ),
         name="out_project",
-    )(info, *rows, own, *mine, *theirs)
+    )(info, *rows, own, held)
 
 
 def swap_cores(value):
@@ -330,32 +372,45 @@
     info = jnp.concatenate([here, jnp.stack([core, text_length[0], z * Y + y, plane])])
 
     own_out = project_out.reshape(TRIPLE, WIDTH)
-    half_out = lax.dynamic_slice_in_dim(own_out, core * (WIDTH // CORES), WIDTH // CORES, 1)
-    mine = [shifted(half_out, "head", PLANES, k) for k in (1, 2, 3)]
+    wide = WIDTH // CORES // 2
+    pieces = [
+        lax.dynamic_slice_in_dim(own_out, (2 * core + part) * wide, wide, 1) for part in range(2)
+    ]
 
     weights = jnp.transpose(project_in, (1, 0, 2))
     packed = project(video_tokens, text_tokens, weights)
     moved = lax.all_to_all(packed, ("z", "y"), 0, 0, tiled=True)
     partner = swap_cores(packed)
 
-    text_own = moved[:, TOKEN_PART:, :]
-    text_other = swap_cores(text_own)
+    right = [shifted(p, "head", PLANES, 1) for p in pieces]
+    left = [shifted(p, "head", PLANES, PLANES - 1) for p in pieces]
+    first_swap = [swap_cores(m) for m in right]
+    moved, partner, left, first_swap = lax.optimization_barrier((moved, partner, left, first_swap))
+    later_swap = [swap_cores(m) for m in left]
+    across = [
+        shifted(right[0], "head", PLANES, 1),
+        shifted(left[1], "head", PLANES, PLANES - 1),
+    ]
 
     first_piece = moved[0, :TOKEN_PART, HEAD:]
     copies = jnp.broadcast_to(first_piece[None], (Z,) + first_piece.shape)
     column = lax.all_to_all(copies, "z", 0, 0, tiled=True)
+    text_own = moved[:, TOKEN_PART:, :]
+    text_other = swap_cores(text_own)
     over_time, text = temporal(info, moved, text_own, text_other)
-    column, over_time = lax.optimization_barrier((column, over_time))
+    column, over_time, later_swap = lax.optimization_barrier((column, over_time, later_swap))
+    theirs = first_swap + later_swap
     back = lax.all_to_all(over_time, ("z", "y"), 0, 0, tiled=True)
     columns = [column] + [shifted(column, "y", Y, k) for k in range(1, Y)]
     firsts = columns + [swap_cores(c) for c in columns]
 
     over_space = spatial(info, packed, partner, firsts, text)
-    mine, over_space, back = lax.optimization_barrier((mine, over_space, back))
-    theirs = [swap_cores(m) for m in mine]
     parts = merge(info, over_space, back)
-    gathered = [parts[0]] + [shifted(parts[k], "head", PLANES, k) for k in (1, 2, 3)]
-    return out_project(info, gathered, own_out, mine, theirs)
+    mine = right + left + across
+    theirs = theirs + [swap_cores(a) for a in across]
+    held = hold(mine + theirs)
+    gathered = [parts[0]] + [shifted(parts[k], "head", PLANES, k) for k in (1, 3, 2)]
+    return out_project(info, gathered, own_out, held)
 
 
 def solution(mesh):

time: 121 us -> 116 us (0.959)
  waiting for transfers between devices: 43.8 us -> 36.5 us
  Pallas kernels: 23.8 us -> 26.9 us
  starting transfers between devices: 44 us -> 45.8 us
  local copies, waits for them, and re-layouts: 6.54 us -> 4.85 us
    all_to_all x1, waiting for transfers between devices: 26 us -> 1.89 us  [local(): moved = lax.all_to_all(packed, ('z', 'y'), 0, 0, tiled=True)]
    ppermute x9 -> x12, waiting for transfers between devices: 14.1 us -> 27.1 us  [shifted(): lax.ppermute(value, axis, [(i, (i + k) % count) for i in range(count)])]
    all_to_all x1, waiting for transfers between devices: 0.01 us -> 4.76 us  [local(): back = lax.all_to_all(over_time, ('z', 'y'), 0, 0, tiled=True)]
    pallas_call x3 -> x4, Pallas kernels: 9.66 us -> 12.7 us  [the longest x1 5.08 us: spatial(): pl.pallas_call(spatial_kernel, in_specs=specs(2 + 2 * Y) + [pl.BlockSpec(...]
    all_to_all x1, starting transfers between devices: 6.77 us -> 9.18 us  [local(): back = lax.all_to_all(over_time, ('z', 'y'), 0, 0, tiled=True)]
    dynamic_slice x1, local copies, waits for them, and re-layouts: 2.38 us -> 0.14 us  [local(): lax.dynamic_slice_in_dim(own_out, (2 * core + part) * wide, wide, 1)]
    ppermute x9 -> x12, starting transfers between devices: 19.2 us -> 17.9 us  [shifted(): lax.ppermute(value, axis, [(i, (i + k) % count) for i in range(count)])]
    unnamed x10 -> x12, local copies, waits for them, and re-layouts: 3.27 us -> 2.17 us
  transfers between devices with their start and end apart: 21 -> 27, of which waited for: 11 -> 10; matrix products, arithmetic and copies ran while one was open for 3% -> 2% of each run, Pallas kernels for 8% -> 13%
where the time goes in v3:
time: 116 us; the launch traced here: 115 us
  starting transfers between devices  45.8 us (39%)
  waiting for transfers between devices  36.5 us (31%)
  Pallas kernels  26.9 us (23%)
  local copies, waits for them, and re-layouts  4.85 us (4%)
    ppermute x12, waiting for transfers between devices, shifted(): lax.ppermute(value, axis, [(i, (i + k) % count) for i in range(count)])  27.1 us
    ppermute x12, starting transfers between devices, shifted(): lax.ppermute(value, axis, [(i, (i + k) % count) for i in range(count)])  17.9 us
    all_to_all x1, starting transfers between devices, local(): moved = lax.all_to_all(packed, ('z', 'y'), 0, 0, tiled=True)  11.5 us
    all_to_all x1, starting transfers between devices, local(): back = lax.all_to_all(over_time, ('z', 'y'), 0, 0, tiled=True)  9.18 us
    pallas_call x1, Pallas kernels, project(): pl.pallas_call(project_kernel, in_specs=[hbm, vmem, hbm], out_specs=vmem,...  8.96 us
    pallas_call x1, Pallas kernels, temporal(): pl.pallas_call(temporal_kernel, in_specs=specs(3), out_specs=[pl.BlockSpe...  5.3 us
    pallas_call x1, Pallas kernels, spatial(): pl.pallas_call(spatial_kernel, in_specs=specs(2 + 2 * Y) + [pl.BlockSpec(...  5.08 us
    all_to_all x1, starting transfers between devices, local(): column = lax.all_to_all(copies, 'z', 0, 0, tiled=True)  5 us
  transfers between devices with their start and end apart: 27, of which 10 were waited for; matrix products, arithmetic and copies ran while one was open for 2% of the time, Pallas kernels for 13%

profile of v3, /device:TPU:32, one launch (start us, length us, event | category | flops | bytes accessed | tf_op | source)
XLA Modules:
  0.0 115.0 jit_solution(16873520098495717973)
XLA Ops:
  0.0 9.0 %project.1.own = bf16[32,56,384]{2,1,0:T(8,128)(2,1)} custom-call(bf16[512,3072]{1,0:T(8,128)(2,1)} %x_hbm.1, bf16[4,3072]{1,0:T(4,128)(2,1)} %text_ref.1, bf16[3,3072,384]{2,1,0:T(8,128)(2,1)} %bitcast.9), custom_call_target="tpu_custom_call" | custom-call | flops 3623878656 | bytes 12000000 | tf_op jit(solution)/shard_map/project/pallas_call | solution.py:95
  9.0 11.5 %all-to-all-start = ((bf16[32,56,384]{2,1,0:T(8,128)(2,1)}), bf16[32,56,384]{2,1,0:T(8,128)(2,1)}, u32[]{:S(2)}, u32[]{:S(2)}) async-start(bf16[32,56,384]{2,1,0:T(8,128)(2,1)} %project.1.own), calls=%async_computation | async-start | bytes 2752512 | tf_op jit(solution)/shard_map/all_to_all | solution.py:382
  20.5 0.1 collective-permute-start
  20.7 0.1 constant_dynamic-slice_fusion
  20.8 1.6 %collective-permute-start.5 = (bf16[384,768]{1,0:T(8,128)(2,1)S(1)}, bf16[384,768]{1,0:T(8,128)(2,1)S(1)}, u32[]{:S(2)}, u32[]{:S(2)}) collective-permute-start(bf16[384,768]{1,0:T(8,128)(2,1)S(1)} %get-tuple-element.37), channel_id=1, source_target_pairs={{0,1},{1,2},{2,3},{3,0},{4,5},{5,6},{6,7},{7,4},{8,9},{9,10},{10,1... | collective-permute-start | bytes 1769480 | tf_op jit(solution)/shard_map/ppermute | solution.py:365
  22.4 1.5 %collective-permute-start.3 = (bf16[384,768]{1,0:T(8,128)(2,1)S(1)}, bf16[384,768]{1,0:T(8,128)(2,1)}, u32[]{:S(2)}, u32[]{:S(2)}) collective-permute-start(bf16[384,768]{1,0:T(8,128)(2,1)S(1)} %get-tuple-element.38), channel_id=1, source_target_pairs={{0,1},{1,2},{2,3},{3,0},{4,5},{5,6},{6,7},{7,4},{8,9},{9,10},{10,1... | collective-permute-start | bytes 1769480 | tf_op jit(solution)/shard_map/ppermute | solution.py:365
  23.9 1.7 %collective-permute-start.2 = (bf16[384,768]{1,0:T(8,128)(2,1)S(1)}, bf16[384,768]{1,0:T(8,128)(2,1)}, u32[]{:S(2)}, u32[]{:S(2)}) collective-permute-start(bf16[384,768]{1,0:T(8,128)(2,1)S(1)} %get-tuple-element.37), channel_id=1, source_target_pairs={{0,3},{1,0},{2,1},{3,2},{4,7},{5,4},{6,5},{7,6},{8,11},{9,8},{10,9... | collective-permute-start | bytes 1769480 | tf_op jit(solution)/shard_map/ppermute | solution.py:365
  25.6 0.5 collective-permute-start.1
  26.1 12.1 %collective-permute-done.5.refs_1_ = bf16[384,768]{1,0:T(8,128)(2,1)S(1)} collective-permute-done((bf16[384,768]{1,0:T(8,128)(2,1)S(1)}, bf16[384,768]{1,0:T(8,128)(2,1)S(1)}, u32[]{:S(2)}, u32[]{:S(2)}) %collective-permute-start.5) | collective-permute-done | bytes 589856 | tf_op jit(solution)/shard_map/ppermute | solution.py:365
  38.2 0.8 copy-done.2
  39.0 11.5 %collective-permute-done.3.refs_0_ = bf16[384,768]{1,0:T(8,128)(2,1)} collective-permute-done((bf16[384,768]{1,0:T(8,128)(2,1)S(1)}, bf16[384,768]{1,0:T(8,128)(2,1)}, u32[]{:S(2)}, u32[]{:S(2)}) %collective-permute-start.3) | collective-permute-done | bytes 589856 | tf_op jit(solution)/shard_map/ppermute | solution.py:365
  50.6 1.1 collective-permute-done.1.refs_2_
  51.7 1.2 %collective-permute-done.4.refs_6_ = bf16[384,768]{1,0:T(8,128)(2,1)} collective-permute-done((bf16[384,768]{1,0:T(8,128)(2,1)}, bf16[384,768]{1,0:T(8,128)(2,1)}, u32[]{:S(2)}, u32[]{:S(2)}) %collective-permute-start.4) | collective-permute-done | bytes 589856 | tf_op jit(solution)/shard_map/ppermute | solution.py:361
  52.9 1.9 %all-to-all-done.rows_ref = bf16[32,56,384]{2,1,0:T(8,128)(2,1)} async-done(((bf16[32,56,384]{2,1,0:T(8,128)(2,1)}), bf16[32,56,384]{2,1,0:T(8,128)(2,1)}, u32[]{:S(2)}, u32[]{:S(2)}) %all-to-all-start) | async-done | bytes 1376288 | tf_op jit(solution)/shard_map/all_to_all | solution.py:382
  54.8 0.5 collective-permute-start.9
  55.3 1.5 %collective-permute-start.20 = (bf16[384,768]{1,0:T(8,128)(2,1)}, bf16[384,768]{1,0:T(8,128)(2,1)}, u32[]{:S(2)}, u32[]{:S(2)}) collective-permute-start(bf16[384,768]{1,0:T(8,128)(2,1)} %collective-permute-done.3.refs_0_), channel_id=1, source_target_pairs={{0,1},{1,2},{2,3},{3,0},{4,5},{5,6},{6,7},{7,4},{8,9},{9,10},{10,1... | collective-permute-start | bytes 1769480 | tf_op jit(solution)/shard_map/ppermute | solution.py:365
  56.8 0.7 slice_bitcast_fusion
  57.5 0.7 broadcast_in_dim.8
  58.2 5.0 %all-to-all-start.1 = ((bf16[8,48,256]{2,1,0:T(8,128)(2,1)}), bf16[8,48,256]{2,1,0:T(8,128)(2,1)S(1)}, u32[]{:S(2)}, u32[]{:S(2)}) async-start(bf16[8,48,256]{2,1,0:T(8,128)(2,1)} %broadcast_in_dim.8), calls=%async_computation.1 | async-start | bytes 393216 | tf_op jit(solution)/shard_map/all_to_all | solution.py:397
  63.2 2.1 %collective-permute-start.21 = (bf16[384,768]{1,0:T(8,128)(2,1)}, bf16[384,768]{1,0:T(8,128)(2,1)}, u32[]{:S(2)}, u32[]{:S(2)}) collective-permute-start(bf16[384,768]{1,0:T(8,128)(2,1)} %collective-permute-done.2.refs_3_), channel_id=1, source_target_pairs={{0,3},{1,0},{2,1},{3,2},{4,7},{5,4},{6,5},{7,6},{8,11},{9,8},{10,9... | collective-permute-start | bytes 1769480 | tf_op jit(solution)/shard_map/ppermute | solution.py:365
  65.3 0.9 slice.7.text_own
  66.3 0.3 collective-permute-start.7
  67.2 0.1 dynamic_slice.9
  67.3 0.1 concatenate.3.info
  67.4 0.6 collective-permute-done.7.text_other
  68.0 5.3 %temporal.1 = (bf16[32,48,128]{2,1,0:T(8,128)(2,1)}, bf16[3,2,256,128]{3,2,1,0:T(8,128)(2,1)}) custom-call(s32[7]{0:T(128)S(1)} %concatenate.3.info, bf16[32,56,384]{2,1,0:T(8,128)(2,1)} %all-to-all-done.rows_ref, bf16[32,8,384]{2,1,0:T(8,128)(2,1)S(1)} %slice.7.text_own, bf16[32,8,384]{2,1,0:T(8,128)(2,1)S(1)} %collective-permute-done.7.text_other), custom_call_target="tpu_custom_call" | custom-call | flops 400000000 | bytes 3000000 | tf_op jit(solution)/shard_map/temporal/pallas_call | solution.py:186
  73.3 2.7 %collective-permute-start.12 = (bf16[8,48,256]{2,1,0:T(8,128)(2,1)S(1)}, bf16[8,48,256]{2,1,0:T(8,128)(2,1)S(1)}, u32[]{:S(2)}, u32[]{:S(2)}) collective-permute-start(bf16[8,48,256]{2,1,0:T(8,128)(2,1)S(1)} %all-to-all-done.1.refs_0_), channel_id=1, source_target_pairs={{0,24},{8,0},{16,8},{24,16},{1,25},{9,1},{17,9},{25,17},{2,26},{10... | collective-permute-start | bytes 589832 | tf_op jit(solution)/shard_map/ppermute | solution.py:365
  76.0 0.9 collective-permute-start.11
  76.9 0.9 collective-permute-start.10
  77.7 9.2 %all-to-all-start.2 = ((bf16[32,48,128]{2,1,0:T(8,128)(2,1)}), bf16[32,48,128]{2,1,0:T(8,128)(2,1)S(1)}, u32[]{:S(2)}, u32[]{:S(2)}) async-start(bf16[32,48,128]{2,1,0:T(8,128)(2,1)} %get-tuple-element.28), calls=%async_computation.2 | async-start | bytes 786432 | tf_op jit(solution)/shard_map/all_to_all | solution.py:403
  86.9 0.1 collective-permute-start.13
  87.1 0.5 collective-permute-start.16
  87.6 0.1 collective-permute-start.15
  87.7 0.8 collective-permute-done.10.refs_1_
  88.4 0.0 collective-permute-start.14
  88.4 0.5 collective-permute-start.22
  88.9 0.1 collective-permute-start.23
  89.0 0.9 collective-permute-done.14.refs_5_
  89.9 1.3 %copy-done.1 = bf16[32,56,384]{2,1,0:T(8,128)(2,1)S(1)} copy-done((bf16[32,56,384]{2,1,0:T(8,128)(2,1)S(1)}, bf16[32,56,384]{2,1,0:T(8,128)(2,1)}, u32[]{:S(2)}) %copy-start.1) | copy-done | bytes 1376280
  91.3 5.1 %spatial.1.spatial_ref = bf16[512,384]{1,0:T(8,128)(2,1)} custom-call(s32[7]{0:T(128)S(1)} %concatenate.3.info, bf16[32,56,384]{2,1,0:T(8,128)(2,1)S(1)} %copy-done.1, bf16[32,56,384]{2,1,0:T(8,128)(2,1)} %collective-permute-done.partner, bf16[8,48,256]{2,1,0:T(8,128)(2,1)S(1)} %all-to-all-done.1.refs_0_, ...), custom_call_target="tpu_custom_call" | custom-call | flops 4000000000 | bytes 1000000 | tf_op jit(solution)/shard_map/spatial/pallas_call | solution.py:252
  96.3 4.8 %all-to-all-done.2.back = bf16[32,48,128]{2,1,0:T(8,128)(2,1)S(1)} async-done(((bf16[32,48,128]{2,1,0:T(8,128)(2,1)}), bf16[32,48,128]{2,1,0:T(8,128)(2,1)S(1)}, u32[]{:S(2)}, u32[]{:S(2)}) %all-to-all-start.2) | async-done | bytes 393248 | tf_op jit(solution)/shard_map/all_to_all | solution.py:403
  101.1 1.2 %merge.1 = (bf16[128,384]{1,0:T(8,128)(2,1)S(1)}, bf16[128,384]{1,0:T(8,128)(2,1)S(1)}, bf16[128,384]{1,0:T(8,128)(2,1)S(1)}, bf16[128,384]{1,0:T(8,128)(2,1)S(1)}) custom-call(s32[7]{0:T(128)S(1)} %concatenate.3.info, bf16[512,384]{1,0:T(8,128)(2,1)} %spatial.1.spatial_ref, bf16[32,48,128]{2,1,0:T(8,128)(2,1)S(1)} %all-to-all-done.2.back), custom_call_target="tpu_custom_call" | custom-call | tf_op jit(solution)/shard_map/merge/pallas_call | solution.py:287
  102.3 0.1 collective-permute-start.17
  102.4 3.2 %collective-permute-start.18 = (bf16[128,384]{1,0:T(8,128)(2,1)S(1)}, bf16[128,384]{1,0:T(8,128)(2,1)S(1)}, u32[]{:S(2)}, u32[]{:S(2)}) collective-permute-start(bf16[128,384]{1,0:T(8,128)(2,1)S(1)} %get-tuple-element.31), channel_id=1, source_target_pairs={{0,3},{1,0},{2,1},{3,2},{4,7},{5,4},{6,5},{7,6},{8,11},{9,8},{10,9... | collective-permute-start | bytes 294920 | tf_op jit(solution)/shard_map/ppermute | solution.py:365
  105.6 1.3 %collective-permute-start.19 = (bf16[128,384]{1,0:T(8,128)(2,1)S(1)}, bf16[128,384]{1,0:T(8,128)(2,1)S(1)}, u32[]{:S(2)}, u32[]{:S(2)}) collective-permute-start(bf16[128,384]{1,0:T(8,128)(2,1)S(1)} %get-tuple-element.32), channel_id=1, source_target_pairs={{0,2},{1,3},{2,0},{3,1},{4,6},{5,7},{6,4},{7,5},{8,10},{9,11},{10,... | collective-permute-start | bytes 294920 | tf_op jit(solution)/shard_map/ppermute | solution.py:365
  106.9 3.2 %hold.1.held = bf16[4,3,384,768]{3,2,1,0:T(8,128)(2,1)S(1)} custom-call(bf16[384,768]{1,0:T(8,128)(2,1)} %collective-permute-done.3.refs_0_, bf16[384,768]{1,0:T(8,128)(2,1)} %copy-done.2, bf16[384,768]{1,0:T(8,128)(2,1)} %copy-done.3, bf16[384,768]{1,0:T(8,128)(2,1)} %collective-permute-done.2.refs_3_, bf16[384,768]{1,0:T(8,128)(2,1)} %collective-permute-done.20.refs_4_, ...), custom_call_target="tpu_custom_call" | custom-call | flops 1000000 | bytes 7000000 | tf_op jit(solution)/shard_map/hold/pallas_call | solution.py:317
  110.1 1.7 %collective-permute-done.19.r3 = bf16[128,384]{1,0:T(8,128)(2,1)S(1)} collective-permute-done((bf16[128,384]{1,0:T(8,128)(2,1)S(1)}, bf16[128,384]{1,0:T(8,128)(2,1)S(1)}, u32[]{:S(2)}, u32[]{:S(2)}) %collective-permute-start.19) | collective-permute-done | bytes 98336 | tf_op jit(solution)/shard_map/ppermute | solution.py:365
  111.8 3.2 %out_project.1 = bf16[128,3072]{1,0:T(8,128)(2,1)} custom-call(s32[7]{0:T(128)S(1)} %concatenate.3.info, bf16[128,384]{1,0:T(8,128)(2,1)S(1)} %get-tuple-element.29.r0, bf16[128,384]{1,0:T(8,128)(2,1)S(1)} %collective-permute-done.17.r1, bf16[128,384]{1,0:T(8,128)(2,1)S(1)} %collective-permute-done.18.r2, bf16[128,384]{1,0:T(8,128)(2,1)S(1)} %collective-permute-done.19.r3, ...), custom_call_target="tpu_custom_call" | custom-call | flops 1207959552 | bytes 10500000 | tf_op jit(solution)/shard_map/out_project/pallas_call | solution.py:347
  (30 shorter events, 0.1 us)
Async XLA Ops:
  9.0 11.7 %copy-start = (bf16[3,128,3072]{2,1,0:T(8,128)(2,1)S(1)}, bf16[3,128,3072]{2,1,0:T(8,128)(2,1)}, u32[]{:S(2)}) copy-start(bf16[3,128,3072]{2,1,0:T(8,128)(2,1)} %param.9) | copy-start | bytes 7077892
  9.0 45.8 %all-to-all-start = ((bf16[32,56,384]{2,1,0:T(8,128)(2,1)}), bf16[32,56,384]{2,1,0:T(8,128)(2,1)}, u32[]{:S(2)}, u32[]{:S(2)}) async-start(bf16[32,56,384]{2,1,0:T(8,128)(2,1)} %project.1.own), calls=%async_computation | async-start | bytes 2752512 | tf_op jit(solution)/shard_map/all_to_all | solution.py:382
  20.5 46.7 %copy-start.5 = (s32[12]{0:T(128)S(1)}, s32[12]{0:T(128)}, u32[]{:S(2)}) copy-start(s32[12]{0:T(128)} %param.10) | copy-start | bytes 148
  20.5 32.3 %collective-permute-start = (bf16[32,56,384]{2,1,0:T(8,128)(2,1)}, bf16[32,56,384]{2,1,0:T(8,128)(2,1)}, u32[]{:S(2)}, u32[]{:S(2)}) collective-permute-start(bf16[32,56,384]{2,1,0:T(8,128)(2,1)} %project.1.own), channel_id=1, source_target_pairs={{0,4},{4,0},{1,5},{5,1},{2,6},{6,2},{3,7},{7,3},{8,12},{12,8},{9,1... | collective-permute-start | bytes 4128776 | tf_op jit(solution)/shard_map/ppermute | solution.py:361
  20.8 17.4 %collective-permute-start.5 = (bf16[384,768]{1,0:T(8,128)(2,1)S(1)}, bf16[384,768]{1,0:T(8,128)(2,1)S(1)}, u32[]{:S(2)}, u32[]{:S(2)}) collective-permute-start(bf16[384,768]{1,0:T(8,128)(2,1)S(1)} %get-tuple-element.37), channel_id=1, source_target_pairs={{0,1},{1,2},{2,3},{3,0},{4,5},{5,6},{6,7},{7,4},{8,9},{9,10},{10,1... | collective-permute-start | bytes 1769480 | tf_op jit(solution)/shard_map/ppermute | solution.py:365
  22.4 28.2 %collective-permute-start.3 = (bf16[384,768]{1,0:T(8,128)(2,1)S(1)}, bf16[384,768]{1,0:T(8,128)(2,1)}, u32[]{:S(2)}, u32[]{:S(2)}) collective-permute-start(bf16[384,768]{1,0:T(8,128)(2,1)S(1)} %get-tuple-element.38), channel_id=1, source_target_pairs={{0,1},{1,2},{2,3},{3,0},{4,5},{5,6},{6,7},{7,4},{8,9},{9,10},{10,1... | collective-permute-start | bytes 1769480 | tf_op jit(solution)/shard_map/ppermute | solution.py:365
  23.9 26.7 %collective-permute-start.2 = (bf16[384,768]{1,0:T(8,128)(2,1)S(1)}, bf16[384,768]{1,0:T(8,128)(2,1)}, u32[]{:S(2)}, u32[]{:S(2)}) collective-permute-start(bf16[384,768]{1,0:T(8,128)(2,1)S(1)} %get-tuple-element.37), channel_id=1, source_target_pairs={{0,3},{1,0},{2,1},{3,2},{4,7},{5,4},{6,5},{7,6},{8,11},{9,8},{10,9... | collective-permute-start | bytes 1769480 | tf_op jit(solution)/shard_map/ppermute | solution.py:365
  25.6 26.0 %collective-permute-start.1 = (bf16[384,768]{1,0:T(8,128)(2,1)S(1)}, bf16[384,768]{1,0:T(8,128)(2,1)S(1)}, u32[]{:S(2)}, u32[]{:S(2)}) collective-permute-start(bf16[384,768]{1,0:T(8,128)(2,1)S(1)} %get-tuple-element.38), channel_id=1, source_target_pairs={{0,3},{1,0},{2,1},{3,2},{4,7},{5,4},{6,5},{7,6},{8,11},{9,8},{10,9... | collective-permute-start | bytes 1769480 | tf_op jit(solution)/shard_map/ppermute | solution.py:365
  38.2 0.8 copy-start.2
  39.0 12.6 %collective-permute-start.6 = (bf16[384,768]{1,0:T(8,128)(2,1)S(1)}, bf16[384,768]{1,0:T(8,128)(2,1)S(1)}, u32[]{:S(2)}, u32[]{:S(2)}) collective-permute-start(bf16[384,768]{1,0:T(8,128)(2,1)S(1)} %collective-permute-done.5.refs_1_), channel_id=1, source_target_pairs={{0,4},{4,0},{1,5},{5,1},{2,6},{6,2},{3,7},{7,3},{8,12},{12,8},{9,1... | collective-permute-start | bytes 1769480 | tf_op jit(solution)/shard_map/ppermute | solution.py:361
  50.5 2.3 %collective-permute-start.4 = (bf16[384,768]{1,0:T(8,128)(2,1)}, bf16[384,768]{1,0:T(8,128)(2,1)}, u32[]{:S(2)}, u32[]{:S(2)}) collective-permute-start(bf16[384,768]{1,0:T(8,128)(2,1)} %collective-permute-done.3.refs_0_), channel_id=1, source_target_pairs={{0,4},{4,0},{1,5},{5,1},{2,6},{6,2},{3,7},{7,3},{8,12},{12,8},{9,1... | collective-permute-start | bytes 1769480 | tf_op jit(solution)/shard_map/ppermute | solution.py:361
  51.7 21.6 %copy-start.3 = (bf16[384,768]{1,0:T(8,128)(2,1)}, bf16[384,768]{1,0:T(8,128)(2,1)S(1)}, u32[]{:S(2)}) copy-start(bf16[384,768]{1,0:T(8,128)(2,1)S(1)} %collective-permute-done.1.refs_2_) | copy-start | bytes 1769476
  51.7 6.6 %copy-start.4 = (bf16[384,768]{1,0:T(8,128)(2,1)}, bf16[384,768]{1,0:T(8,128)(2,1)S(1)}, u32[]{:S(2)}) copy-start(bf16[384,768]{1,0:T(8,128)(2,1)S(1)} %collective-permute-done.6.refs_7_) | copy-start | bytes 1769476
  54.8 18.5 %collective-permute-start.8 = (bf16[384,768]{1,0:T(8,128)(2,1)S(1)}, bf16[384,768]{1,0:T(8,128)(2,1)}, u32[]{:S(2)}, u32[]{:S(2)}) collective-permute-start(bf16[384,768]{1,0:T(8,128)(2,1)S(1)} %collective-permute-done.1.refs_2_), channel_id=1, source_target_pairs={{0,4},{4,0},{1,5},{5,1},{2,6},{6,2},{3,7},{7,3},{8,12},{12,8},{9,1... | collective-permute-start | bytes 1769480 | tf_op jit(solution)/shard_map/ppermute | solution.py:361
  54.8 18.5 %collective-permute-start.9 = (bf16[384,768]{1,0:T(8,128)(2,1)}, bf16[384,768]{1,0:T(8,128)(2,1)}, u32[]{:S(2)}, u32[]{:S(2)}) collective-permute-start(bf16[384,768]{1,0:T(8,128)(2,1)} %collective-permute-done.2.refs_3_), channel_id=1, source_target_pairs={{0,4},{4,0},{1,5},{5,1},{2,6},{6,2},{3,7},{7,3},{8,12},{12,8},{9,1... | collective-permute-start | bytes 1769480 | tf_op jit(solution)/shard_map/ppermute | solution.py:361
  55.3 31.6 %collective-permute-start.20 = (bf16[384,768]{1,0:T(8,128)(2,1)}, bf16[384,768]{1,0:T(8,128)(2,1)}, u32[]{:S(2)}, u32[]{:S(2)}) collective-permute-start(bf16[384,768]{1,0:T(8,128)(2,1)} %collective-permute-done.3.refs_0_), channel_id=1, source_target_pairs={{0,1},{1,2},{2,3},{3,0},{4,5},{5,6},{6,7},{7,4},{8,9},{9,10},{10,1... | collective-permute-start | bytes 1769480 | tf_op jit(solution)/shard_map/ppermute | solution.py:365
  58.2 15.0 %all-to-all-start.1 = ((bf16[8,48,256]{2,1,0:T(8,128)(2,1)}), bf16[8,48,256]{2,1,0:T(8,128)(2,1)S(1)}, u32[]{:S(2)}, u32[]{:S(2)}) async-start(bf16[8,48,256]{2,1,0:T(8,128)(2,1)} %broadcast_in_dim.8), calls=%async_computation.1 | async-start | bytes 393216 | tf_op jit(solution)/shard_map/all_to_all | solution.py:397
  63.2 25.2 %collective-permute-start.21 = (bf16[384,768]{1,0:T(8,128)(2,1)}, bf16[384,768]{1,0:T(8,128)(2,1)}, u32[]{:S(2)}, u32[]{:S(2)}) collective-permute-start(bf16[384,768]{1,0:T(8,128)(2,1)} %collective-permute-done.2.refs_3_), channel_id=1, source_target_pairs={{0,3},{1,0},{2,1},{3,2},{4,7},{5,4},{6,5},{7,6},{8,11},{9,8},{10,9... | collective-permute-start | bytes 1769480 | tf_op jit(solution)/shard_map/ppermute | solution.py:365
  66.3 1.7 %collective-permute-start.7 = (bf16[32,8,384]{2,1,0:T(8,128)(2,1)S(1)}, bf16[32,8,384]{2,1,0:T(8,128)(2,1)S(1)}, u32[]{:S(2)}, u32[]{:S(2)}) collective-permute-start(bf16[32,8,384]{2,1,0:T(8,128)(2,1)S(1)} %slice.7.text_own), channel_id=1, source_target_pairs={{0,4},{4,0},{1,5},{5,1},{2,6},{6,2},{3,7},{7,3},{8,12},{12,8},{9,1... | collective-permute-start | bytes 589832 | tf_op jit(solution)/shard_map/ppermute | solution.py:361
  73.3 13.8 %collective-permute-start.12 = (bf16[8,48,256]{2,1,0:T(8,128)(2,1)S(1)}, bf16[8,48,256]{2,1,0:T(8,128)(2,1)S(1)}, u32[]{:S(2)}, u32[]{:S(2)}) collective-permute-start(bf16[8,48,256]{2,1,0:T(8,128)(2,1)S(1)} %all-to-all-done.1.refs_0_), channel_id=1, source_target_pairs={{0,24},{8,0},{16,8},{24,16},{1,25},{9,1},{17,9},{25,17},{2,26},{10... | collective-permute-start | bytes 589832 | tf_op jit(solution)/shard_map/ppermute | solution.py:365
  76.0 11.5 %collective-permute-start.11 = (bf16[8,48,256]{2,1,0:T(8,128)(2,1)S(1)}, bf16[8,48,256]{2,1,0:T(8,128)(2,1)S(1)}, u32[]{:S(2)}, u32[]{:S(2)}) collective-permute-start(bf16[8,48,256]{2,1,0:T(8,128)(2,1)S(1)} %all-to-all-done.1.refs_0_), channel_id=1, source_target_pairs={{0,16},{8,24},{16,0},{24,8},{1,17},{9,25},{17,1},{25,9},{2,18},{10... | collective-permute-start | bytes 589832 | tf_op jit(solution)/shard_map/ppermute | solution.py:365
  76.9 11.5 %collective-permute-start.10 = (bf16[8,48,256]{2,1,0:T(8,128)(2,1)S(1)}, bf16[8,48,256]{2,1,0:T(8,128)(2,1)S(1)}, u32[]{:S(2)}, u32[]{:S(2)}) collective-permute-start(bf16[8,48,256]{2,1,0:T(8,128)(2,1)S(1)} %all-to-all-done.1.refs_0_), channel_id=1, source_target_pairs={{0,8},{8,16},{16,24},{24,0},{1,9},{9,17},{17,25},{25,1},{2,10},{10... | collective-permute-start | bytes 589832 | tf_op jit(solution)/shard_map/ppermute | solution.py:365
  77.7 23.4 %all-to-all-start.2 = ((bf16[32,48,128]{2,1,0:T(8,128)(2,1)}), bf16[32,48,128]{2,1,0:T(8,128)(2,1)S(1)}, u32[]{:S(2)}, u32[]{:S(2)}) async-start(bf16[32,48,128]{2,1,0:T(8,128)(2,1)} %get-tuple-element.28), calls=%async_computation.2 | async-start | bytes 786432 | tf_op jit(solution)/shard_map/all_to_all | solution.py:403
  86.9 2.0 %collective-permute-start.13 = (bf16[8,48,256]{2,1,0:T(8,128)(2,1)S(1)}, bf16[8,48,256]{2,1,0:T(8,128)(2,1)S(1)}, u32[]{:S(2)}, u32[]{:S(2)}) collective-permute-start(bf16[8,48,256]{2,1,0:T(8,128)(2,1)S(1)} %all-to-all-done.1.refs_0_), channel_id=1, source_target_pairs={{0,4},{4,0},{1,5},{5,1},{2,6},{6,2},{3,7},{7,3},{8,12},{12,8},{9,1... | collective-permute-start | bytes 589832 | tf_op jit(solution)/shard_map/ppermute | solution.py:361
  87.1 2.0 %collective-permute-start.16 = (bf16[8,48,256]{2,1,0:T(8,128)(2,1)S(1)}, bf16[8,48,256]{2,1,0:T(8,128)(2,1)S(1)}, u32[]{:S(2)}, u32[]{:S(2)}) collective-permute-start(bf16[8,48,256]{2,1,0:T(8,128)(2,1)S(1)} %collective-permute-done.12.refs_3_), channel_id=1, source_target_pairs={{0,4},{4,0},{1,5},{5,1},{2,6},{6,2},{3,7},{7,3},{8,12},{12,8},{9,1... | collective-permute-start | bytes 589832 | tf_op jit(solution)/shard_map/ppermute | solution.py:361
  87.6 1.5 %collective-permute-start.15 = (bf16[8,48,256]{2,1,0:T(8,128)(2,1)S(1)}, bf16[8,48,256]{2,1,0:T(8,128)(2,1)S(1)}, u32[]{:S(2)}, u32[]{:S(2)}) collective-permute-start(bf16[8,48,256]{2,1,0:T(8,128)(2,1)S(1)} %collective-permute-done.11.refs_2_), channel_id=1, source_target_pairs={{0,4},{4,0},{1,5},{5,1},{2,6},{6,2},{3,7},{7,3},{8,12},{12,8},{9,1... | collective-permute-start | bytes 589832 | tf_op jit(solution)/shard_map/ppermute | solution.py:361
  88.4 1.5 %collective-permute-start.14 = (bf16[8,48,256]{2,1,0:T(8,128)(2,1)S(1)}, bf16[8,48,256]{2,1,0:T(8,128)(2,1)S(1)}, u32[]{:S(2)}, u32[]{:S(2)}) collective-permute-start(bf16[8,48,256]{2,1,0:T(8,128)(2,1)S(1)} %collective-permute-done.10.refs_1_), channel_id=1, source_target_pairs={{0,4},{4,0},{1,5},{5,1},{2,6},{6,2},{3,7},{7,3},{8,12},{12,8},{9,1... | collective-permute-start | bytes 589832 | tf_op jit(solution)/shard_map/ppermute | solution.py:361
  88.4 18.5 %collective-permute-start.22 = (bf16[384,768]{1,0:T(8,128)(2,1)}, bf16[384,768]{1,0:T(8,128)(2,1)}, u32[]{:S(2)}, u32[]{:S(2)}) collective-permute-start(bf16[384,768]{1,0:T(8,128)(2,1)} %collective-permute-done.20.refs_4_), channel_id=1, source_target_pairs={{0,4},{4,0},{1,5},{5,1},{2,6},{6,2},{3,7},{7,3},{8,12},{12,8},{9,1... | collective-permute-start | bytes 1769480 | tf_op jit(solution)/shard_map/ppermute | solution.py:361
  88.9 18.0 %collective-permute-start.23 = (bf16[384,768]{1,0:T(8,128)(2,1)}, bf16[384,768]{1,0:T(8,128)(2,1)}, u32[]{:S(2)}, u32[]{:S(2)}) collective-permute-start(bf16[384,768]{1,0:T(8,128)(2,1)} %collective-permute-done.21.refs_5_), channel_id=1, source_target_pairs={{0,4},{4,0},{1,5},{5,1},{2,6},{6,2},{3,7},{7,3},{8,12},{12,8},{9,1... | collective-permute-start | bytes 1769480 | tf_op jit(solution)/shard_map/ppermute | solution.py:361
  89.9 1.3 %copy-start.1 = (bf16[32,56,384]{2,1,0:T(8,128)(2,1)S(1)}, bf16[32,56,384]{2,1,0:T(8,128)(2,1)}, u32[]{:S(2)}) copy-start(bf16[32,56,384]{2,1,0:T(8,128)(2,1)} %project.1.own) | copy-start | bytes 4128772
  102.3 7.8 %collective-permute-start.17 = (bf16[128,384]{1,0:T(8,128)(2,1)S(1)}, bf16[128,384]{1,0:T(8,128)(2,1)S(1)}, u32[]{:S(2)}, u32[]{:S(2)}) collective-permute-start(bf16[128,384]{1,0:T(8,128)(2,1)S(1)} %get-tuple-element.30), channel_id=1, source_target_pairs={{0,1},{1,2},{2,3},{3,0},{4,5},{5,6},{6,7},{7,4},{8,9},{9,10},{10,1... | collective-permute-start | bytes 294920 | tf_op jit(solution)/shard_map/ppermute | solution.py:365
  102.4 7.7 %collective-permute-start.18 = (bf16[128,384]{1,0:T(8,128)(2,1)S(1)}, bf16[128,384]{1,0:T(8,128)(2,1)S(1)}, u32[]{:S(2)}, u32[]{:S(2)}) collective-permute-start(bf16[128,384]{1,0:T(8,128)(2,1)S(1)} %get-tuple-element.31), channel_id=1, source_target_pairs={{0,3},{1,0},{2,1},{3,2},{4,7},{5,4},{6,5},{7,6},{8,11},{9,8},{10,9... | collective-permute-start | bytes 294920 | tf_op jit(solution)/shard_map/ppermute | solution.py:365
  105.6 6.1 %collective-permute-start.19 = (bf16[128,384]{1,0:T(8,128)(2,1)S(1)}, bf16[128,384]{1,0:T(8,128)(2,1)S(1)}, u32[]{:S(2)}, u32[]{:S(2)}) collective-permute-start(bf16[128,384]{1,0:T(8,128)(2,1)S(1)} %get-tuple-element.32), channel_id=1, source_target_pairs={{0,2},{1,3},{2,0},{3,1},{4,6},{5,7},{6,4},{7,5},{8,10},{9,11},{10,... | collective-permute-start | bytes 294920 | tf_op jit(solution)/shard_map/ppermute | solution.py:365

commit v4 on v3

--- a/solution.py
+++ b/solution.py
@@ -139,7 +139,7 @@
     for side, source in enumerate((text_own, text_other)):
         for h in range(HEADS_HERE):
             lanes = source[:, :, h * HEAD : (h + 1) * HEAD].astype(f32)
-            spread[...] = lanes.reshape(CHIPS * 2 * TEXT_HERE, HEAD)
+            spread[: CHIPS * 2 * TEXT_HERE, :] = lanes.reshape(CHIPS * 2 * TEXT_HERE, HEAD)
             for kind in range(2):
                 for t in range(TEXT_HERE):
                     rows = pl.ds(kind * TEXT_HERE + t, CHIPS, stride=2 * TEXT_HERE)
@@ -191,7 +191,7 @@
             pltpu.HBM((CHIPS, TOKEN_PART, HEAD), bf16),
             pltpu.HBM((HEADS_HERE, 2, CORES * TEXT_CORE, HEAD), bf16),
         ],
-        scratch_shapes=[pltpu.VMEM((CHIPS * 2 * TEXT_HERE, HEAD), f32)],
+        scratch_shapes=[pltpu.VMEM(((CHIPS + 1) * 2 * TEXT_HERE, HEAD), f32)],
         compiler_params=params(14),
         cost_estimate=pl.CostEstimate(
             flops=400_000_000, bytes_accessed=3_000_000, transcendentals=1_200_000
@@ -357,6 +357,31 @@
     )(info, *rows, own, held)
 
 
+def repeat_kernel(rows_hbm, out_ref, piece, sem):
+    copy = pltpu.make_async_copy(
+        rows_hbm.at[0, pl.ds(0, TOKEN_PART), pl.ds(HEAD, 2 * HEAD)], piece, sem.at[0]
+    )
+    copy.start()
+    copy.wait()
+    out_ref[...] = jnp.broadcast_to(piece[...][None], out_ref.shape)
+
+
+def repeat_first(rows):
+    return pl.pallas_call(
+        repeat_kernel,
+        in_specs=[pl.BlockSpec(memory_space=pltpu.HBM)],
+        out_specs=pl.BlockSpec(memory_space=pltpu.VMEM),
+        out_shape=jax.ShapeDtypeStruct((Z, TOKEN_PART, 2 * HEAD), bf16),
+        scratch_shapes=[
+            pltpu.VMEM((TOKEN_PART, 2 * HEAD), bf16),
+            pltpu.SemaphoreType.DMA((1,)),
+        ],
+        compiler_params=params(4),
+        cost_estimate=pl.CostEstimate(flops=0, bytes_accessed=300_000, transcendentals=0),
+        name="repeat_first",
+    )(rows)
+
+
 def swap_cores(value):
     return lax.ppermute(value, "core", [(0, 1), (1, 0)])
 
@@ -392,9 +417,7 @@
         shifted(left[1], "head", PLANES, PLANES - 1),
     ]
 
-    first_piece = moved[0, :TOKEN_PART, HEAD:]
-    copies = jnp.broadcast_to(first_piece[None], (Z,) + first_piece.shape)
-    column = lax.all_to_all(copies, "z", 0, 0, tiled=True)
+    column = lax.all_to_all(repeat_first(moved), "z", 0, 0, tiled=True)
     text_own = moved[:, TOKEN_PART:, :]
     text_other = swap_cores(text_own)
     over_time, text = temporal(info, moved, text_own, text_other)

time: 116 us -> 115 us (level)
  local copies, waits for them, and re-layouts: 4.85 us -> 2.34 us
  Pallas kernels: 26.9 us -> 28.1 us
    pallas_call x1, Pallas kernels: 5.08 us -> 7.74 us  [spatial(): pl.pallas_call(spatial_kernel, in_specs=specs(2 + 2 * Y) + [pl.BlockSpec(...]
    pallas_call x1, Pallas kernels: 5.3 us -> 3.15 us  [temporal(): pl.pallas_call(temporal_kernel, in_specs=specs(3), out_specs=[pl.BlockSpe...]
    all_to_all x1, waiting for transfers between devices: 1.89 us -> 0.01 us  [local(): moved = lax.all_to_all(packed, ('z', 'y'), 0, 0, tiled=True)]
    all_to_all x1, waiting for transfers between devices: 0.01 us -> 1.88 us  [local(): column = lax.all_to_all(repeat_first(moved), 'z', 0, 0, tiled=True)]
    all_to_all x1, starting transfers between devices: 9.18 us -> 7.38 us  [local(): back = lax.all_to_all(over_time, ('z', 'y'), 0, 0, tiled=True)]
    all_to_all x1, starting transfers between devices: 5 us -> 6.8 us  [local(): column = lax.all_to_all(repeat_first(moved), 'z', 0, 0, tiled=True)]
    all_to_all x1, waiting for transfers between devices: 4.76 us -> 3.31 us  [local(): back = lax.all_to_all(over_time, ('z', 'y'), 0, 0, tiled=True)]
    broadcast_in_dim x2 -> x0, local copies, waits for them, and re-layouts: 1.43 us -> none  [local(): copies = jnp.broadcast_to(first_piece[None], (Z,) + first_piece.shape)]
  transfers between devices with their start and end apart: 27 -> 27, of which waited for: 10 -> 10; matrix products, arithmetic and copies ran while one was open for 2% -> 1% of each run, Pallas kernels for 13% -> 14%
where the time goes in v4:
time: 115 us; the launch traced here: 113 us
  starting transfers between devices  46.1 us (40%)
  waiting for transfers between devices  35.7 us (31%)
  Pallas kernels  28.1 us (24%)
  local copies, waits for them, and re-layouts  2.34 us (2%)
    ppermute x12, waiting for transfers between devices, shifted(): lax.ppermute(value, axis, [(i, (i + k) % count) for i in range(count)])  27.8 us
    ppermute x12, starting transfers between devices, shifted(): lax.ppermute(value, axis, [(i, (i + k) % count) for i in range(count)])  18.2 us
    all_to_all x1, starting transfers between devices, local(): moved = lax.all_to_all(packed, ('z', 'y'), 0, 0, tiled=True)  11.5 us
    pallas_call x1, Pallas kernels, project(): pl.pallas_call(project_kernel, in_specs=[hbm, vmem, hbm], out_specs=vmem,...  8.93 us
    pallas_call x1, Pallas kernels, spatial(): pl.pallas_call(spatial_kernel, in_specs=specs(2 + 2 * Y) + [pl.BlockSpec(...  7.74 us
    all_to_all x1, starting transfers between devices, local(): back = lax.all_to_all(over_time, ('z', 'y'), 0, 0, tiled=True)  7.38 us
    all_to_all x1, starting transfers between devices, local(): column = lax.all_to_all(repeat_first(moved), 'z', 0, 0, tiled=True)  6.8 us
    all_to_all x1, waiting for transfers between devices, local(): back = lax.all_to_all(over_time, ('z', 'y'), 0, 0, tiled=True)  3.31 us
  transfers between devices with their start and end apart: 27, of which 10 were waited for; matrix products, arithmetic and copies ran while one was open for 1% of the time, Pallas kernels for 14%

profile of v4, /device:TPU:32, one launch (start us, length us, event | category | flops | bytes accessed | tf_op | source)
XLA Modules:
  0.0 113.0 jit_solution(11341464287218220526)
XLA Ops:
  0.0 8.9 %project.1.own = bf16[32,56,384]{2,1,0:T(8,128)(2,1)} custom-call(bf16[512,3072]{1,0:T(8,128)(2,1)} %x_hbm.1, bf16[4,3072]{1,0:T(4,128)(2,1)} %text_ref.1, bf16[3,3072,384]{2,1,0:T(8,128)(2,1)} %bitcast.7), custom_call_target="tpu_custom_call" | custom-call | flops 3623878656 | bytes 12000000 | tf_op jit(solution)/shard_map/project/pallas_call | solution.py:95
  8.9 11.5 %all-to-all-start = ((bf16[32,56,384]{2,1,0:T(8,128)(2,1)}), bf16[32,56,384]{2,1,0:T(8,128)(2,1)S(1)}, u32[]{:S(2)}, u32[]{:S(2)}) async-start(bf16[32,56,384]{2,1,0:T(8,128)(2,1)} %project.1.own), calls=%async_computation | async-start | bytes 2752512 | tf_op jit(solution)/shard_map/all_to_all | solution.py:407
  20.5 0.1 collective-permute-start
  20.6 0.0 copy-start.5
  20.6 1.3 %constant_dynamic-slice_fusion = (bf16[384,768]{1,0:T(8,128)(2,1)S(1)}, bf16[384,768]{1,0:T(8,128)(2,1)S(1)}) fusion(bf16[384,3072]{1,0:T(8,128)(2,1)} %bitcast.5, s32[]{:T(128)S(6)} %select_n.11, s32[]{:T(128)S(6)} %select_n.10), kind=kLoop, calls=%fused_computation | loop fusion | bytes 2359304 | tf_op jit(solution)/shard_map/dynamic_slice | solution.py:402
  21.9 1.6 %collective-permute-start.5 = (bf16[384,768]{1,0:T(8,128)(2,1)S(1)}, bf16[384,768]{1,0:T(8,128)(2,1)S(1)}, u32[]{:S(2)}, u32[]{:S(2)}) collective-permute-start(bf16[384,768]{1,0:T(8,128)(2,1)S(1)} %get-tuple-element.37), channel_id=1, source_target_pairs={{0,1},{1,2},{2,3},{3,0},{4,5},{5,6},{6,7},{7,4},{8,9},{9,10},{10,1... | collective-permute-start | bytes 1769480 | tf_op jit(solution)/shard_map/ppermute | solution.py:390
  23.5 1.5 %collective-permute-start.3 = (bf16[384,768]{1,0:T(8,128)(2,1)S(1)}, bf16[384,768]{1,0:T(8,128)(2,1)}, u32[]{:S(2)}, u32[]{:S(2)}) collective-permute-start(bf16[384,768]{1,0:T(8,128)(2,1)S(1)} %get-tuple-element.38), channel_id=1, source_target_pairs={{0,1},{1,2},{2,3},{3,0},{4,5},{5,6},{6,7},{7,4},{8,9},{9,10},{10,1... | collective-permute-start | bytes 1769480 | tf_op jit(solution)/shard_map/ppermute | solution.py:390
  25.0 1.7 %collective-permute-start.2 = (bf16[384,768]{1,0:T(8,128)(2,1)S(1)}, bf16[384,768]{1,0:T(8,128)(2,1)}, u32[]{:S(2)}, u32[]{:S(2)}) collective-permute-start(bf16[384,768]{1,0:T(8,128)(2,1)S(1)} %get-tuple-element.37), channel_id=1, source_target_pairs={{0,3},{1,0},{2,1},{3,2},{4,7},{5,4},{6,5},{7,6},{8,11},{9,8},{10,9... | collective-permute-start | bytes 1769480 | tf_op jit(solution)/shard_map/ppermute | solution.py:390
  26.7 0.5 collective-permute-start.1
  27.3 12.1 %collective-permute-done.5.refs_1_ = bf16[384,768]{1,0:T(8,128)(2,1)S(1)} collective-permute-done((bf16[384,768]{1,0:T(8,128)(2,1)S(1)}, bf16[384,768]{1,0:T(8,128)(2,1)S(1)}, u32[]{:S(2)}, u32[]{:S(2)}) %collective-permute-start.5) | collective-permute-done | bytes 589856 | tf_op jit(solution)/shard_map/ppermute | solution.py:390
  39.3 12.3 %collective-permute-done.3.refs_0_ = bf16[384,768]{1,0:T(8,128)(2,1)} collective-permute-done((bf16[384,768]{1,0:T(8,128)(2,1)S(1)}, bf16[384,768]{1,0:T(8,128)(2,1)}, u32[]{:S(2)}, u32[]{:S(2)}) %collective-permute-start.3) | collective-permute-done | bytes 589856 | tf_op jit(solution)/shard_map/ppermute | solution.py:390
  51.7 0.0 collective-permute-start.4
  51.7 1.2 %collective-permute-done.1.refs_2_ = bf16[384,768]{1,0:T(8,128)(2,1)} collective-permute-done((bf16[384,768]{1,0:T(8,128)(2,1)S(1)}, bf16[384,768]{1,0:T(8,128)(2,1)}, u32[]{:S(2)}, u32[]{:S(2)}) %collective-permute-start.1) | collective-permute-done | bytes 589856 | tf_op jit(solution)/shard_map/ppermute | solution.py:390
  52.9 1.0 collective-permute-done.4.refs_6_
  53.9 0.8 copy-done.4
  54.7 0.1 collective-permute-start.8
  54.8 0.4 collective-permute-start.9
  55.2 1.4 %collective-permute-start.20 = (bf16[384,768]{1,0:T(8,128)(2,1)}, bf16[384,768]{1,0:T(8,128)(2,1)}, u32[]{:S(2)}, u32[]{:S(2)}) collective-permute-start(bf16[384,768]{1,0:T(8,128)(2,1)} %collective-permute-done.3.refs_0_), channel_id=1, source_target_pairs={{0,1},{1,2},{2,3},{3,0},{4,5},{5,6},{6,7},{7,4},{8,9},{9,10},{10,1... | collective-permute-start | bytes 1769480 | tf_op jit(solution)/shard_map/ppermute | solution.py:390
  56.7 0.7 repeat_first.1
  57.4 6.8 %all-to-all-start.1 = ((bf16[8,48,256]{2,1,0:T(8,128)(2,1)}), bf16[8,48,256]{2,1,0:T(8,128)(2,1)S(1)}, u32[]{:S(2)}, u32[]{:S(2)}) async-start(bf16[8,48,256]{2,1,0:T(8,128)(2,1)} %repeat_first.1), calls=%async_computation.1 | async-start | bytes 393216 | tf_op jit(solution)/shard_map/all_to_all | solution.py:420
  64.2 2.2 %collective-permute-start.21 = (bf16[384,768]{1,0:T(8,128)(2,1)}, bf16[384,768]{1,0:T(8,128)(2,1)}, u32[]{:S(2)}, u32[]{:S(2)}) collective-permute-start(bf16[384,768]{1,0:T(8,128)(2,1)} %collective-permute-done.2.refs_3_), channel_id=1, source_target_pairs={{0,3},{1,0},{2,1},{3,2},{4,7},{5,4},{6,5},{7,6},{8,11},{9,8},{10,9... | collective-permute-start | bytes 1769480 | tf_op jit(solution)/shard_map/ppermute | solution.py:390
  66.4 0.3 collective-permute-start.7
  67.4 0.1 dynamic_slice.9
  67.4 0.1 concatenate.3.info
  67.5 0.6 collective-permute-done.7.text_other
  68.1 3.2 %temporal.1 = (bf16[32,48,128]{2,1,0:T(8,128)(2,1)}, bf16[3,2,256,128]{3,2,1,0:T(8,128)(2,1)}) custom-call(s32[7]{0:T(128)S(1)} %concatenate.3.info, bf16[32,56,384]{2,1,0:T(8,128)(2,1)S(1)} %all-to-all-done.rows_hbm.rows_ref, bf16[32,8,384]{2,1,0:T(8,128)(2,1)S(1)} %slice.3.text_own, bf16[32,8,384]{2,1,0:T(8,128)(2,1)S(1)} %collective-permute-done.7.text_other), custom_call_target="tpu_custom_call" | custom-call | flops 400000000 | bytes 3000000 | tf_op jit(solution)/shard_map/temporal/pallas_call | solution.py:186
  71.3 1.9 %all-to-all-done.1.refs_0_ = bf16[8,48,256]{2,1,0:T(8,128)(2,1)S(1)} async-done(((bf16[8,48,256]{2,1,0:T(8,128)(2,1)}), bf16[8,48,256]{2,1,0:T(8,128)(2,1)S(1)}, u32[]{:S(2)}, u32[]{:S(2)}) %all-to-all-start.1) | async-done | bytes 196640 | tf_op jit(solution)/shard_map/all_to_all | solution.py:420
  73.2 2.7 %collective-permute-start.12 = (bf16[8,48,256]{2,1,0:T(8,128)(2,1)S(1)}, bf16[8,48,256]{2,1,0:T(8,128)(2,1)S(1)}, u32[]{:S(2)}, u32[]{:S(2)}) collective-permute-start(bf16[8,48,256]{2,1,0:T(8,128)(2,1)S(1)} %all-to-all-done.1.refs_0_), channel_id=1, source_target_pairs={{0,24},{8,0},{16,8},{24,16},{1,25},{9,1},{17,9},{25,17},{2,26},{10... | collective-permute-start | bytes 589832 | tf_op jit(solution)/shard_map/ppermute | solution.py:390
  75.9 0.9 collective-permute-start.11
  76.7 0.9 collective-permute-start.10
  77.6 7.4 %all-to-all-start.2 = ((bf16[32,48,128]{2,1,0:T(8,128)(2,1)}), bf16[32,48,128]{2,1,0:T(8,128)(2,1)S(1)}, u32[]{:S(2)}, u32[]{:S(2)}) async-start(bf16[32,48,128]{2,1,0:T(8,128)(2,1)} %get-tuple-element.28), calls=%async_computation.2 | async-start | bytes 786432 | tf_op jit(solution)/shard_map/all_to_all | solution.py:426
  85.0 0.1 collective-permute-start.13
  85.1 0.5 collective-permute-start.16
  85.6 0.1 collective-permute-start.15
  85.7 0.7 collective-permute-done.10.refs_1_
  86.4 0.5 collective-permute-start.22
  86.9 0.1 collective-permute-start.23
  87.0 0.0 collective-permute-done.15.refs_6_
  87.1 1.0 collective-permute-done.14.refs_5_
  88.1 7.7 %spatial.1.spatial_ref = bf16[512,384]{1,0:T(8,128)(2,1)} custom-call(s32[7]{0:T(128)S(1)} %concatenate.3.info, bf16[32,56,384]{2,1,0:T(8,128)(2,1)S(1)} %copy-done.1, bf16[32,56,384]{2,1,0:T(8,128)(2,1)} %collective-permute-done.partner, bf16[8,48,256]{2,1,0:T(8,128)(2,1)S(1)} %all-to-all-done.1.refs_0_, ...), custom_call_target="tpu_custom_call" | custom-call | flops 4000000000 | bytes 1000000 | tf_op jit(solution)/shard_map/spatial/pallas_call | solution.py:252
  95.8 3.3 %all-to-all-done.2.back = bf16[32,48,128]{2,1,0:T(8,128)(2,1)S(1)} async-done(((bf16[32,48,128]{2,1,0:T(8,128)(2,1)}), bf16[32,48,128]{2,1,0:T(8,128)(2,1)S(1)}, u32[]{:S(2)}, u32[]{:S(2)}) %all-to-all-start.2) | async-done | bytes 393248 | tf_op jit(solution)/shard_map/all_to_all | solution.py:426
  99.1 1.2 %merge.1 = (bf16[128,384]{1,0:T(8,128)(2,1)S(1)}, bf16[128,384]{1,0:T(8,128)(2,1)S(1)}, bf16[128,384]{1,0:T(8,128)(2,1)S(1)}, bf16[128,384]{1,0:T(8,128)(2,1)S(1)}) custom-call(s32[7]{0:T(128)S(1)} %concatenate.3.info, bf16[512,384]{1,0:T(8,128)(2,1)} %spatial.1.spatial_ref, bf16[32,48,128]{2,1,0:T(8,128)(2,1)S(1)} %all-to-all-done.2.back), custom_call_target="tpu_custom_call" | custom-call | tf_op jit(solution)/shard_map/merge/pallas_call | solution.py:287
  100.3 2.7 %collective-permute-start.17 = (bf16[128,384]{1,0:T(8,128)(2,1)S(1)}, bf16[128,384]{1,0:T(8,128)(2,1)S(1)}, u32[]{:S(2)}, u32[]{:S(2)}) collective-permute-start(bf16[128,384]{1,0:T(8,128)(2,1)S(1)} %get-tuple-element.30), channel_id=1, source_target_pairs={{0,1},{1,2},{2,3},{3,0},{4,5},{5,6},{6,7},{7,4},{8,9},{9,10},{10,1... | collective-permute-start | bytes 294920 | tf_op jit(solution)/shard_map/ppermute | solution.py:390
  103.0 0.6 collective-permute-start.18
  103.7 1.5 %collective-permute-start.19 = (bf16[128,384]{1,0:T(8,128)(2,1)S(1)}, bf16[128,384]{1,0:T(8,128)(2,1)S(1)}, u32[]{:S(2)}, u32[]{:S(2)}) collective-permute-start(bf16[128,384]{1,0:T(8,128)(2,1)S(1)} %get-tuple-element.32), channel_id=1, source_target_pairs={{0,2},{1,3},{2,0},{3,1},{4,6},{5,7},{6,4},{7,5},{8,10},{9,11},{10,... | collective-permute-start | bytes 294920 | tf_op jit(solution)/shard_map/ppermute | solution.py:390
  105.2 3.1 %hold.1.held = bf16[4,3,384,768]{3,2,1,0:T(8,128)(2,1)S(1)} custom-call(bf16[384,768]{1,0:T(8,128)(2,1)} %collective-permute-done.3.refs_0_, bf16[384,768]{1,0:T(8,128)(2,1)} %copy-done.2, bf16[384,768]{1,0:T(8,128)(2,1)} %collective-permute-done.1.refs_2_, bf16[384,768]{1,0:T(8,128)(2,1)} %collective-permute-done.2.refs_3_, ...), custom_call_target="tpu_custom_call" | custom-call | flops 1000000 | bytes 7000000 | tf_op jit(solution)/shard_map/hold/pallas_call | solution.py:317
  108.3 1.4 %collective-permute-done.19.r3 = bf16[128,384]{1,0:T(8,128)(2,1)S(1)} collective-permute-done((bf16[128,384]{1,0:T(8,128)(2,1)S(1)}, bf16[128,384]{1,0:T(8,128)(2,1)S(1)}, u32[]{:S(2)}, u32[]{:S(2)}) %collective-permute-start.19) | collective-permute-done | bytes 98336 | tf_op jit(solution)/shard_map/ppermute | solution.py:390
  109.8 3.2 %out_project.1 = bf16[128,3072]{1,0:T(8,128)(2,1)} custom-call(s32[7]{0:T(128)S(1)} %concatenate.3.info, bf16[128,384]{1,0:T(8,128)(2,1)S(1)} %get-tuple-element.29.r0, bf16[128,384]{1,0:T(8,128)(2,1)S(1)} %collective-permute-done.17.r1, bf16[128,384]{1,0:T(8,128)(2,1)S(1)} %collective-permute-done.18.r2, bf16[128,384]{1,0:T(8,128)(2,1)S(1)} %collective-permute-done.19.r3, ...), custom_call_target="tpu_custom_call" | custom-call | flops 1207959552 | bytes 10500000 | tf_op jit(solution)/shard_map/out_project/pallas_call | solution.py:347
  (29 shorter events, 0.1 us)
Async XLA Ops:
  8.9 11.5 %copy-start.1 = (bf16[32,56,384]{2,1,0:T(8,128)(2,1)S(1)}, bf16[32,56,384]{2,1,0:T(8,128)(2,1)}, u32[]{:S(2)}) copy-start(bf16[32,56,384]{2,1,0:T(8,128)(2,1)} %project.1.own) | copy-start | bytes 4128772
  8.9 45.8 %all-to-all-start = ((bf16[32,56,384]{2,1,0:T(8,128)(2,1)}), bf16[32,56,384]{2,1,0:T(8,128)(2,1)S(1)}, u32[]{:S(2)}, u32[]{:S(2)}) async-start(bf16[32,56,384]{2,1,0:T(8,128)(2,1)} %project.1.own), calls=%async_computation | async-start | bytes 2752512 | tf_op jit(solution)/shard_map/all_to_all | solution.py:407
  20.5 34.2 %collective-permute-start = (bf16[32,56,384]{2,1,0:T(8,128)(2,1)S(1)}, bf16[32,56,384]{2,1,0:T(8,128)(2,1)}, u32[]{:S(2)}, u32[]{:S(2)}) collective-permute-start(bf16[32,56,384]{2,1,0:T(8,128)(2,1)S(1)} %copy-done.1), channel_id=1, source_target_pairs={{0,4},{4,0},{1,5},{5,1},{2,6},{6,2},{3,7},{7,3},{8,12},{12,8},{9,1... | collective-permute-start | bytes 4128776 | tf_op jit(solution)/shard_map/ppermute | solution.py:386
  20.6 46.8 %copy-start.5 = (s32[12]{0:T(128)S(1)}, s32[12]{0:T(128)}, u32[]{:S(2)}) copy-start(s32[12]{0:T(128)} %param.10) | copy-start | bytes 148
  21.9 17.4 %collective-permute-start.5 = (bf16[384,768]{1,0:T(8,128)(2,1)S(1)}, bf16[384,768]{1,0:T(8,128)(2,1)S(1)}, u32[]{:S(2)}, u32[]{:S(2)}) collective-permute-start(bf16[384,768]{1,0:T(8,128)(2,1)S(1)} %get-tuple-element.37), channel_id=1, source_target_pairs={{0,1},{1,2},{2,3},{3,0},{4,5},{5,6},{6,7},{7,4},{8,9},{9,10},{10,1... | collective-permute-start | bytes 1769480 | tf_op jit(solution)/shard_map/ppermute | solution.py:390
  23.5 28.2 %collective-permute-start.3 = (bf16[384,768]{1,0:T(8,128)(2,1)S(1)}, bf16[384,768]{1,0:T(8,128)(2,1)}, u32[]{:S(2)}, u32[]{:S(2)}) collective-permute-start(bf16[384,768]{1,0:T(8,128)(2,1)S(1)} %get-tuple-element.38), channel_id=1, source_target_pairs={{0,1},{1,2},{2,3},{3,0},{4,5},{5,6},{6,7},{7,4},{8,9},{9,10},{10,1... | collective-permute-start | bytes 1769480 | tf_op jit(solution)/shard_map/ppermute | solution.py:390
  25.0 26.7 %collective-permute-start.2 = (bf16[384,768]{1,0:T(8,128)(2,1)S(1)}, bf16[384,768]{1,0:T(8,128)(2,1)}, u32[]{:S(2)}, u32[]{:S(2)}) collective-permute-start(bf16[384,768]{1,0:T(8,128)(2,1)S(1)} %get-tuple-element.37), channel_id=1, source_target_pairs={{0,3},{1,0},{2,1},{3,2},{4,7},{5,4},{6,5},{7,6},{8,11},{9,8},{10,9... | collective-permute-start | bytes 1769480 | tf_op jit(solution)/shard_map/ppermute | solution.py:390
  26.7 26.2 %collective-permute-start.1 = (bf16[384,768]{1,0:T(8,128)(2,1)S(1)}, bf16[384,768]{1,0:T(8,128)(2,1)}, u32[]{:S(2)}, u32[]{:S(2)}) collective-permute-start(bf16[384,768]{1,0:T(8,128)(2,1)S(1)} %get-tuple-element.38), channel_id=1, source_target_pairs={{0,3},{1,0},{2,1},{3,2},{4,7},{5,4},{6,5},{7,6},{8,11},{9,8},{10,9... | collective-permute-start | bytes 1769480 | tf_op jit(solution)/shard_map/ppermute | solution.py:390
  39.3 14.6 %copy-start.2 = (bf16[384,768]{1,0:T(8,128)(2,1)}, bf16[384,768]{1,0:T(8,128)(2,1)S(1)}, u32[]{:S(2)}) copy-start(bf16[384,768]{1,0:T(8,128)(2,1)S(1)} %collective-permute-done.5.refs_1_) | copy-start | bytes 1769476
  39.3 13.6 %collective-permute-start.6 = (bf16[384,768]{1,0:T(8,128)(2,1)S(1)}, bf16[384,768]{1,0:T(8,128)(2,1)S(1)}, u32[]{:S(2)}, u32[]{:S(2)}) collective-permute-start(bf16[384,768]{1,0:T(8,128)(2,1)S(1)} %collective-permute-done.5.refs_1_), channel_id=1, source_target_pairs={{0,4},{4,0},{1,5},{5,1},{2,6},{6,2},{3,7},{7,3},{8,12},{12,8},{9,1... | collective-permute-start | bytes 1769480 | tf_op jit(solution)/shard_map/ppermute | solution.py:386
  51.7 2.2 %collective-permute-start.4 = (bf16[384,768]{1,0:T(8,128)(2,1)}, bf16[384,768]{1,0:T(8,128)(2,1)S(1)}, u32[]{:S(2)}, u32[]{:S(2)}) collective-permute-start(bf16[384,768]{1,0:T(8,128)(2,1)} %collective-permute-done.3.refs_0_), channel_id=1, source_target_pairs={{0,4},{4,0},{1,5},{5,1},{2,6},{6,2},{3,7},{7,3},{8,12},{12,8},{9,1... | collective-permute-start | bytes 1769480 | tf_op jit(solution)/shard_map/ppermute | solution.py:386
  52.9 1.0 copy-start.3
  53.9 0.8 copy-start.4
  54.7 18.5 %collective-permute-start.8 = (bf16[384,768]{1,0:T(8,128)(2,1)}, bf16[384,768]{1,0:T(8,128)(2,1)}, u32[]{:S(2)}, u32[]{:S(2)}) collective-permute-start(bf16[384,768]{1,0:T(8,128)(2,1)} %collective-permute-done.1.refs_2_), channel_id=1, source_target_pairs={{0,4},{4,0},{1,5},{5,1},{2,6},{6,2},{3,7},{7,3},{8,12},{12,8},{9,1... | collective-permute-start | bytes 1769480 | tf_op jit(solution)/shard_map/ppermute | solution.py:386
  54.8 18.3 %collective-permute-start.9 = (bf16[384,768]{1,0:T(8,128)(2,1)}, bf16[384,768]{1,0:T(8,128)(2,1)}, u32[]{:S(2)}, u32[]{:S(2)}) collective-permute-start(bf16[384,768]{1,0:T(8,128)(2,1)} %collective-permute-done.2.refs_3_), channel_id=1, source_target_pairs={{0,4},{4,0},{1,5},{5,1},{2,6},{6,2},{3,7},{7,3},{8,12},{12,8},{9,1... | collective-permute-start | bytes 1769480 | tf_op jit(solution)/shard_map/ppermute | solution.py:386
  55.2 29.7 %collective-permute-start.20 = (bf16[384,768]{1,0:T(8,128)(2,1)}, bf16[384,768]{1,0:T(8,128)(2,1)}, u32[]{:S(2)}, u32[]{:S(2)}) collective-permute-start(bf16[384,768]{1,0:T(8,128)(2,1)} %collective-permute-done.3.refs_0_), channel_id=1, source_target_pairs={{0,1},{1,2},{2,3},{3,0},{4,5},{5,6},{6,7},{7,4},{8,9},{9,10},{10,1... | collective-permute-start | bytes 1769480 | tf_op jit(solution)/shard_map/ppermute | solution.py:390
  57.4 15.8 %all-to-all-start.1 = ((bf16[8,48,256]{2,1,0:T(8,128)(2,1)}), bf16[8,48,256]{2,1,0:T(8,128)(2,1)S(1)}, u32[]{:S(2)}, u32[]{:S(2)}) async-start(bf16[8,48,256]{2,1,0:T(8,128)(2,1)} %repeat_first.1), calls=%async_computation.1 | async-start | bytes 393216 | tf_op jit(solution)/shard_map/all_to_all | solution.py:420
  64.2 22.3 %collective-permute-start.21 = (bf16[384,768]{1,0:T(8,128)(2,1)}, bf16[384,768]{1,0:T(8,128)(2,1)}, u32[]{:S(2)}, u32[]{:S(2)}) collective-permute-start(bf16[384,768]{1,0:T(8,128)(2,1)} %collective-permute-done.2.refs_3_), channel_id=1, source_target_pairs={{0,3},{1,0},{2,1},{3,2},{4,7},{5,4},{6,5},{7,6},{8,11},{9,8},{10,9... | collective-permute-start | bytes 1769480 | tf_op jit(solution)/shard_map/ppermute | solution.py:390
  66.4 1.7 %collective-permute-start.7 = (bf16[32,8,384]{2,1,0:T(8,128)(2,1)S(1)}, bf16[32,8,384]{2,1,0:T(8,128)(2,1)S(1)}, u32[]{:S(2)}, u32[]{:S(2)}) collective-permute-start(bf16[32,8,384]{2,1,0:T(8,128)(2,1)S(1)} %slice.3.text_own), channel_id=1, source_target_pairs={{0,4},{4,0},{1,5},{5,1},{2,6},{6,2},{3,7},{7,3},{8,12},{12,8},{9,1... | collective-permute-start | bytes 589832 | tf_op jit(solution)/shard_map/ppermute | solution.py:386
  73.2 11.9 %collective-permute-start.12 = (bf16[8,48,256]{2,1,0:T(8,128)(2,1)S(1)}, bf16[8,48,256]{2,1,0:T(8,128)(2,1)S(1)}, u32[]{:S(2)}, u32[]{:S(2)}) collective-permute-start(bf16[8,48,256]{2,1,0:T(8,128)(2,1)S(1)} %all-to-all-done.1.refs_0_), channel_id=1, source_target_pairs={{0,24},{8,0},{16,8},{24,16},{1,25},{9,1},{17,9},{25,17},{2,26},{10... | collective-permute-start | bytes 589832 | tf_op jit(solution)/shard_map/ppermute | solution.py:390
  75.9 9.7 %collective-permute-start.11 = (bf16[8,48,256]{2,1,0:T(8,128)(2,1)S(1)}, bf16[8,48,256]{2,1,0:T(8,128)(2,1)S(1)}, u32[]{:S(2)}, u32[]{:S(2)}) collective-permute-start(bf16[8,48,256]{2,1,0:T(8,128)(2,1)S(1)} %all-to-all-done.1.refs_0_), channel_id=1, source_target_pairs={{0,16},{8,24},{16,0},{24,8},{1,17},{9,25},{17,1},{25,9},{2,18},{10... | collective-permute-start | bytes 589832 | tf_op jit(solution)/shard_map/ppermute | solution.py:390
  76.7 9.7 %collective-permute-start.10 = (bf16[8,48,256]{2,1,0:T(8,128)(2,1)S(1)}, bf16[8,48,256]{2,1,0:T(8,128)(2,1)S(1)}, u32[]{:S(2)}, u32[]{:S(2)}) collective-permute-start(bf16[8,48,256]{2,1,0:T(8,128)(2,1)S(1)} %all-to-all-done.1.refs_0_), channel_id=1, source_target_pairs={{0,8},{8,16},{16,24},{24,0},{1,9},{9,17},{17,25},{25,1},{2,10},{10... | collective-permute-start | bytes 589832 | tf_op jit(solution)/shard_map/ppermute | solution.py:390
  77.6 21.6 %all-to-all-start.2 = ((bf16[32,48,128]{2,1,0:T(8,128)(2,1)}), bf16[32,48,128]{2,1,0:T(8,128)(2,1)S(1)}, u32[]{:S(2)}, u32[]{:S(2)}) async-start(bf16[32,48,128]{2,1,0:T(8,128)(2,1)} %get-tuple-element.28), calls=%async_computation.2 | async-start | bytes 786432 | tf_op jit(solution)/shard_map/all_to_all | solution.py:426
  85.0 2.0 %collective-permute-start.13 = (bf16[8,48,256]{2,1,0:T(8,128)(2,1)S(1)}, bf16[8,48,256]{2,1,0:T(8,128)(2,1)S(1)}, u32[]{:S(2)}, u32[]{:S(2)}) collective-permute-start(bf16[8,48,256]{2,1,0:T(8,128)(2,1)S(1)} %all-to-all-done.1.refs_0_), channel_id=1, source_target_pairs={{0,4},{4,0},{1,5},{5,1},{2,6},{6,2},{3,7},{7,3},{8,12},{12,8},{9,1... | collective-permute-start | bytes 589832 | tf_op jit(solution)/shard_map/ppermute | solution.py:386
  85.1 2.0 %collective-permute-start.16 = (bf16[8,48,256]{2,1,0:T(8,128)(2,1)S(1)}, bf16[8,48,256]{2,1,0:T(8,128)(2,1)S(1)}, u32[]{:S(2)}, u32[]{:S(2)}) collective-permute-start(bf16[8,48,256]{2,1,0:T(8,128)(2,1)S(1)} %collective-permute-done.12.refs_3_), channel_id=1, source_target_pairs={{0,4},{4,0},{1,5},{5,1},{2,6},{6,2},{3,7},{7,3},{8,12},{12,8},{9,1... | collective-permute-start | bytes 589832 | tf_op jit(solution)/shard_map/ppermute | solution.py:386
  85.6 1.5 %collective-permute-start.15 = (bf16[8,48,256]{2,1,0:T(8,128)(2,1)S(1)}, bf16[8,48,256]{2,1,0:T(8,128)(2,1)S(1)}, u32[]{:S(2)}, u32[]{:S(2)}) collective-permute-start(bf16[8,48,256]{2,1,0:T(8,128)(2,1)S(1)} %collective-permute-done.11.refs_2_), channel_id=1, source_target_pairs={{0,4},{4,0},{1,5},{5,1},{2,6},{6,2},{3,7},{7,3},{8,12},{12,8},{9,1... | collective-permute-start | bytes 589832 | tf_op jit(solution)/shard_map/ppermute | solution.py:386
  86.4 1.6 %collective-permute-start.14 = (bf16[8,48,256]{2,1,0:T(8,128)(2,1)S(1)}, bf16[8,48,256]{2,1,0:T(8,128)(2,1)S(1)}, u32[]{:S(2)}, u32[]{:S(2)}) collective-permute-start(bf16[8,48,256]{2,1,0:T(8,128)(2,1)S(1)} %collective-permute-done.10.refs_1_), channel_id=1, source_target_pairs={{0,4},{4,0},{1,5},{5,1},{2,6},{6,2},{3,7},{7,3},{8,12},{12,8},{9,1... | collective-permute-start | bytes 589832 | tf_op jit(solution)/shard_map/ppermute | solution.py:386
  86.4 18.8 %collective-permute-start.22 = (bf16[384,768]{1,0:T(8,128)(2,1)}, bf16[384,768]{1,0:T(8,128)(2,1)}, u32[]{:S(2)}, u32[]{:S(2)}) collective-permute-start(bf16[384,768]{1,0:T(8,128)(2,1)} %collective-permute-done.20.refs_4_), channel_id=1, source_target_pairs={{0,4},{4,0},{1,5},{5,1},{2,6},{6,2},{3,7},{7,3},{8,12},{12,8},{9,1... | collective-permute-start | bytes 1769480 | tf_op jit(solution)/shard_map/ppermute | solution.py:386
  86.9 18.2 %collective-permute-start.23 = (bf16[384,768]{1,0:T(8,128)(2,1)}, bf16[384,768]{1,0:T(8,128)(2,1)}, u32[]{:S(2)}, u32[]{:S(2)}) collective-permute-start(bf16[384,768]{1,0:T(8,128)(2,1)} %collective-permute-done.21.refs_5_), channel_id=1, source_target_pairs={{0,4},{4,0},{1,5},{5,1},{2,6},{6,2},{3,7},{7,3},{8,12},{12,8},{9,1... | collective-permute-start | bytes 1769480 | tf_op jit(solution)/shard_map/ppermute | solution.py:386
  100.3 8.0 %collective-permute-start.17 = (bf16[128,384]{1,0:T(8,128)(2,1)S(1)}, bf16[128,384]{1,0:T(8,128)(2,1)S(1)}, u32[]{:S(2)}, u32[]{:S(2)}) collective-permute-start(bf16[128,384]{1,0:T(8,128)(2,1)S(1)} %get-tuple-element.30), channel_id=1, source_target_pairs={{0,1},{1,2},{2,3},{3,0},{4,5},{5,6},{6,7},{7,4},{8,9},{9,10},{10,1... | collective-permute-start | bytes 294920 | tf_op jit(solution)/shard_map/ppermute | solution.py:390
  103.0 5.3 %collective-permute-start.18 = (bf16[128,384]{1,0:T(8,128)(2,1)S(1)}, bf16[128,384]{1,0:T(8,128)(2,1)S(1)}, u32[]{:S(2)}, u32[]{:S(2)}) collective-permute-start(bf16[128,384]{1,0:T(8,128)(2,1)S(1)} %get-tuple-element.31), channel_id=1, source_target_pairs={{0,3},{1,0},{2,1},{3,2},{4,7},{5,4},{6,5},{7,6},{8,11},{9,8},{10,9... | collective-permute-start | bytes 294920 | tf_op jit(solution)/shard_map/ppermute | solution.py:390
  103.7 6.1 %copy-start = (bf16[3,128,3072]{2,1,0:T(8,128)(2,1)S(1)}, bf16[3,128,3072]{2,1,0:T(8,128)(2,1)}, u32[]{:S(2)}) copy-start(bf16[3,128,3072]{2,1,0:T(8,128)(2,1)} %param.9) | copy-start | bytes 7077892
  103.7 6.1 %collective-permute-start.19 = (bf16[128,384]{1,0:T(8,128)(2,1)S(1)}, bf16[128,384]{1,0:T(8,128)(2,1)S(1)}, u32[]{:S(2)}, u32[]{:S(2)}) collective-permute-start(bf16[128,384]{1,0:T(8,128)(2,1)S(1)} %get-tuple-element.32), channel_id=1, source_target_pairs={{0,2},{1,3},{2,0},{3,1},{4,6},{5,7},{6,4},{7,5},{8,10},{9,11},{10,... | collective-permute-start | bytes 294920 | tf_op jit(solution)/shard_map/ppermute | solution.py:390

commit v5 on v4

--- a/solution.py
+++ b/solution.py
@@ -133,7 +133,7 @@
     return jnp.where(slots < length, scores, MASKED)
 
 
-def temporal_kernel(info, rows_ref, text_own, text_other, out_ref, text_ref, spread):
+def temporal_kernel(info, rows_ref, text_own, text_other, out_ref, text_ref, spread, apart):
     core, length = info[3], info[4]
 
     for side, source in enumerate((text_own, text_other)):
@@ -146,8 +146,11 @@
                     first = side * TEXT_CORE + t * CHIPS
                     text_ref[h, kind, first : first + CHIPS, :] = spread[rows, :].astype(bf16)
 
-    step = 128
+    step = apart.shape[0]
     count = step // PIECE
+    own = lax.broadcasted_iota(jnp.int32, apart.shape, 0) & (PIECE - 1)
+    other = lax.broadcasted_iota(jnp.int32, apart.shape, 1) & (PIECE - 1)
+    apart[...] = jnp.where(own == other, 0.0, MASKED)
     for h in range(HEADS_HERE):
         part = slice(h * PIECE, (h + 1) * PIECE)
 
@@ -158,10 +161,7 @@
             for index in range(ROWS // step):
                 chips = slice(index * count, (index + 1) * count)
                 query = rows_ref[chips, part, :HEAD].reshape(step, HEAD)
-                scores = nt(query, keys)
-                own = lax.broadcasted_iota(jnp.int32, scores.shape, 0) & (PIECE - 1)
-                other = lax.broadcasted_iota(jnp.int32, scores.shape, 1) & (PIECE - 1)
-                scores = jnp.where(own == other, scores, MASKED)
+                scores = nt(query, keys) + apart[...]
                 text = mask_text(nt(query, text_ref[h, 0]), core, length)
                 top = FACTOR * jnp.maximum(
                     jnp.max(scores, axis=1, keepdims=True), jnp.max(text, axis=1, keepdims=True)
@@ -191,7 +191,10 @@
             pltpu.HBM((CHIPS, TOKEN_PART, HEAD), bf16),
             pltpu.HBM((HEADS_HERE, 2, CORES * TEXT_CORE, HEAD), bf16),
         ],
-        scratch_shapes=[pltpu.VMEM(((CHIPS + 1) * 2 * TEXT_HERE, HEAD), f32)],
+        scratch_shapes=[
+            pltpu.VMEM(((CHIPS + 1) * 2 * TEXT_HERE, HEAD), f32),
+            pltpu.VMEM((256, ROWS), f32),
+        ],
         compiler_params=params(14),
         cost_estimate=pl.CostEstimate(
             flops=400_000_000, bytes_accessed=3_000_000, transcendentals=1_200_000

time: 115 us -> 114 us (level)
  starting transfers between devices: 46.1 us -> 44.9 us
  Pallas kernels: 28.1 us -> 29.3 us
    all_to_all x1, waiting for transfers between devices: 3.31 us -> 0.01 us  [local(): back = lax.all_to_all(over_time, ('z', 'y'), 0, 0, tiled=True)]
    pallas_call x1, Pallas kernels: 7.74 us -> 10.4 us  [spatial(): pl.pallas_call(spatial_kernel, in_specs=specs(2 + 2 * Y) + [pl.BlockSpec(...]
    all_to_all x1, starting transfers between devices: 7.38 us -> 6.01 us  [local(): back = lax.all_to_all(over_time, ('z', 'y'), 0, 0, tiled=True)]
    pallas_call x1, Pallas kernels: 3.15 us -> 1.79 us  [temporal(): pl.pallas_call(temporal_kernel, in_specs=specs(3), out_specs=[pl.BlockSpe...]
    all_to_all x1, waiting for transfers between devices: 1.88 us -> 3.25 us  [local(): column = lax.all_to_all(repeat_first(moved), 'z', 0, 0, tiled=True)]
  transfers between devices with their start and end apart: 27 -> 27, of which waited for: 10 -> 9; matrix products, arithmetic and copies ran while one was open for 1% -> 1% of each run, Pallas kernels for 14% -> 15%
where the time goes in v5:
time: 114 us; the launch traced here: 112 us
  starting transfers between devices  44.9 us (39%)
  waiting for transfers between devices  34.7 us (30%)
  Pallas kernels  29.3 us (26%)
  local copies, waits for them, and re-layouts  2.34 us (2%)
    ppermute x12, waiting for transfers between devices, shifted(): lax.ppermute(value, axis, [(i, (i + k) % count) for i in range(count)])  28.8 us
    ppermute x12, starting transfers between devices, shifted(): lax.ppermute(value, axis, [(i, (i + k) % count) for i in range(count)])  18.4 us
    all_to_all x1, starting transfers between devices, local(): moved = lax.all_to_all(packed, ('z', 'y'), 0, 0, tiled=True)  11.5 us
    pallas_call x1, Pallas kernels, spatial(): pl.pallas_call(spatial_kernel, in_specs=specs(2 + 2 * Y) + [pl.BlockSpec(...  10.4 us
    pallas_call x1, Pallas kernels, project(): pl.pallas_call(project_kernel, in_specs=[hbm, vmem, hbm], out_specs=vmem,...  8.93 us
    all_to_all x1, starting transfers between devices, local(): column = lax.all_to_all(repeat_first(moved), 'z', 0, 0, tiled=True)  6.8 us
    all_to_all x1, starting transfers between devices, local(): back = lax.all_to_all(over_time, ('z', 'y'), 0, 0, tiled=True)  6.01 us
    all_to_all x1, waiting for transfers between devices, local(): column = lax.all_to_all(repeat_first(moved), 'z', 0, 0, tiled=True)  3.25 us
  transfers between devices with their start and end apart: 27, of which 9 were waited for; matrix products, arithmetic and copies ran while one was open for 1% of the time, Pallas kernels for 15%

profile of v5, /device:TPU:32, one launch (start us, length us, event | category | flops | bytes accessed | tf_op | source)
XLA Modules:
  0.0 112.0 jit_solution(11397181273050561159)
XLA Ops:
  0.0 8.9 %project.1.own = bf16[32,56,384]{2,1,0:T(8,128)(2,1)} custom-call(bf16[512,3072]{1,0:T(8,128)(2,1)} %x_hbm.1, bf16[4,3072]{1,0:T(4,128)(2,1)} %text_ref.1, bf16[3,3072,384]{2,1,0:T(8,128)(2,1)} %bitcast.7), custom_call_target="tpu_custom_call" | custom-call | flops 3623878656 | bytes 12000000 | tf_op jit(solution)/shard_map/project/pallas_call | solution.py:95
  8.9 11.5 %all-to-all-start = ((bf16[32,56,384]{2,1,0:T(8,128)(2,1)}), bf16[32,56,384]{2,1,0:T(8,128)(2,1)S(1)}, u32[]{:S(2)}, u32[]{:S(2)}) async-start(bf16[32,56,384]{2,1,0:T(8,128)(2,1)} %project.1.own), calls=%async_computation | async-start | bytes 2752512 | tf_op jit(solution)/shard_map/all_to_all | solution.py:410
  20.5 0.1 collective-permute-start
  20.6 0.0 copy-start.5
  20.6 1.3 %constant_dynamic-slice_fusion = (bf16[384,768]{1,0:T(8,128)(2,1)S(1)}, bf16[384,768]{1,0:T(8,128)(2,1)S(1)}) fusion(bf16[384,3072]{1,0:T(8,128)(2,1)} %bitcast.5, s32[]{:T(128)S(6)} %select_n.11, s32[]{:T(128)S(6)} %select_n.10), kind=kLoop, calls=%fused_computation | loop fusion | bytes 2359304 | tf_op jit(solution)/shard_map/dynamic_slice | solution.py:405
  21.9 1.6 %collective-permute-start.5 = (bf16[384,768]{1,0:T(8,128)(2,1)S(1)}, bf16[384,768]{1,0:T(8,128)(2,1)S(1)}, u32[]{:S(2)}, u32[]{:S(2)}) collective-permute-start(bf16[384,768]{1,0:T(8,128)(2,1)S(1)} %get-tuple-element.37), channel_id=1, source_target_pairs={{0,1},{1,2},{2,3},{3,0},{4,5},{5,6},{6,7},{7,4},{8,9},{9,10},{10,1... | collective-permute-start | bytes 1769480 | tf_op jit(solution)/shard_map/ppermute | solution.py:393
  23.5 1.5 %collective-permute-start.3 = (bf16[384,768]{1,0:T(8,128)(2,1)S(1)}, bf16[384,768]{1,0:T(8,128)(2,1)}, u32[]{:S(2)}, u32[]{:S(2)}) collective-permute-start(bf16[384,768]{1,0:T(8,128)(2,1)S(1)} %get-tuple-element.38), channel_id=1, source_target_pairs={{0,1},{1,2},{2,3},{3,0},{4,5},{5,6},{6,7},{7,4},{8,9},{9,10},{10,1... | collective-permute-start | bytes 1769480 | tf_op jit(solution)/shard_map/ppermute | solution.py:393
  25.0 1.7 %collective-permute-start.2 = (bf16[384,768]{1,0:T(8,128)(2,1)S(1)}, bf16[384,768]{1,0:T(8,128)(2,1)}, u32[]{:S(2)}, u32[]{:S(2)}) collective-permute-start(bf16[384,768]{1,0:T(8,128)(2,1)S(1)} %get-tuple-element.37), channel_id=1, source_target_pairs={{0,3},{1,0},{2,1},{3,2},{4,7},{5,4},{6,5},{7,6},{8,11},{9,8},{10,9... | collective-permute-start | bytes 1769480 | tf_op jit(solution)/shard_map/ppermute | solution.py:393
  26.7 0.5 collective-permute-start.1
  27.3 12.1 %collective-permute-done.5.refs_1_ = bf16[384,768]{1,0:T(8,128)(2,1)S(1)} collective-permute-done((bf16[384,768]{1,0:T(8,128)(2,1)S(1)}, bf16[384,768]{1,0:T(8,128)(2,1)S(1)}, u32[]{:S(2)}, u32[]{:S(2)}) %collective-permute-start.5) | collective-permute-done | bytes 589856 | tf_op jit(solution)/shard_map/ppermute | solution.py:393
  39.3 12.3 %collective-permute-done.3.refs_0_ = bf16[384,768]{1,0:T(8,128)(2,1)} collective-permute-done((bf16[384,768]{1,0:T(8,128)(2,1)S(1)}, bf16[384,768]{1,0:T(8,128)(2,1)}, u32[]{:S(2)}, u32[]{:S(2)}) %collective-permute-start.3) | collective-permute-done | bytes 589856 | tf_op jit(solution)/shard_map/ppermute | solution.py:393
  51.7 0.0 collective-permute-start.4
  51.7 0.0 collective-permute-done.2.refs_3_
  51.7 1.2 %collective-permute-done.1.refs_2_ = bf16[384,768]{1,0:T(8,128)(2,1)} collective-permute-done((bf16[384,768]{1,0:T(8,128)(2,1)S(1)}, bf16[384,768]{1,0:T(8,128)(2,1)}, u32[]{:S(2)}, u32[]{:S(2)}) %collective-permute-start.1) | collective-permute-done | bytes 589856 | tf_op jit(solution)/shard_map/ppermute | solution.py:393
  52.9 1.0 collective-permute-done.4.refs_6_
  53.9 0.8 copy-done.4
  54.7 0.0 all-to-all-done.rows_hbm.rows_ref
  54.7 0.1 collective-permute-start.8
  54.8 0.4 collective-permute-start.9
  55.2 1.4 %collective-permute-start.20 = (bf16[384,768]{1,0:T(8,128)(2,1)}, bf16[384,768]{1,0:T(8,128)(2,1)}, u32[]{:S(2)}, u32[]{:S(2)}) collective-permute-start(bf16[384,768]{1,0:T(8,128)(2,1)} %collective-permute-done.3.refs_0_), channel_id=1, source_target_pairs={{0,1},{1,2},{2,3},{3,0},{4,5},{5,6},{6,7},{7,4},{8,9},{9,10},{10,1... | collective-permute-start | bytes 1769480 | tf_op jit(solution)/shard_map/ppermute | solution.py:393
  56.7 0.7 repeat_first.1
  57.4 6.8 %all-to-all-start.1 = ((bf16[8,48,256]{2,1,0:T(8,128)(2,1)}), bf16[8,48,256]{2,1,0:T(8,128)(2,1)S(1)}, u32[]{:S(2)}, u32[]{:S(2)}) async-start(bf16[8,48,256]{2,1,0:T(8,128)(2,1)} %repeat_first.1), calls=%async_computation.1 | async-start | bytes 393216 | tf_op jit(solution)/shard_map/all_to_all | solution.py:423
  64.2 2.2 %collective-permute-start.21 = (bf16[384,768]{1,0:T(8,128)(2,1)}, bf16[384,768]{1,0:T(8,128)(2,1)}, u32[]{:S(2)}, u32[]{:S(2)}) collective-permute-start(bf16[384,768]{1,0:T(8,128)(2,1)} %collective-permute-done.2.refs_3_), channel_id=1, source_target_pairs={{0,3},{1,0},{2,1},{3,2},{4,7},{5,4},{6,5},{7,6},{8,11},{9,8},{10,9... | collective-permute-start | bytes 1769480 | tf_op jit(solution)/shard_map/ppermute | solution.py:393
  66.4 0.3 collective-permute-start.7
  67.4 0.1 dynamic_slice.9
  67.4 0.1 concatenate.3.info
  67.5 0.6 collective-permute-done.7.text_other
  68.1 1.8 %temporal.1 = (bf16[32,48,128]{2,1,0:T(8,128)(2,1)}, bf16[3,2,256,128]{3,2,1,0:T(8,128)(2,1)}) custom-call(s32[7]{0:T(128)S(1)} %concatenate.3.info, bf16[32,56,384]{2,1,0:T(8,128)(2,1)S(1)} %all-to-all-done.rows_hbm.rows_ref, bf16[32,8,384]{2,1,0:T(8,128)(2,1)S(1)} %slice.3.text_own, bf16[32,8,384]{2,1,0:T(8,128)(2,1)S(1)} %collective-permute-done.7.text_other), custom_call_target="tpu_custom_call" | custom-call | flops 400000000 | bytes 3000000 | tf_op jit(solution)/shard_map/temporal/pallas_call | solution.py:186
  69.9 3.2 %all-to-all-done.1.refs_0_ = bf16[8,48,256]{2,1,0:T(8,128)(2,1)S(1)} async-done(((bf16[8,48,256]{2,1,0:T(8,128)(2,1)}), bf16[8,48,256]{2,1,0:T(8,128)(2,1)S(1)}, u32[]{:S(2)}, u32[]{:S(2)}) %all-to-all-start.1) | async-done | bytes 196640 | tf_op jit(solution)/shard_map/all_to_all | solution.py:423
  73.2 2.7 %collective-permute-start.12 = (bf16[8,48,256]{2,1,0:T(8,128)(2,1)S(1)}, bf16[8,48,256]{2,1,0:T(8,128)(2,1)S(1)}, u32[]{:S(2)}, u32[]{:S(2)}) collective-permute-start(bf16[8,48,256]{2,1,0:T(8,128)(2,1)S(1)} %all-to-all-done.1.refs_0_), channel_id=1, source_target_pairs={{0,24},{8,0},{16,8},{24,16},{1,25},{9,1},{17,9},{25,17},{2,26},{10... | collective-permute-start | bytes 589832 | tf_op jit(solution)/shard_map/ppermute | solution.py:393
  75.9 0.9 collective-permute-start.11
  76.7 0.9 collective-permute-start.10
  77.6 6.0 %all-to-all-start.2 = ((bf16[32,48,128]{2,1,0:T(8,128)(2,1)}), bf16[32,48,128]{2,1,0:T(8,128)(2,1)S(1)}, u32[]{:S(2)}, u32[]{:S(2)}) async-start(bf16[32,48,128]{2,1,0:T(8,128)(2,1)} %get-tuple-element.28), calls=%async_computation.2 | async-start | bytes 786432 | tf_op jit(solution)/shard_map/all_to_all | solution.py:429
  83.6 0.1 collective-permute-start.13
  83.7 0.5 collective-permute-start.16
  84.2 0.1 collective-permute-start.15
  84.3 1.5 %collective-permute-done.10.refs_1_ = bf16[8,48,256]{2,1,0:T(8,128)(2,1)S(1)} collective-permute-done((bf16[8,48,256]{2,1,0:T(8,128)(2,1)S(1)}, bf16[8,48,256]{2,1,0:T(8,128)(2,1)S(1)}, u32[]{:S(2)}, u32[]{:S(2)}) %collective-permute-start.10) | collective-permute-done | bytes 196640 | tf_op jit(solution)/shard_map/ppermute | solution.py:393
  85.8 0.5 collective-permute-start.22
  86.4 0.1 collective-permute-start.23
  86.5 1.0 collective-permute-done.14.refs_5_
  87.5 10.4 %spatial.1.spatial_ref = bf16[512,384]{1,0:T(8,128)(2,1)} custom-call(s32[7]{0:T(128)S(1)} %concatenate.3.info, bf16[32,56,384]{2,1,0:T(8,128)(2,1)S(1)} %copy-done.1, bf16[32,56,384]{2,1,0:T(8,128)(2,1)} %collective-permute-done.partner, bf16[8,48,256]{2,1,0:T(8,128)(2,1)S(1)} %all-to-all-done.1.refs_0_, ...), custom_call_target="tpu_custom_call" | custom-call | flops 4000000000 | bytes 1000000 | tf_op jit(solution)/shard_map/spatial/pallas_call | solution.py:255
  97.9 1.2 %merge.1 = (bf16[128,384]{1,0:T(8,128)(2,1)S(1)}, bf16[128,384]{1,0:T(8,128)(2,1)S(1)}, bf16[128,384]{1,0:T(8,128)(2,1)S(1)}, bf16[128,384]{1,0:T(8,128)(2,1)S(1)}) custom-call(s32[7]{0:T(128)S(1)} %concatenate.3.info, bf16[512,384]{1,0:T(8,128)(2,1)} %spatial.1.spatial_ref, bf16[32,48,128]{2,1,0:T(8,128)(2,1)S(1)} %all-to-all-done.2.back), custom_call_target="tpu_custom_call" | custom-call | tf_op jit(solution)/shard_map/merge/pallas_call | solution.py:290
  99.1 1.2 %collective-permute-start.17 = (bf16[128,384]{1,0:T(8,128)(2,1)S(1)}, bf16[128,384]{1,0:T(8,128)(2,1)S(1)}, u32[]{:S(2)}, u32[]{:S(2)}) collective-permute-start(bf16[128,384]{1,0:T(8,128)(2,1)S(1)} %get-tuple-element.30), channel_id=1, source_target_pairs={{0,1},{1,2},{2,3},{3,0},{4,5},{5,6},{6,7},{7,4},{8,9},{9,10},{10,1... | collective-permute-start | bytes 294920 | tf_op jit(solution)/shard_map/ppermute | solution.py:393
  100.3 2.4 %collective-permute-start.18 = (bf16[128,384]{1,0:T(8,128)(2,1)S(1)}, bf16[128,384]{1,0:T(8,128)(2,1)S(1)}, u32[]{:S(2)}, u32[]{:S(2)}) collective-permute-start(bf16[128,384]{1,0:T(8,128)(2,1)S(1)} %get-tuple-element.31), channel_id=1, source_target_pairs={{0,3},{1,0},{2,1},{3,2},{4,7},{5,4},{6,5},{7,6},{8,11},{9,8},{10,9... | collective-permute-start | bytes 294920 | tf_op jit(solution)/shard_map/ppermute | solution.py:393
  102.7 1.4 %collective-permute-start.19 = (bf16[128,384]{1,0:T(8,128)(2,1)S(1)}, bf16[128,384]{1,0:T(8,128)(2,1)S(1)}, u32[]{:S(2)}, u32[]{:S(2)}) collective-permute-start(bf16[128,384]{1,0:T(8,128)(2,1)S(1)} %get-tuple-element.32), channel_id=1, source_target_pairs={{0,2},{1,3},{2,0},{3,1},{4,6},{5,7},{6,4},{7,5},{8,10},{9,11},{10,... | collective-permute-start | bytes 294920 | tf_op jit(solution)/shard_map/ppermute | solution.py:393
  104.1 3.1 %hold.1.held = bf16[4,3,384,768]{3,2,1,0:T(8,128)(2,1)S(1)} custom-call(bf16[384,768]{1,0:T(8,128)(2,1)} %collective-permute-done.3.refs_0_, bf16[384,768]{1,0:T(8,128)(2,1)} %copy-done.2, bf16[384,768]{1,0:T(8,128)(2,1)} %collective-permute-done.1.refs_2_, bf16[384,768]{1,0:T(8,128)(2,1)} %collective-permute-done.2.refs_3_, ...), custom_call_target="tpu_custom_call" | custom-call | flops 1000000 | bytes 7000000 | tf_op jit(solution)/shard_map/hold/pallas_call | solution.py:320
  107.2 1.6 %collective-permute-done.19.r3 = bf16[128,384]{1,0:T(8,128)(2,1)S(1)} collective-permute-done((bf16[128,384]{1,0:T(8,128)(2,1)S(1)}, bf16[128,384]{1,0:T(8,128)(2,1)S(1)}, u32[]{:S(2)}, u32[]{:S(2)}) %collective-permute-start.19) | collective-permute-done | bytes 98336 | tf_op jit(solution)/shard_map/ppermute | solution.py:393
  108.8 3.2 %out_project.1 = bf16[128,3072]{1,0:T(8,128)(2,1)} custom-call(s32[7]{0:T(128)S(1)} %concatenate.3.info, bf16[128,384]{1,0:T(8,128)(2,1)S(1)} %get-tuple-element.29.r0, bf16[128,384]{1,0:T(8,128)(2,1)S(1)} %collective-permute-done.17.r1, bf16[128,384]{1,0:T(8,128)(2,1)S(1)} %collective-permute-done.18.r2, bf16[128,384]{1,0:T(8,128)(2,1)S(1)} %collective-permute-done.19.r3, ...), custom_call_target="tpu_custom_call" | custom-call | flops 1207959552 | bytes 10500000 | tf_op jit(solution)/shard_map/out_project/pallas_call | solution.py:350
  (29 shorter events, 0.1 us)
Async XLA Ops:
  8.9 11.5 %copy-start.1 = (bf16[32,56,384]{2,1,0:T(8,128)(2,1)S(1)}, bf16[32,56,384]{2,1,0:T(8,128)(2,1)}, u32[]{:S(2)}) copy-start(bf16[32,56,384]{2,1,0:T(8,128)(2,1)} %project.1.own) | copy-start | bytes 4128772
  8.9 45.8 %all-to-all-start = ((bf16[32,56,384]{2,1,0:T(8,128)(2,1)}), bf16[32,56,384]{2,1,0:T(8,128)(2,1)S(1)}, u32[]{:S(2)}, u32[]{:S(2)}) async-start(bf16[32,56,384]{2,1,0:T(8,128)(2,1)} %project.1.own), calls=%async_computation | async-start | bytes 2752512 | tf_op jit(solution)/shard_map/all_to_all | solution.py:410
  20.5 34.2 %collective-permute-start = (bf16[32,56,384]{2,1,0:T(8,128)(2,1)S(1)}, bf16[32,56,384]{2,1,0:T(8,128)(2,1)}, u32[]{:S(2)}, u32[]{:S(2)}) collective-permute-start(bf16[32,56,384]{2,1,0:T(8,128)(2,1)S(1)} %copy-done.1), channel_id=1, source_target_pairs={{0,4},{4,0},{1,5},{5,1},{2,6},{6,2},{3,7},{7,3},{8,12},{12,8},{9,1... | collective-permute-start | bytes 4128776 | tf_op jit(solution)/shard_map/ppermute | solution.py:389
  20.6 46.8 %copy-start.5 = (s32[12]{0:T(128)S(1)}, s32[12]{0:T(128)}, u32[]{:S(2)}) copy-start(s32[12]{0:T(128)} %param.10) | copy-start | bytes 148
  21.9 17.4 %collective-permute-start.5 = (bf16[384,768]{1,0:T(8,128)(2,1)S(1)}, bf16[384,768]{1,0:T(8,128)(2,1)S(1)}, u32[]{:S(2)}, u32[]{:S(2)}) collective-permute-start(bf16[384,768]{1,0:T(8,128)(2,1)S(1)} %get-tuple-element.37), channel_id=1, source_target_pairs={{0,1},{1,2},{2,3},{3,0},{4,5},{5,6},{6,7},{7,4},{8,9},{9,10},{10,1... | collective-permute-start | bytes 1769480 | tf_op jit(solution)/shard_map/ppermute | solution.py:393
  23.5 28.2 %collective-permute-start.3 = (bf16[384,768]{1,0:T(8,128)(2,1)S(1)}, bf16[384,768]{1,0:T(8,128)(2,1)}, u32[]{:S(2)}, u32[]{:S(2)}) collective-permute-start(bf16[384,768]{1,0:T(8,128)(2,1)S(1)} %get-tuple-element.38), channel_id=1, source_target_pairs={{0,1},{1,2},{2,3},{3,0},{4,5},{5,6},{6,7},{7,4},{8,9},{9,10},{10,1... | collective-permute-start | bytes 1769480 | tf_op jit(solution)/shard_map/ppermute | solution.py:393
  25.0 26.7 %collective-permute-start.2 = (bf16[384,768]{1,0:T(8,128)(2,1)S(1)}, bf16[384,768]{1,0:T(8,128)(2,1)}, u32[]{:S(2)}, u32[]{:S(2)}) collective-permute-start(bf16[384,768]{1,0:T(8,128)(2,1)S(1)} %get-tuple-element.37), channel_id=1, source_target_pairs={{0,3},{1,0},{2,1},{3,2},{4,7},{5,4},{6,5},{7,6},{8,11},{9,8},{10,9... | collective-permute-start | bytes 1769480 | tf_op jit(solution)/shard_map/ppermute | solution.py:393
  26.7 26.2 %collective-permute-start.1 = (bf16[384,768]{1,0:T(8,128)(2,1)S(1)}, bf16[384,768]{1,0:T(8,128)(2,1)}, u32[]{:S(2)}, u32[]{:S(2)}) collective-permute-start(bf16[384,768]{1,0:T(8,128)(2,1)S(1)} %get-tuple-element.38), channel_id=1, source_target_pairs={{0,3},{1,0},{2,1},{3,2},{4,7},{5,4},{6,5},{7,6},{8,11},{9,8},{10,9... | collective-permute-start | bytes 1769480 | tf_op jit(solution)/shard_map/ppermute | solution.py:393
  39.3 14.6 %copy-start.2 = (bf16[384,768]{1,0:T(8,128)(2,1)}, bf16[384,768]{1,0:T(8,128)(2,1)S(1)}, u32[]{:S(2)}) copy-start(bf16[384,768]{1,0:T(8,128)(2,1)S(1)} %collective-permute-done.5.refs_1_) | copy-start | bytes 1769476
  39.3 13.6 %collective-permute-start.6 = (bf16[384,768]{1,0:T(8,128)(2,1)S(1)}, bf16[384,768]{1,0:T(8,128)(2,1)S(1)}, u32[]{:S(2)}, u32[]{:S(2)}) collective-permute-start(bf16[384,768]{1,0:T(8,128)(2,1)S(1)} %collective-permute-done.5.refs_1_), channel_id=1, source_target_pairs={{0,4},{4,0},{1,5},{5,1},{2,6},{6,2},{3,7},{7,3},{8,12},{12,8},{9,1... | collective-permute-start | bytes 1769480 | tf_op jit(solution)/shard_map/ppermute | solution.py:389
  51.7 2.2 %collective-permute-start.4 = (bf16[384,768]{1,0:T(8,128)(2,1)}, bf16[384,768]{1,0:T(8,128)(2,1)S(1)}, u32[]{:S(2)}, u32[]{:S(2)}) collective-permute-start(bf16[384,768]{1,0:T(8,128)(2,1)} %collective-permute-done.3.refs_0_), channel_id=1, source_target_pairs={{0,4},{4,0},{1,5},{5,1},{2,6},{6,2},{3,7},{7,3},{8,12},{12,8},{9,1... | collective-permute-start | bytes 1769480 | tf_op jit(solution)/shard_map/ppermute | solution.py:389
  52.9 1.0 copy-start.3
  53.9 0.8 copy-start.4
  54.7 18.5 %collective-permute-start.8 = (bf16[384,768]{1,0:T(8,128)(2,1)}, bf16[384,768]{1,0:T(8,128)(2,1)}, u32[]{:S(2)}, u32[]{:S(2)}) collective-permute-start(bf16[384,768]{1,0:T(8,128)(2,1)} %collective-permute-done.1.refs_2_), channel_id=1, source_target_pairs={{0,4},{4,0},{1,5},{5,1},{2,6},{6,2},{3,7},{7,3},{8,12},{12,8},{9,1... | collective-permute-start | bytes 1769480 | tf_op jit(solution)/shard_map/ppermute | solution.py:389
  54.8 18.3 %collective-permute-start.9 = (bf16[384,768]{1,0:T(8,128)(2,1)}, bf16[384,768]{1,0:T(8,128)(2,1)}, u32[]{:S(2)}, u32[]{:S(2)}) collective-permute-start(bf16[384,768]{1,0:T(8,128)(2,1)} %collective-permute-done.2.refs_3_), channel_id=1, source_target_pairs={{0,4},{4,0},{1,5},{5,1},{2,6},{6,2},{3,7},{7,3},{8,12},{12,8},{9,1... | collective-permute-start | bytes 1769480 | tf_op jit(solution)/shard_map/ppermute | solution.py:389
  55.2 28.4 %collective-permute-start.20 = (bf16[384,768]{1,0:T(8,128)(2,1)}, bf16[384,768]{1,0:T(8,128)(2,1)}, u32[]{:S(2)}, u32[]{:S(2)}) collective-permute-start(bf16[384,768]{1,0:T(8,128)(2,1)} %collective-permute-done.3.refs_0_), channel_id=1, source_target_pairs={{0,1},{1,2},{2,3},{3,0},{4,5},{5,6},{6,7},{7,4},{8,9},{9,10},{10,1... | collective-permute-start | bytes 1769480 | tf_op jit(solution)/shard_map/ppermute | solution.py:393
  57.4 15.8 %all-to-all-start.1 = ((bf16[8,48,256]{2,1,0:T(8,128)(2,1)}), bf16[8,48,256]{2,1,0:T(8,128)(2,1)S(1)}, u32[]{:S(2)}, u32[]{:S(2)}) async-start(bf16[8,48,256]{2,1,0:T(8,128)(2,1)} %repeat_first.1), calls=%async_computation.1 | async-start | bytes 393216 | tf_op jit(solution)/shard_map/all_to_all | solution.py:423
  64.2 21.7 %collective-permute-start.21 = (bf16[384,768]{1,0:T(8,128)(2,1)}, bf16[384,768]{1,0:T(8,128)(2,1)}, u32[]{:S(2)}, u32[]{:S(2)}) collective-permute-start(bf16[384,768]{1,0:T(8,128)(2,1)} %collective-permute-done.2.refs_3_), channel_id=1, source_target_pairs={{0,3},{1,0},{2,1},{3,2},{4,7},{5,4},{6,5},{7,6},{8,11},{9,8},{10,9... | collective-permute-start | bytes 1769480 | tf_op jit(solution)/shard_map/ppermute | solution.py:393
  66.4 1.7 %collective-permute-start.7 = (bf16[32,8,384]{2,1,0:T(8,128)(2,1)S(1)}, bf16[32,8,384]{2,1,0:T(8,128)(2,1)S(1)}, u32[]{:S(2)}, u32[]{:S(2)}) collective-permute-start(bf16[32,8,384]{2,1,0:T(8,128)(2,1)S(1)} %slice.3.text_own), channel_id=1, source_target_pairs={{0,4},{4,0},{1,5},{5,1},{2,6},{6,2},{3,7},{7,3},{8,12},{12,8},{9,1... | collective-permute-start | bytes 589832 | tf_op jit(solution)/shard_map/ppermute | solution.py:389
  73.2 10.5 %collective-permute-start.12 = (bf16[8,48,256]{2,1,0:T(8,128)(2,1)S(1)}, bf16[8,48,256]{2,1,0:T(8,128)(2,1)S(1)}, u32[]{:S(2)}, u32[]{:S(2)}) collective-permute-start(bf16[8,48,256]{2,1,0:T(8,128)(2,1)S(1)} %all-to-all-done.1.refs_0_), channel_id=1, source_target_pairs={{0,24},{8,0},{16,8},{24,16},{1,25},{9,1},{17,9},{25,17},{2,26},{10... | collective-permute-start | bytes 589832 | tf_op jit(solution)/shard_map/ppermute | solution.py:393
  75.9 8.4 %collective-permute-start.11 = (bf16[8,48,256]{2,1,0:T(8,128)(2,1)S(1)}, bf16[8,48,256]{2,1,0:T(8,128)(2,1)S(1)}, u32[]{:S(2)}, u32[]{:S(2)}) collective-permute-start(bf16[8,48,256]{2,1,0:T(8,128)(2,1)S(1)} %all-to-all-done.1.refs_0_), channel_id=1, source_target_pairs={{0,16},{8,24},{16,0},{24,8},{1,17},{9,25},{17,1},{25,9},{2,18},{10... | collective-permute-start | bytes 589832 | tf_op jit(solution)/shard_map/ppermute | solution.py:393
  76.7 9.1 %collective-permute-start.10 = (bf16[8,48,256]{2,1,0:T(8,128)(2,1)S(1)}, bf16[8,48,256]{2,1,0:T(8,128)(2,1)S(1)}, u32[]{:S(2)}, u32[]{:S(2)}) collective-permute-start(bf16[8,48,256]{2,1,0:T(8,128)(2,1)S(1)} %all-to-all-done.1.refs_0_), channel_id=1, source_target_pairs={{0,8},{8,16},{16,24},{24,0},{1,9},{9,17},{17,25},{25,1},{2,10},{10... | collective-permute-start | bytes 589832 | tf_op jit(solution)/shard_map/ppermute | solution.py:393
  77.6 20.3 %all-to-all-start.2 = ((bf16[32,48,128]{2,1,0:T(8,128)(2,1)}), bf16[32,48,128]{2,1,0:T(8,128)(2,1)S(1)}, u32[]{:S(2)}, u32[]{:S(2)}) async-start(bf16[32,48,128]{2,1,0:T(8,128)(2,1)} %get-tuple-element.28), calls=%async_computation.2 | async-start | bytes 786432 | tf_op jit(solution)/shard_map/all_to_all | solution.py:429
  83.6 2.8 %collective-permute-start.13 = (bf16[8,48,256]{2,1,0:T(8,128)(2,1)S(1)}, bf16[8,48,256]{2,1,0:T(8,128)(2,1)S(1)}, u32[]{:S(2)}, u32[]{:S(2)}) collective-permute-start(bf16[8,48,256]{2,1,0:T(8,128)(2,1)S(1)} %all-to-all-done.1.refs_0_), channel_id=1, source_target_pairs={{0,4},{4,0},{1,5},{5,1},{2,6},{6,2},{3,7},{7,3},{8,12},{12,8},{9,1... | collective-permute-start | bytes 589832 | tf_op jit(solution)/shard_map/ppermute | solution.py:389
  83.7 2.7 %collective-permute-start.16 = (bf16[8,48,256]{2,1,0:T(8,128)(2,1)S(1)}, bf16[8,48,256]{2,1,0:T(8,128)(2,1)S(1)}, u32[]{:S(2)}, u32[]{:S(2)}) collective-permute-start(bf16[8,48,256]{2,1,0:T(8,128)(2,1)S(1)} %collective-permute-done.12.refs_3_), channel_id=1, source_target_pairs={{0,4},{4,0},{1,5},{5,1},{2,6},{6,2},{3,7},{7,3},{8,12},{12,8},{9,1... | collective-permute-start | bytes 589832 | tf_op jit(solution)/shard_map/ppermute | solution.py:389
  84.2 2.2 %collective-permute-start.15 = (bf16[8,48,256]{2,1,0:T(8,128)(2,1)S(1)}, bf16[8,48,256]{2,1,0:T(8,128)(2,1)S(1)}, u32[]{:S(2)}, u32[]{:S(2)}) collective-permute-start(bf16[8,48,256]{2,1,0:T(8,128)(2,1)S(1)} %collective-permute-done.11.refs_2_), channel_id=1, source_target_pairs={{0,4},{4,0},{1,5},{5,1},{2,6},{6,2},{3,7},{7,3},{8,12},{12,8},{9,1... | collective-permute-start | bytes 589832 | tf_op jit(solution)/shard_map/ppermute | solution.py:389
  85.8 1.6 %collective-permute-start.14 = (bf16[8,48,256]{2,1,0:T(8,128)(2,1)S(1)}, bf16[8,48,256]{2,1,0:T(8,128)(2,1)S(1)}, u32[]{:S(2)}, u32[]{:S(2)}) collective-permute-start(bf16[8,48,256]{2,1,0:T(8,128)(2,1)S(1)} %collective-permute-done.10.refs_1_), channel_id=1, source_target_pairs={{0,4},{4,0},{1,5},{5,1},{2,6},{6,2},{3,7},{7,3},{8,12},{12,8},{9,1... | collective-permute-start | bytes 589832 | tf_op jit(solution)/shard_map/ppermute | solution.py:389
  85.8 18.2 %collective-permute-start.22 = (bf16[384,768]{1,0:T(8,128)(2,1)}, bf16[384,768]{1,0:T(8,128)(2,1)}, u32[]{:S(2)}, u32[]{:S(2)}) collective-permute-start(bf16[384,768]{1,0:T(8,128)(2,1)} %collective-permute-done.20.refs_4_), channel_id=1, source_target_pairs={{0,4},{4,0},{1,5},{5,1},{2,6},{6,2},{3,7},{7,3},{8,12},{12,8},{9,1... | collective-permute-start | bytes 1769480 | tf_op jit(solution)/shard_map/ppermute | solution.py:389
  86.4 17.7 %collective-permute-start.23 = (bf16[384,768]{1,0:T(8,128)(2,1)}, bf16[384,768]{1,0:T(8,128)(2,1)}, u32[]{:S(2)}, u32[]{:S(2)}) collective-permute-start(bf16[384,768]{1,0:T(8,128)(2,1)} %collective-permute-done.21.refs_5_), channel_id=1, source_target_pairs={{0,4},{4,0},{1,5},{5,1},{2,6},{6,2},{3,7},{7,3},{8,12},{12,8},{9,1... | collective-permute-start | bytes 1769480 | tf_op jit(solution)/shard_map/ppermute | solution.py:389
  99.1 8.1 %collective-permute-start.17 = (bf16[128,384]{1,0:T(8,128)(2,1)S(1)}, bf16[128,384]{1,0:T(8,128)(2,1)S(1)}, u32[]{:S(2)}, u32[]{:S(2)}) collective-permute-start(bf16[128,384]{1,0:T(8,128)(2,1)S(1)} %get-tuple-element.30), channel_id=1, source_target_pairs={{0,1},{1,2},{2,3},{3,0},{4,5},{5,6},{6,7},{7,4},{8,9},{9,10},{10,1... | collective-permute-start | bytes 294920 | tf_op jit(solution)/shard_map/ppermute | solution.py:393
  100.3 6.9 %collective-permute-start.18 = (bf16[128,384]{1,0:T(8,128)(2,1)S(1)}, bf16[128,384]{1,0:T(8,128)(2,1)S(1)}, u32[]{:S(2)}, u32[]{:S(2)}) collective-permute-start(bf16[128,384]{1,0:T(8,128)(2,1)S(1)} %get-tuple-element.31), channel_id=1, source_target_pairs={{0,3},{1,0},{2,1},{3,2},{4,7},{5,4},{6,5},{7,6},{8,11},{9,8},{10,9... | collective-permute-start | bytes 294920 | tf_op jit(solution)/shard_map/ppermute | solution.py:393
  102.7 6.1 %copy-start = (bf16[3,128,3072]{2,1,0:T(8,128)(2,1)S(1)}, bf16[3,128,3072]{2,1,0:T(8,128)(2,1)}, u32[]{:S(2)}) copy-start(bf16[3,128,3072]{2,1,0:T(8,128)(2,1)} %param.9) | copy-start | bytes 7077892
  102.7 6.1 %collective-permute-start.19 = (bf16[128,384]{1,0:T(8,128)(2,1)S(1)}, bf16[128,384]{1,0:T(8,128)(2,1)S(1)}, u32[]{:S(2)}, u32[]{:S(2)}) collective-permute-start(bf16[128,384]{1,0:T(8,128)(2,1)S(1)} %get-tuple-element.32), channel_id=1, source_target_pairs={{0,2},{1,3},{2,0},{3,1},{4,6},{5,7},{6,4},{7,5},{8,10},{9,11},{10,... | collective-permute-start | bytes 294920 | tf_op jit(solution)/shard_map/ppermute | solution.py:393

commit v6 on v5

--- a/solution.py
+++ b/solution.py
@@ -275,8 +275,12 @@
 
             @pl.when(step == k)
             def _():
-                out_ref[...] = spatial_ref[index * BLOCK : (index + 1) * BLOCK, :]
                 for h in range(HEADS_HERE):
+                    lanes = slice(h * HEAD, (h + 1) * HEAD)
+
+                    @pl.when(info[h] != 0)
+                    def _():
+                        out_ref[:, lanes] = spatial_ref[index * BLOCK : (index + 1) * BLOCK, lanes]
 
                     @pl.when(info[h] == 0)
                     def _():

time: 114 us -> 114 us (level); the launches traced: 112 us -> 114 us
  waiting for transfers between devices: 34.7 us -> 39.1 us
  Pallas kernels: 29.3 us -> 26.3 us
    all_to_all x1, waiting for transfers between devices: 0.01 us -> 5.97 us  [local(): back = lax.all_to_all(over_time, ('z', 'y'), 0, 0, tiled=True)]
    pallas_call x1, Pallas kernels: 10.4 us -> 5.08 us  [spatial(): pl.pallas_call(spatial_kernel, in_specs=specs(2 + 2 * Y) + [pl.BlockSpec(...]
    pallas_call x1, Pallas kernels: 1.79 us -> 3.77 us  [temporal(): pl.pallas_call(temporal_kernel, in_specs=specs(3), out_specs=[pl.BlockSpe...]
    all_to_all x1, waiting for transfers between devices: 3.25 us -> 1.26 us  [local(): column = lax.all_to_all(repeat_first(moved), 'z', 0, 0, tiled=True)]
    all_to_all x1, starting transfers between devices: 6.01 us -> 8 us  [local(): back = lax.all_to_all(over_time, ('z', 'y'), 0, 0, tiled=True)]
    ppermute x12, starting transfers between devices: 18.4 us -> 16.7 us  [shifted(): lax.ppermute(value, axis, [(i, (i + k) % count) for i in range(count)])]
  transfers between devices with their start and end apart: 27 -> 27, of which waited for: 9 -> 10; matrix products, arithmetic and copies ran while one was open for 1% -> 1% of each run, Pallas kernels for 15% -> 12%
where the time goes in v6:
time: 114 us
  starting transfers between devices  45.2 us (40%)
  waiting for transfers between devices  39.1 us (34%)
  Pallas kernels  26.3 us (23%)
  local copies, waits for them, and re-layouts  2.34 us (2%)
    ppermute x12, waiting for transfers between devices, shifted(): lax.ppermute(value, axis, [(i, (i + k) % count) for i in range(count)])  29.2 us
    ppermute x12, starting transfers between devices, shifted(): lax.ppermute(value, axis, [(i, (i + k) % count) for i in range(count)])  16.7 us
    all_to_all x1, starting transfers between devices, local(): moved = lax.all_to_all(packed, ('z', 'y'), 0, 0, tiled=True)  11.5 us
    pallas_call x1, Pallas kernels, project(): pl.pallas_call(project_kernel, in_specs=[hbm, vmem, hbm], out_specs=vmem,...  8.93 us
    all_to_all x1, starting transfers between devices, local(): back = lax.all_to_all(over_time, ('z', 'y'), 0, 0, tiled=True)  8 us
    all_to_all x1, starting transfers between devices, local(): column = lax.all_to_all(repeat_first(moved), 'z', 0, 0, tiled=True)  6.8 us
    all_to_all x1, waiting for transfers between devices, local(): back = lax.all_to_all(over_time, ('z', 'y'), 0, 0, tiled=True)  5.97 us
    pallas_call x1, Pallas kernels, spatial(): pl.pallas_call(spatial_kernel, in_specs=specs(2 + 2 * Y) + [pl.BlockSpec(...  5.08 us
  transfers between devices with their start and end apart: 27, of which 10 were waited for; matrix products, arithmetic and copies ran while one was open for 1% of the time, Pallas kernels for 12%

profile of v6, /device:TPU:32, one launch (start us, length us, event | category | flops | bytes accessed | tf_op | source)
XLA Modules:
  0.0 113.7 jit_solution(8857381382199226321)
XLA Ops:
  0.0 8.9 %project.1.own = bf16[32,56,384]{2,1,0:T(8,128)(2,1)} custom-call(bf16[512,3072]{1,0:T(8,128)(2,1)} %x_hbm.1, bf16[4,3072]{1,0:T(4,128)(2,1)} %text_ref.1, bf16[3,3072,384]{2,1,0:T(8,128)(2,1)} %bitcast.7), custom_call_target="tpu_custom_call" | custom-call | flops 3623878656 | bytes 12000000 | tf_op jit(solution)/shard_map/project/pallas_call | solution.py:95
  8.9 11.5 %all-to-all-start = ((bf16[32,56,384]{2,1,0:T(8,128)(2,1)}), bf16[32,56,384]{2,1,0:T(8,128)(2,1)S(1)}, u32[]{:S(2)}, u32[]{:S(2)}) async-start(bf16[32,56,384]{2,1,0:T(8,128)(2,1)} %project.1.own), calls=%async_computation | async-start | bytes 2752512 | tf_op jit(solution)/shard_map/all_to_all | solution.py:414
  20.5 0.1 collective-permute-start
  20.6 0.0 copy-start.5
  20.6 1.3 %constant_dynamic-slice_fusion = (bf16[384,768]{1,0:T(8,128)(2,1)S(1)}, bf16[384,768]{1,0:T(8,128)(2,1)S(1)}) fusion(bf16[384,3072]{1,0:T(8,128)(2,1)} %bitcast.5, s32[]{:T(128)S(6)} %select_n.11, s32[]{:T(128)S(6)} %select_n.10), kind=kLoop, calls=%fused_computation | loop fusion | bytes 2359304 | tf_op jit(solution)/shard_map/dynamic_slice | solution.py:409
  21.9 1.6 %collective-permute-start.5 = (bf16[384,768]{1,0:T(8,128)(2,1)S(1)}, bf16[384,768]{1,0:T(8,128)(2,1)S(1)}, u32[]{:S(2)}, u32[]{:S(2)}) collective-permute-start(bf16[384,768]{1,0:T(8,128)(2,1)S(1)} %get-tuple-element.37), channel_id=1, source_target_pairs={{0,1},{1,2},{2,3},{3,0},{4,5},{5,6},{6,7},{7,4},{8,9},{9,10},{10,1... | collective-permute-start | bytes 1769480 | tf_op jit(solution)/shard_map/ppermute | solution.py:397
  23.5 1.5 %collective-permute-start.3 = (bf16[384,768]{1,0:T(8,128)(2,1)S(1)}, bf16[384,768]{1,0:T(8,128)(2,1)}, u32[]{:S(2)}, u32[]{:S(2)}) collective-permute-start(bf16[384,768]{1,0:T(8,128)(2,1)S(1)} %get-tuple-element.38), channel_id=1, source_target_pairs={{0,1},{1,2},{2,3},{3,0},{4,5},{5,6},{6,7},{7,4},{8,9},{9,10},{10,1... | collective-permute-start | bytes 1769480 | tf_op jit(solution)/shard_map/ppermute | solution.py:397
  25.0 1.7 %collective-permute-start.2 = (bf16[384,768]{1,0:T(8,128)(2,1)S(1)}, bf16[384,768]{1,0:T(8,128)(2,1)}, u32[]{:S(2)}, u32[]{:S(2)}) collective-permute-start(bf16[384,768]{1,0:T(8,128)(2,1)S(1)} %get-tuple-element.37), channel_id=1, source_target_pairs={{0,3},{1,0},{2,1},{3,2},{4,7},{5,4},{6,5},{7,6},{8,11},{9,8},{10,9... | collective-permute-start | bytes 1769480 | tf_op jit(solution)/shard_map/ppermute | solution.py:397
  26.7 0.5 collective-permute-start.1
  27.3 12.1 %collective-permute-done.5.refs_1_ = bf16[384,768]{1,0:T(8,128)(2,1)S(1)} collective-permute-done((bf16[384,768]{1,0:T(8,128)(2,1)S(1)}, bf16[384,768]{1,0:T(8,128)(2,1)S(1)}, u32[]{:S(2)}, u32[]{:S(2)}) %collective-permute-start.5) | collective-permute-done | bytes 589856 | tf_op jit(solution)/shard_map/ppermute | solution.py:397
  39.3 12.3 %collective-permute-done.3.refs_0_ = bf16[384,768]{1,0:T(8,128)(2,1)} collective-permute-done((bf16[384,768]{1,0:T(8,128)(2,1)S(1)}, bf16[384,768]{1,0:T(8,128)(2,1)}, u32[]{:S(2)}, u32[]{:S(2)}) %collective-permute-start.3) | collective-permute-done | bytes 589856 | tf_op jit(solution)/shard_map/ppermute | solution.py:397
  51.7 0.0 collective-permute-start.4
  51.7 0.0 collective-permute-done.2.refs_3_
  51.7 1.2 %collective-permute-done.1.refs_2_ = bf16[384,768]{1,0:T(8,128)(2,1)} collective-permute-done((bf16[384,768]{1,0:T(8,128)(2,1)S(1)}, bf16[384,768]{1,0:T(8,128)(2,1)}, u32[]{:S(2)}, u32[]{:S(2)}) %collective-permute-start.1) | collective-permute-done | bytes 589856 | tf_op jit(solution)/shard_map/ppermute | solution.py:397
  52.9 1.0 collective-permute-done.4.refs_6_
  53.9 0.8 copy-done.4
  54.7 0.1 collective-permute-start.8
  54.8 0.4 collective-permute-start.9
  55.2 1.4 %collective-permute-start.20 = (bf16[384,768]{1,0:T(8,128)(2,1)}, bf16[384,768]{1,0:T(8,128)(2,1)}, u32[]{:S(2)}, u32[]{:S(2)}) collective-permute-start(bf16[384,768]{1,0:T(8,128)(2,1)} %collective-permute-done.3.refs_0_), channel_id=1, source_target_pairs={{0,1},{1,2},{2,3},{3,0},{4,5},{5,6},{6,7},{7,4},{8,9},{9,10},{10,1... | collective-permute-start | bytes 1769480 | tf_op jit(solution)/shard_map/ppermute | solution.py:397
  56.7 0.7 repeat_first.1
  57.4 6.8 %all-to-all-start.1 = ((bf16[8,48,256]{2,1,0:T(8,128)(2,1)}), bf16[8,48,256]{2,1,0:T(8,128)(2,1)S(1)}, u32[]{:S(2)}, u32[]{:S(2)}) async-start(bf16[8,48,256]{2,1,0:T(8,128)(2,1)} %repeat_first.1), calls=%async_computation.1 | async-start | bytes 393216 | tf_op jit(solution)/shard_map/all_to_all | solution.py:427
  64.2 2.2 %collective-permute-start.21 = (bf16[384,768]{1,0:T(8,128)(2,1)}, bf16[384,768]{1,0:T(8,128)(2,1)}, u32[]{:S(2)}, u32[]{:S(2)}) collective-permute-start(bf16[384,768]{1,0:T(8,128)(2,1)} %collective-permute-done.2.refs_3_), channel_id=1, source_target_pairs={{0,3},{1,0},{2,1},{3,2},{4,7},{5,4},{6,5},{7,6},{8,11},{9,8},{10,9... | collective-permute-start | bytes 1769480 | tf_op jit(solution)/shard_map/ppermute | solution.py:397
  66.4 0.3 collective-permute-start.7
  67.4 0.1 dynamic_slice.9
  67.4 0.1 concatenate.3.info
  67.5 0.6 collective-permute-done.7.text_other
  68.1 3.8 %temporal.1 = (bf16[32,48,128]{2,1,0:T(8,128)(2,1)}, bf16[3,2,256,128]{3,2,1,0:T(8,128)(2,1)}) custom-call(s32[7]{0:T(128)S(1)} %concatenate.3.info, bf16[32,56,384]{2,1,0:T(8,128)(2,1)S(1)} %all-to-all-done.rows_hbm.rows_ref, bf16[32,8,384]{2,1,0:T(8,128)(2,1)S(1)} %slice.3.text_own, bf16[32,8,384]{2,1,0:T(8,128)(2,1)S(1)} %collective-permute-done.7.text_other), custom_call_target="tpu_custom_call" | custom-call | flops 400000000 | bytes 3000000 | tf_op jit(solution)/shard_map/temporal/pallas_call | solution.py:186
  71.9 1.3 %all-to-all-done.1.refs_0_ = bf16[8,48,256]{2,1,0:T(8,128)(2,1)S(1)} async-done(((bf16[8,48,256]{2,1,0:T(8,128)(2,1)}), bf16[8,48,256]{2,1,0:T(8,128)(2,1)S(1)}, u32[]{:S(2)}, u32[]{:S(2)}) %all-to-all-start.1) | async-done | bytes 196640 | tf_op jit(solution)/shard_map/all_to_all | solution.py:427
  73.2 2.7 %collective-permute-start.12 = (bf16[8,48,256]{2,1,0:T(8,128)(2,1)S(1)}, bf16[8,48,256]{2,1,0:T(8,128)(2,1)S(1)}, u32[]{:S(2)}, u32[]{:S(2)}) collective-permute-start(bf16[8,48,256]{2,1,0:T(8,128)(2,1)S(1)} %all-to-all-done.1.refs_0_), channel_id=1, source_target_pairs={{0,24},{8,0},{16,8},{24,16},{1,25},{9,1},{17,9},{25,17},{2,26},{10... | collective-permute-start | bytes 589832 | tf_op jit(solution)/shard_map/ppermute | solution.py:397
  75.9 0.9 collective-permute-start.11
  76.7 0.9 collective-permute-start.10
  77.6 8.0 %all-to-all-start.2 = ((bf16[32,48,128]{2,1,0:T(8,128)(2,1)}), bf16[32,48,128]{2,1,0:T(8,128)(2,1)S(1)}, u32[]{:S(2)}, u32[]{:S(2)}) async-start(bf16[32,48,128]{2,1,0:T(8,128)(2,1)} %get-tuple-element.28), calls=%async_computation.2 | async-start | bytes 786432 | tf_op jit(solution)/shard_map/all_to_all | solution.py:433
  85.6 0.1 collective-permute-start.13
  85.7 0.5 collective-permute-start.16
  86.2 0.1 collective-permute-start.15
  86.3 0.7 collective-permute-done.10.refs_1_
  87.1 0.5 collective-permute-start.22
  87.6 0.1 collective-permute-start.23
  87.7 0.0 collective-permute-done.15.refs_6_
  87.7 1.0 collective-permute-done.14.refs_5_
  88.7 5.1 %spatial.1.spatial_ref = bf16[512,384]{1,0:T(8,128)(2,1)} custom-call(s32[7]{0:T(128)S(1)} %concatenate.3.info, bf16[32,56,384]{2,1,0:T(8,128)(2,1)S(1)} %copy-done.1, bf16[32,56,384]{2,1,0:T(8,128)(2,1)} %collective-permute-done.partner, bf16[8,48,256]{2,1,0:T(8,128)(2,1)S(1)} %all-to-all-done.1.refs_0_, ...), custom_call_target="tpu_custom_call" | custom-call | flops 4000000000 | bytes 1000000 | tf_op jit(solution)/shard_map/spatial/pallas_call | solution.py:255
  93.8 6.0 %all-to-all-done.2.back = bf16[32,48,128]{2,1,0:T(8,128)(2,1)S(1)} async-done(((bf16[32,48,128]{2,1,0:T(8,128)(2,1)}), bf16[32,48,128]{2,1,0:T(8,128)(2,1)S(1)}, u32[]{:S(2)}, u32[]{:S(2)}) %all-to-all-start.2) | async-done | bytes 393248 | tf_op jit(solution)/shard_map/all_to_all | solution.py:433
  99.7 1.3 %merge.1 = (bf16[128,384]{1,0:T(8,128)(2,1)S(1)}, bf16[128,384]{1,0:T(8,128)(2,1)S(1)}, bf16[128,384]{1,0:T(8,128)(2,1)S(1)}, bf16[128,384]{1,0:T(8,128)(2,1)S(1)}) custom-call(s32[7]{0:T(128)S(1)} %concatenate.3.info, bf16[512,384]{1,0:T(8,128)(2,1)} %spatial.1.spatial_ref, bf16[32,48,128]{2,1,0:T(8,128)(2,1)S(1)} %all-to-all-done.2.back), custom_call_target="tpu_custom_call" | custom-call | tf_op jit(solution)/shard_map/merge/pallas_call | solution.py:294
  101.0 0.1 collective-permute-start.17
  101.1 3.2 %collective-permute-start.18 = (bf16[128,384]{1,0:T(8,128)(2,1)S(1)}, bf16[128,384]{1,0:T(8,128)(2,1)S(1)}, u32[]{:S(2)}, u32[]{:S(2)}) collective-permute-start(bf16[128,384]{1,0:T(8,128)(2,1)S(1)} %get-tuple-element.31), channel_id=1, source_target_pairs={{0,3},{1,0},{2,1},{3,2},{4,7},{5,4},{6,5},{7,6},{8,11},{9,8},{10,9... | collective-permute-start | bytes 294920 | tf_op jit(solution)/shard_map/ppermute | solution.py:397
  104.4 3.3 %hold.1.held = bf16[4,3,384,768]{3,2,1,0:T(8,128)(2,1)S(1)} custom-call(bf16[384,768]{1,0:T(8,128)(2,1)} %collective-permute-done.3.refs_0_, bf16[384,768]{1,0:T(8,128)(2,1)} %copy-done.2, bf16[384,768]{1,0:T(8,128)(2,1)} %collective-permute-done.1.refs_2_, bf16[384,768]{1,0:T(8,128)(2,1)} %collective-permute-done.2.refs_3_, ...), custom_call_target="tpu_custom_call" | custom-call | flops 1000000 | bytes 7000000 | tf_op jit(solution)/shard_map/hold/pallas_call | solution.py:324
  107.7 2.8 %collective-permute-done.19.r3 = bf16[128,384]{1,0:T(8,128)(2,1)S(1)} collective-permute-done((bf16[128,384]{1,0:T(8,128)(2,1)S(1)}, bf16[128,384]{1,0:T(8,128)(2,1)S(1)}, u32[]{:S(2)}, u32[]{:S(2)}) %collective-permute-start.19) | collective-permute-done | bytes 98336 | tf_op jit(solution)/shard_map/ppermute | solution.py:397
  110.5 3.2 %out_project.1 = bf16[128,3072]{1,0:T(8,128)(2,1)} custom-call(s32[7]{0:T(128)S(1)} %concatenate.3.info, bf16[128,384]{1,0:T(8,128)(2,1)S(1)} %get-tuple-element.29.r0, bf16[128,384]{1,0:T(8,128)(2,1)S(1)} %collective-permute-done.17.r1, bf16[128,384]{1,0:T(8,128)(2,1)S(1)} %collective-permute-done.18.r2, bf16[128,384]{1,0:T(8,128)(2,1)S(1)} %collective-permute-done.19.r3, ...), custom_call_target="tpu_custom_call" | custom-call | flops 1207959552 | bytes 10500000 | tf_op jit(solution)/shard_map/out_project/pallas_call | solution.py:354
  (29 shorter events, 0.1 us)
Async XLA Ops:
  8.9 11.5 %copy-start.1 = (bf16[32,56,384]{2,1,0:T(8,128)(2,1)S(1)}, bf16[32,56,384]{2,1,0:T(8,128)(2,1)}, u32[]{:S(2)}) copy-start(bf16[32,56,384]{2,1,0:T(8,128)(2,1)} %project.1.own) | copy-start | bytes 4128772
  8.9 45.8 %all-to-all-start = ((bf16[32,56,384]{2,1,0:T(8,128)(2,1)}), bf16[32,56,384]{2,1,0:T(8,128)(2,1)S(1)}, u32[]{:S(2)}, u32[]{:S(2)}) async-start(bf16[32,56,384]{2,1,0:T(8,128)(2,1)} %project.1.own), calls=%async_computation | async-start | bytes 2752512 | tf_op jit(solution)/shard_map/all_to_all | solution.py:414
  20.5 34.2 %collective-permute-start = (bf16[32,56,384]{2,1,0:T(8,128)(2,1)S(1)}, bf16[32,56,384]{2,1,0:T(8,128)(2,1)}, u32[]{:S(2)}, u32[]{:S(2)}) collective-permute-start(bf16[32,56,384]{2,1,0:T(8,128)(2,1)S(1)} %copy-done.1), channel_id=1, source_target_pairs={{0,4},{4,0},{1,5},{5,1},{2,6},{6,2},{3,7},{7,3},{8,12},{12,8},{9,1... | collective-permute-start | bytes 4128776 | tf_op jit(solution)/shard_map/ppermute | solution.py:393
  20.6 46.8 %copy-start.5 = (s32[12]{0:T(128)S(1)}, s32[12]{0:T(128)}, u32[]{:S(2)}) copy-start(s32[12]{0:T(128)} %param.10) | copy-start | bytes 148
  21.9 17.4 %collective-permute-start.5 = (bf16[384,768]{1,0:T(8,128)(2,1)S(1)}, bf16[384,768]{1,0:T(8,128)(2,1)S(1)}, u32[]{:S(2)}, u32[]{:S(2)}) collective-permute-start(bf16[384,768]{1,0:T(8,128)(2,1)S(1)} %get-tuple-element.37), channel_id=1, source_target_pairs={{0,1},{1,2},{2,3},{3,0},{4,5},{5,6},{6,7},{7,4},{8,9},{9,10},{10,1... | collective-permute-start | bytes 1769480 | tf_op jit(solution)/shard_map/ppermute | solution.py:397
  23.5 28.2 %collective-permute-start.3 = (bf16[384,768]{1,0:T(8,128)(2,1)S(1)}, bf16[384,768]{1,0:T(8,128)(2,1)}, u32[]{:S(2)}, u32[]{:S(2)}) collective-permute-start(bf16[384,768]{1,0:T(8,128)(2,1)S(1)} %get-tuple-element.38), channel_id=1, source_target_pairs={{0,1},{1,2},{2,3},{3,0},{4,5},{5,6},{6,7},{7,4},{8,9},{9,10},{10,1... | collective-permute-start | bytes 1769480 | tf_op jit(solution)/shard_map/ppermute | solution.py:397
  25.0 26.7 %collective-permute-start.2 = (bf16[384,768]{1,0:T(8,128)(2,1)S(1)}, bf16[384,768]{1,0:T(8,128)(2,1)}, u32[]{:S(2)}, u32[]{:S(2)}) collective-permute-start(bf16[384,768]{1,0:T(8,128)(2,1)S(1)} %get-tuple-element.37), channel_id=1, source_target_pairs={{0,3},{1,0},{2,1},{3,2},{4,7},{5,4},{6,5},{7,6},{8,11},{9,8},{10,9... | collective-permute-start | bytes 1769480 | tf_op jit(solution)/shard_map/ppermute | solution.py:397
  26.7 26.2 %collective-permute-start.1 = (bf16[384,768]{1,0:T(8,128)(2,1)S(1)}, bf16[384,768]{1,0:T(8,128)(2,1)}, u32[]{:S(2)}, u32[]{:S(2)}) collective-permute-start(bf16[384,768]{1,0:T(8,128)(2,1)S(1)} %get-tuple-element.38), channel_id=1, source_target_pairs={{0,3},{1,0},{2,1},{3,2},{4,7},{5,4},{6,5},{7,6},{8,11},{9,8},{10,9... | collective-permute-start | bytes 1769480 | tf_op jit(solution)/shard_map/ppermute | solution.py:397
  39.3 14.6 %copy-start.2 = (bf16[384,768]{1,0:T(8,128)(2,1)}, bf16[384,768]{1,0:T(8,128)(2,1)S(1)}, u32[]{:S(2)}) copy-start(bf16[384,768]{1,0:T(8,128)(2,1)S(1)} %collective-permute-done.5.refs_1_) | copy-start | bytes 1769476
  39.3 13.6 %collective-permute-start.6 = (bf16[384,768]{1,0:T(8,128)(2,1)S(1)}, bf16[384,768]{1,0:T(8,128)(2,1)S(1)}, u32[]{:S(2)}, u32[]{:S(2)}) collective-permute-start(bf16[384,768]{1,0:T(8,128)(2,1)S(1)} %collective-permute-done.5.refs_1_), channel_id=1, source_target_pairs={{0,4},{4,0},{1,5},{5,1},{2,6},{6,2},{3,7},{7,3},{8,12},{12,8},{9,1... | collective-permute-start | bytes 1769480 | tf_op jit(solution)/shard_map/ppermute | solution.py:393
  51.7 2.2 %collective-permute-start.4 = (bf16[384,768]{1,0:T(8,128)(2,1)}, bf16[384,768]{1,0:T(8,128)(2,1)S(1)}, u32[]{:S(2)}, u32[]{:S(2)}) collective-permute-start(bf16[384,768]{1,0:T(8,128)(2,1)} %collective-permute-done.3.refs_0_), channel_id=1, source_target_pairs={{0,4},{4,0},{1,5},{5,1},{2,6},{6,2},{3,7},{7,3},{8,12},{12,8},{9,1... | collective-permute-start | bytes 1769480 | tf_op jit(solution)/shard_map/ppermute | solution.py:393
  52.9 1.0 copy-start.3
  53.9 0.8 copy-start.4
  54.7 18.5 %collective-permute-start.8 = (bf16[384,768]{1,0:T(8,128)(2,1)}, bf16[384,768]{1,0:T(8,128)(2,1)}, u32[]{:S(2)}, u32[]{:S(2)}) collective-permute-start(bf16[384,768]{1,0:T(8,128)(2,1)} %collective-permute-done.1.refs_2_), channel_id=1, source_target_pairs={{0,4},{4,0},{1,5},{5,1},{2,6},{6,2},{3,7},{7,3},{8,12},{12,8},{9,1... | collective-permute-start | bytes 1769480 | tf_op jit(solution)/shard_map/ppermute | solution.py:393
  54.8 18.3 %collective-permute-start.9 = (bf16[384,768]{1,0:T(8,128)(2,1)}, bf16[384,768]{1,0:T(8,128)(2,1)}, u32[]{:S(2)}, u32[]{:S(2)}) collective-permute-start(bf16[384,768]{1,0:T(8,128)(2,1)} %collective-permute-done.2.refs_3_), channel_id=1, source_target_pairs={{0,4},{4,0},{1,5},{5,1},{2,6},{6,2},{3,7},{7,3},{8,12},{12,8},{9,1... | collective-permute-start | bytes 1769480 | tf_op jit(solution)/shard_map/ppermute | solution.py:393
  55.2 30.4 %collective-permute-start.20 = (bf16[384,768]{1,0:T(8,128)(2,1)}, bf16[384,768]{1,0:T(8,128)(2,1)}, u32[]{:S(2)}, u32[]{:S(2)}) collective-permute-start(bf16[384,768]{1,0:T(8,128)(2,1)} %collective-permute-done.3.refs_0_), channel_id=1, source_target_pairs={{0,1},{1,2},{2,3},{3,0},{4,5},{5,6},{6,7},{7,4},{8,9},{9,10},{10,1... | collective-permute-start | bytes 1769480 | tf_op jit(solution)/shard_map/ppermute | solution.py:397
  57.4 15.8 %all-to-all-start.1 = ((bf16[8,48,256]{2,1,0:T(8,128)(2,1)}), bf16[8,48,256]{2,1,0:T(8,128)(2,1)S(1)}, u32[]{:S(2)}, u32[]{:S(2)}) async-start(bf16[8,48,256]{2,1,0:T(8,128)(2,1)} %repeat_first.1), calls=%async_computation.1 | async-start | bytes 393216 | tf_op jit(solution)/shard_map/all_to_all | solution.py:427
  64.2 22.9 %collective-permute-start.21 = (bf16[384,768]{1,0:T(8,128)(2,1)}, bf16[384,768]{1,0:T(8,128)(2,1)}, u32[]{:S(2)}, u32[]{:S(2)}) collective-permute-start(bf16[384,768]{1,0:T(8,128)(2,1)} %collective-permute-done.2.refs_3_), channel_id=1, source_target_pairs={{0,3},{1,0},{2,1},{3,2},{4,7},{5,4},{6,5},{7,6},{8,11},{9,8},{10,9... | collective-permute-start | bytes 1769480 | tf_op jit(solution)/shard_map/ppermute | solution.py:397
  66.4 1.7 %collective-permute-start.7 = (bf16[32,8,384]{2,1,0:T(8,128)(2,1)S(1)}, bf16[32,8,384]{2,1,0:T(8,128)(2,1)S(1)}, u32[]{:S(2)}, u32[]{:S(2)}) collective-permute-start(bf16[32,8,384]{2,1,0:T(8,128)(2,1)S(1)} %slice.3.text_own), channel_id=1, source_target_pairs={{0,4},{4,0},{1,5},{5,1},{2,6},{6,2},{3,7},{7,3},{8,12},{12,8},{9,1... | collective-permute-start | bytes 589832 | tf_op jit(solution)/shard_map/ppermute | solution.py:393
  73.2 12.5 %collective-permute-start.12 = (bf16[8,48,256]{2,1,0:T(8,128)(2,1)S(1)}, bf16[8,48,256]{2,1,0:T(8,128)(2,1)S(1)}, u32[]{:S(2)}, u32[]{:S(2)}) collective-permute-start(bf16[8,48,256]{2,1,0:T(8,128)(2,1)S(1)} %all-to-all-done.1.refs_0_), channel_id=1, source_target_pairs={{0,24},{8,0},{16,8},{24,16},{1,25},{9,1},{17,9},{25,17},{2,26},{10... | collective-permute-start | bytes 589832 | tf_op jit(solution)/shard_map/ppermute | solution.py:397
  75.9 10.3 %collective-permute-start.11 = (bf16[8,48,256]{2,1,0:T(8,128)(2,1)S(1)}, bf16[8,48,256]{2,1,0:T(8,128)(2,1)S(1)}, u32[]{:S(2)}, u32[]{:S(2)}) collective-permute-start(bf16[8,48,256]{2,1,0:T(8,128)(2,1)S(1)} %all-to-all-done.1.refs_0_), channel_id=1, source_target_pairs={{0,16},{8,24},{16,0},{24,8},{1,17},{9,25},{17,1},{25,9},{2,18},{10... | collective-permute-start | bytes 589832 | tf_op jit(solution)/shard_map/ppermute | solution.py:397
  76.7 10.3 %collective-permute-start.10 = (bf16[8,48,256]{2,1,0:T(8,128)(2,1)S(1)}, bf16[8,48,256]{2,1,0:T(8,128)(2,1)S(1)}, u32[]{:S(2)}, u32[]{:S(2)}) collective-permute-start(bf16[8,48,256]{2,1,0:T(8,128)(2,1)S(1)} %all-to-all-done.1.refs_0_), channel_id=1, source_target_pairs={{0,8},{8,16},{16,24},{24,0},{1,9},{9,17},{17,25},{25,1},{2,10},{10... | collective-permute-start | bytes 589832 | tf_op jit(solution)/shard_map/ppermute | solution.py:397
  77.6 22.2 %all-to-all-start.2 = ((bf16[32,48,128]{2,1,0:T(8,128)(2,1)}), bf16[32,48,128]{2,1,0:T(8,128)(2,1)S(1)}, u32[]{:S(2)}, u32[]{:S(2)}) async-start(bf16[32,48,128]{2,1,0:T(8,128)(2,1)} %get-tuple-element.28), calls=%async_computation.2 | async-start | bytes 786432 | tf_op jit(solution)/shard_map/all_to_all | solution.py:433
  85.6 2.0 %collective-permute-start.13 = (bf16[8,48,256]{2,1,0:T(8,128)(2,1)S(1)}, bf16[8,48,256]{2,1,0:T(8,128)(2,1)S(1)}, u32[]{:S(2)}, u32[]{:S(2)}) collective-permute-start(bf16[8,48,256]{2,1,0:T(8,128)(2,1)S(1)} %all-to-all-done.1.refs_0_), channel_id=1, source_target_pairs={{0,4},{4,0},{1,5},{5,1},{2,6},{6,2},{3,7},{7,3},{8,12},{12,8},{9,1... | collective-permute-start | bytes 589832 | tf_op jit(solution)/shard_map/ppermute | solution.py:393
  85.7 2.0 %collective-permute-start.16 = (bf16[8,48,256]{2,1,0:T(8,128)(2,1)S(1)}, bf16[8,48,256]{2,1,0:T(8,128)(2,1)S(1)}, u32[]{:S(2)}, u32[]{:S(2)}) collective-permute-start(bf16[8,48,256]{2,1,0:T(8,128)(2,1)S(1)} %collective-permute-done.12.refs_3_), channel_id=1, source_target_pairs={{0,4},{4,0},{1,5},{5,1},{2,6},{6,2},{3,7},{7,3},{8,12},{12,8},{9,1... | collective-permute-start | bytes 589832 | tf_op jit(solution)/shard_map/ppermute | solution.py:393
  86.2 1.5 %collective-permute-start.15 = (bf16[8,48,256]{2,1,0:T(8,128)(2,1)S(1)}, bf16[8,48,256]{2,1,0:T(8,128)(2,1)S(1)}, u32[]{:S(2)}, u32[]{:S(2)}) collective-permute-start(bf16[8,48,256]{2,1,0:T(8,128)(2,1)S(1)} %collective-permute-done.11.refs_2_), channel_id=1, source_target_pairs={{0,4},{4,0},{1,5},{5,1},{2,6},{6,2},{3,7},{7,3},{8,12},{12,8},{9,1... | collective-permute-start | bytes 589832 | tf_op jit(solution)/shard_map/ppermute | solution.py:393
  87.0 1.6 %collective-permute-start.14 = (bf16[8,48,256]{2,1,0:T(8,128)(2,1)S(1)}, bf16[8,48,256]{2,1,0:T(8,128)(2,1)S(1)}, u32[]{:S(2)}, u32[]{:S(2)}) collective-permute-start(bf16[8,48,256]{2,1,0:T(8,128)(2,1)S(1)} %collective-permute-done.10.refs_1_), channel_id=1, source_target_pairs={{0,4},{4,0},{1,5},{5,1},{2,6},{6,2},{3,7},{7,3},{8,12},{12,8},{9,1... | collective-permute-start | bytes 589832 | tf_op jit(solution)/shard_map/ppermute | solution.py:393
  87.1 17.3 %collective-permute-start.22 = (bf16[384,768]{1,0:T(8,128)(2,1)}, bf16[384,768]{1,0:T(8,128)(2,1)}, u32[]{:S(2)}, u32[]{:S(2)}) collective-permute-start(bf16[384,768]{1,0:T(8,128)(2,1)} %collective-permute-done.20.refs_4_), channel_id=1, source_target_pairs={{0,4},{4,0},{1,5},{5,1},{2,6},{6,2},{3,7},{7,3},{8,12},{12,8},{9,1... | collective-permute-start | bytes 1769480 | tf_op jit(solution)/shard_map/ppermute | solution.py:393
  87.6 16.8 %collective-permute-start.23 = (bf16[384,768]{1,0:T(8,128)(2,1)}, bf16[384,768]{1,0:T(8,128)(2,1)}, u32[]{:S(2)}, u32[]{:S(2)}) collective-permute-start(bf16[384,768]{1,0:T(8,128)(2,1)} %collective-permute-done.21.refs_5_), channel_id=1, source_target_pairs={{0,4},{4,0},{1,5},{5,1},{2,6},{6,2},{3,7},{7,3},{8,12},{12,8},{9,1... | collective-permute-start | bytes 1769480 | tf_op jit(solution)/shard_map/ppermute | solution.py:393
  101.0 6.6 %collective-permute-start.17 = (bf16[128,384]{1,0:T(8,128)(2,1)S(1)}, bf16[128,384]{1,0:T(8,128)(2,1)S(1)}, u32[]{:S(2)}, u32[]{:S(2)}) collective-permute-start(bf16[128,384]{1,0:T(8,128)(2,1)S(1)} %get-tuple-element.30), channel_id=1, source_target_pairs={{0,1},{1,2},{2,3},{3,0},{4,5},{5,6},{6,7},{7,4},{8,9},{9,10},{10,1... | collective-permute-start | bytes 294920 | tf_op jit(solution)/shard_map/ppermute | solution.py:397
  101.1 6.5 %collective-permute-start.18 = (bf16[128,384]{1,0:T(8,128)(2,1)S(1)}, bf16[128,384]{1,0:T(8,128)(2,1)S(1)}, u32[]{:S(2)}, u32[]{:S(2)}) collective-permute-start(bf16[128,384]{1,0:T(8,128)(2,1)S(1)} %get-tuple-element.31), channel_id=1, source_target_pairs={{0,3},{1,0},{2,1},{3,2},{4,7},{5,4},{6,5},{7,6},{8,11},{9,8},{10,9... | collective-permute-start | bytes 294920 | tf_op jit(solution)/shard_map/ppermute | solution.py:397
  104.4 6.1 %copy-start = (bf16[3,128,3072]{2,1,0:T(8,128)(2,1)S(1)}, bf16[3,128,3072]{2,1,0:T(8,128)(2,1)}, u32[]{:S(2)}) copy-start(bf16[3,128,3072]{2,1,0:T(8,128)(2,1)} %param.9) | copy-start | bytes 7077892
  104.4 6.1 %collective-permute-start.19 = (bf16[128,384]{1,0:T(8,128)(2,1)S(1)}, bf16[128,384]{1,0:T(8,128)(2,1)S(1)}, u32[]{:S(2)}, u32[]{:S(2)}) collective-permute-start(bf16[128,384]{1,0:T(8,128)(2,1)S(1)} %get-tuple-element.32), channel_id=1, source_target_pairs={{0,2},{1,3},{2,0},{3,1},{4,6},{5,7},{6,4},{7,5},{8,10},{9,11},{10,... | collective-permute-start | bytes 294920 | tf_op jit(solution)/shard_map/ppermute | solution.py:397
